TPU v7x, 32 devices: a whole 2x2x4 slice. The times are simulated.
32 devices in a mesh: parts: 2 (over y), tm: 4 (over z), space: 2 (over x), stn: 2 (over core).
Axes of the slice: x: 2, y: 2, z: 4, core: 2. Of those that a mesh axis runs over, the one named last changes fastest.
Arguments:
- fluxes: float32 [64, 4096], P('tm', ('parts', 'space')), parts along dimension 1, may hold values from -6 to 6
- prior_weight: float32 [64, 4096], P('tm', ('parts', 'space')), parts along dimension 1, may hold values from 0.05 to 0.5
- footprint: bfloat16 [256, 64, 4096], P(('tm', 'stn'), None, ('parts', 'space')), parts along dimension 2, may hold values from 1 to 127, as said below
- block_scale: float32 [512, 64], P(('parts', 'tm', 'stn')), parts along dimension 0, as said below
- block_index: int32 [384, 16], P(('parts', 'tm'), 'stn'), parts along dimension 0, may hold values from 0 to 31
- foot_length: int32 [32], P(('parts', 'stn')), parts along dimension 0, may hold values from 1 to 64, as said below
- observed: float32 [384, 16], P(('parts', 'tm'), 'stn'), parts along dimension 0, may hold values from -12 to 12
- obs_weight: float32 [384, 16], P(('parts', 'tm'), 'stn'), parts along dimension 0, may hold values from 0.25 to 2
Outputs:
- weighted_residual: float32 [384, 16], P(('parts', 'tm'), 'stn'), parts along dimension 0
- gradient: float32 [64, 4096], P('tm', ('parts', 'space')), parts along dimension 1
There are 2 independent parts, one for each index of `parts`. A program takes and returns all parts, laid end to end along the dimension named above; each array names one. Nothing has to cross between parts.
Inputs may be any that keep to these rules, and one draw needn't show every extreme that they name: `foot_length`: some station has length 64 and some has length 1. `footprint`: integer codes. `block_scale`: positive.
All inputs are finite; a program needn't handle non-finite values.
Results may differ from a plain program's by a relative error of at most 0.0065.
Values may be sent and summed in bfloat16 or wider, within the bound.
No kernel may reach another device: no remote copies, remote signals or barrier semaphores. Data moves between devices by JAX's collectives and lax.ppermute only.
A program may use at most 64 MiB of HBM per device.

v0:
```python
import jax
import jax.numpy as jnp
from jax import lax
from jax.sharding import PartitionSpec as P


def shifted(x, axis, by):
    devices = lax.axis_size(axis)
    pairs = [(i, i + by) for i in range(devices) if 0 <= i + by < devices]
    return lax.ppermute(x, axis, pairs)


def on_device(
    fluxes, prior_weight, footprint, block_scale, block_index, foot_length, observed, obs_weight
):
    slot_count = fluxes.shape[0]
    cell_count = fluxes.shape[1]
    block_count = footprint.shape[0]
    lag_count = footprint.shape[1]
    hour_count = block_index.shape[0]
    width = slot_count + lag_count
    reach_back = lag_count // slot_count
    own_piece = fluxes.astype(jnp.bfloat16)
    pieces = [own_piece]
    moving = own_piece
    for distance in range(reach_back):
        moving = shifted(moving, "tm", 1)
        pieces.insert(0, moving)
    window_low = jnp.concatenate(pieces, 0)
    table_rows = footprint.reshape(block_count * lag_count, cell_count)
    products = jnp.einsum("kc,jc->kj", table_rows, window_low, preferred_element_type=jnp.float32)
    products = products.reshape(block_count, lag_count, width)
    lag_ids = jnp.arange(lag_count, dtype=jnp.int32)
    in_reach = (lag_ids[None, :] < foot_length[:, None]).astype(jnp.float32)
    hour_ids = jnp.arange(hour_count, dtype=jnp.int32)
    target = lag_count + hour_ids // 3
    choose = (
        jnp.arange(width, dtype=jnp.int32)[None, None, :]
        == target[:, None, None] - lag_ids[None, :, None]
    ).astype(jnp.float32)
    picker = (
        block_index[:, :, None] == jnp.arange(block_count, dtype=jnp.int32)[None, None, :]
    ).astype(jnp.float32)
    weights_lag = in_reach[None, :, :] * jnp.einsum("hsb,bl->hsl", picker, block_scale)
    per_row = jnp.einsum("hsb,blj->hslj", picker, products)
    along = jnp.einsum("hslj,hlj->hsl", per_row, choose)
    partial_model = jnp.sum(weights_lag * along, axis=2)
    modeled = lax.psum(partial_model, "space")
    resid = obs_weight * (modeled - observed)
    spread_rows = jnp.einsum("hsl,hlj->hslj", weights_lag * resid[:, :, None], choose)
    spread = jnp.einsum("hsb,hslj->blj", picker, spread_rows).astype(jnp.bfloat16)
    returned = jnp.einsum(
        "kj,kc->jc",
        spread.reshape(block_count * lag_count, width),
        table_rows,
        preferred_element_type=jnp.float32,
    )
    total = returned[lag_count:]
    for distance in range(1, reach_back + 1):
        start_row = (reach_back - distance) * slot_count
        piece = returned[start_row : start_row + slot_count]
        total = total + shifted(piece, "tm", -distance)
    summed = lax.psum(total, "stn")
    gradient = summed + prior_weight * fluxes
    return (resid, gradient)


def solution(mesh):
    placed = (
        P("tm", ("parts", "space")),
        P("tm", ("parts", "space")),
        P(("tm", "stn"), None, ("parts", "space")),
        P(("parts", "tm", "stn"), None),
        P(("parts", "tm"), "stn"),
        P(("parts", "stn")),
        P(("parts", "tm"), "stn"),
        P(("parts", "tm"), "stn"),
    )
    return jax.shard_map(
        on_device,
        mesh=mesh,
        in_specs=placed,
        out_specs=(P(("parts", "tm"), "stn"), P("tm", ("parts", "space"))),
        check_vma=False,
    )
```

profile of v0, /device:TPU:0, one launch (start us, length us, event | category | flops | bytes accessed | tf_op | source)
XLA Modules:
  0.0 108.2 jit_solution(10366744572349132630)
XLA Ops:
  8.1 4.9 %collective-permute-start = (bf16[16,1024]{1,0:T(8,128)(2,1)S(1)}, bf16[16,1024]{1,0:T(8,128)(2,1)S(1)}, u32[]{:S(2)}, u32[]{:S(2)}) collective-permute-start(bf16[16,1024]{1,0:T(8,128)(2,1)S(1)} %convert_element_type.16), channel_id=1, source_target_pairs={{0,4},{4,8},{8,12},{1,5},{5,9},{9,13},{2,6},{6,10},{10,14},{3,7},{... | collective-permute-start | bytes 98312 | tf_op jit(solution)/shard_map/ppermute | solution.py:10
  13.0 1.6 %collective-permute-done = bf16[16,1024]{1,0:T(8,128)(2,1)S(1)} collective-permute-done((bf16[16,1024]{1,0:T(8,128)(2,1)S(1)}, bf16[16,1024]{1,0:T(8,128)(2,1)S(1)}, u32[]{:S(2)}, u32[]{:S(2)}) %collective-permute-start) | collective-permute-done | bytes 32800 | tf_op jit(solution)/shard_map/ppermute | solution.py:10
  14.6 4.2 %collective-permute-start.1 = (bf16[16,1024]{1,0:T(8,128)(2,1)S(1)}, bf16[16,1024]{1,0:T(8,128)(2,1)S(1)}, u32[]{:S(2)}, u32[]{:S(2)}) collective-permute-start(bf16[16,1024]{1,0:T(8,128)(2,1)S(1)} %collective-permute-done), channel_id=1, source_target_pairs={{0,4},{4,8},{8,12},{1,5},{5,9},{9,13},{2,6},{6,10},{10,14},{3,7},{... | collective-permute-start | bytes 98312 | tf_op jit(solution)/shard_map/ppermute | solution.py:10
  18.9 1.5 %collective-permute-done.1 = bf16[16,1024]{1,0:T(8,128)(2,1)S(1)} collective-permute-done((bf16[16,1024]{1,0:T(8,128)(2,1)S(1)}, bf16[16,1024]{1,0:T(8,128)(2,1)S(1)}, u32[]{:S(2)}, u32[]{:S(2)}) %collective-permute-start.1) | collective-permute-done | bytes 32800 | tf_op jit(solution)/shard_map/ppermute | solution.py:10
  20.4 4.2 %collective-permute-start.2 = (bf16[16,1024]{1,0:T(8,128)(2,1)S(1)}, bf16[16,1024]{1,0:T(8,128)(2,1)S(1)}, u32[]{:S(2)}, u32[]{:S(2)}) collective-permute-start(bf16[16,1024]{1,0:T(8,128)(2,1)S(1)} %collective-permute-done.1), channel_id=1, source_target_pairs={{0,4},{4,8},{8,12},{1,5},{5,9},{9,13},{2,6},{6,10},{10,14},{3,7},{... | collective-permute-start | bytes 98312 | tf_op jit(solution)/shard_map/ppermute | solution.py:10
  25.1 1.1 %collective-permute-done.2 = bf16[16,1024]{1,0:T(8,128)(2,1)S(1)} collective-permute-done((bf16[16,1024]{1,0:T(8,128)(2,1)S(1)}, bf16[16,1024]{1,0:T(8,128)(2,1)S(1)}, u32[]{:S(2)}, u32[]{:S(2)}) %collective-permute-start.2) | collective-permute-done | bytes 32800 | tf_op jit(solution)/shard_map/ppermute | solution.py:10
  26.2 4.2 %collective-permute-start.3 = (bf16[16,1024]{1,0:T(8,128)(2,1)S(1)}, bf16[16,1024]{1,0:T(8,128)(2,1)S(1)}, u32[]{:S(2)}, u32[]{:S(2)}) collective-permute-start(bf16[16,1024]{1,0:T(8,128)(2,1)S(1)} %collective-permute-done.2), channel_id=1, source_target_pairs={{0,4},{4,8},{8,12},{1,5},{5,9},{9,13},{2,6},{6,10},{10,14},{3,7},{... | collective-permute-start | bytes 98312 | tf_op jit(solution)/shard_map/ppermute | solution.py:10
  30.4 1.3 %fusion.36 = f32[8,64]{1,0:T(8,128)} fusion(s32[8]{0:T(128)} %param.13), kind=kLoop, calls=%fused_computation.41 | loop fusion | flops 1024 | bytes 2080 | tf_op jit(solution)/shard_map/convert_element_type | solution.py:34
  32.8 3.6 %convolution_bitcast_fusion = bf16[2048,80]{0,1:T(8,128)(2,1)S(1)} fusion(bf16[80,1024]{1,0:T(8,128)(2,1)S(1)} %constant_dynamic-update-slice_fusion, bf16[2048,1024]{1,0:T(8,128)(2,1)} %bitcast.51), kind=kOutput, calls=%fused_computation.8 | convolution fusion | flops 335544320 | bytes 4685824 | tf_op jit(solution)/shard_map/kc,jc->kj/dot_general | solution.py:31
  37.1 1.2 %copy.12 = bf16[32,64,80]{2,0,1:T(8,128)(2,1)S(1)} copy(bf16[32,64,80]{1,0,2:T(8,128)(2,1)S(1)} %reshape.71) | data formatting | bytes 655360 | tf_op jit(solution)/shard_map/reshape | solution.py:32
  38.3 1.8 %fusion.18 = bf16[48,8,64,80]{3,0,2,1:T(8,128)(2,1)S(1)} fusion(bf16[32,64,80]{2,0,1:T(8,128)(2,1)S(1)} %copy.12, s32[48,8]{0,1:T(8,128)S(1)} %copy-done.3), kind=kOutput, calls=%fused_computation.16 | convolution fusion | flops 125841408 | bytes 4261376 | tf_op jit(solution)/shard_map/hsb,blj->hslj/dot_general | solution.py:45
  40.2 7.7 %fusion = f32[48,64,1,8]{3,2,1,0:T(1,128)S(1)} fusion(bf16[48,8,64,80]{3,0,2,1:T(8,128)(2,1)S(1)} %fusion.18, pred[48,64,80,1]{2,1,0,3:T(32,128)(4,1)S(1)} %get-tuple-element.7), kind=kOutput, calls=%fused_computation | convolution fusion | flops 3932160 | bytes 4276224 | tf_op jit(solution)/shard_map/hslj,hlj->hsl/dot_general | solution.py:46
  48.8 1.0 fusion.22
  49.8 4.9 %psum.14 = f32[48,8]{0,1:T(8,128)S(1)} all-reduce(f32[48,8]{0,1:T(8,128)S(1)} %get-tuple-element.8), channel_id=1, replica_groups=mesh['parts'=2,'tm'=4,'space'=2,'stn'=2] {'space'}, use_global_device_ids=true, to_apply=%region_1.2 | all-reduce | flops 384 | bytes 3072 | tf_op jit(solution)/shard_map/psum | solution.py:48
  56.1 4.8 %multiply_bitcast_fusion = bf16[48,8,64,80]{3,1,2,0:T(8,128)(2,1)} fusion(f32[48,64,8]{2,1,0:T(8,128)S(1)} %copy.13, f32[48,64,80]{2,1,0:T(8,128)S(1)} %get-tuple-element.6), kind=kLoop, calls=%fused_computation.4 | loop fusion | flops 3932160 | bytes 5013504 | tf_op jit(solution)/shard_map/hsl,hlj->hslj/transpose | solution.py:50
  60.9 10.1 %fusion.15 = f32[80,1024]{1,0:T(8,128)S(1)} fusion(bf16[32,64,1024]{2,1,0:T(8,128)(2,1)} %param.10, bf16[48,8,64,80]{3,1,2,0:T(8,128)(2,1)} %multiply_bitcast_fusion, s32[48,8]{0,1:T(8,128)S(1)} %copy-done.4), kind=kOutput, calls=%fused_computation.14 | convolution fusion | flops 461385728 | bytes 8455680 | tf_op jit(solution)/shard_map/kj,kc->jc/dot_general | solution.py:52
  71.0 1.3 %collective-permute-start.4 = (f32[16,1024]{1,0:T(8,128)S(1)}, f32[16,1024]{1,0:T(8,128)S(1)}, u32[]{:S(2)}, u32[]{:S(2)}) collective-permute-start(f32[16,1024]{1,0:T(8,128)S(1)} %get-tuple-element.2), channel_id=1, source_target_pairs={{4,0},{8,4},{12,8},{5,1},{9,5},{13,9},{6,2},{10,6},{14,10},{7,3},{... | collective-permute-start | bytes 196616 | tf_op jit(solution)/shard_map/ppermute | solution.py:10
  72.3 1.3 %collective-permute-start.5 = (f32[16,1024]{1,0:T(8,128)S(1)}, f32[16,1024]{1,0:T(8,128)S(1)}, u32[]{:S(2)}, u32[]{:S(2)}) collective-permute-start(f32[16,1024]{1,0:T(8,128)S(1)} %get-tuple-element.5), channel_id=1, source_target_pairs={{8,0},{12,4},{9,1},{13,5},{10,2},{14,6},{11,3},{15,7},{24,16},{28,... | collective-permute-start | bytes 196616 | tf_op jit(solution)/shard_map/ppermute | solution.py:10
  73.6 1.3 %collective-permute-start.6 = (f32[16,1024]{1,0:T(8,128)S(1)}, f32[16,1024]{1,0:T(8,128)S(1)}, u32[]{:S(2)}, u32[]{:S(2)}) collective-permute-start(f32[16,1024]{1,0:T(8,128)S(1)} %get-tuple-element.4), channel_id=1, source_target_pairs={{12,0},{13,1},{14,2},{15,3},{28,16},{29,17},{30,18},{31,19}} | collective-permute-start | bytes 196616 | tf_op jit(solution)/shard_map/ppermute | solution.py:10
  75.6 1.9 %collective-permute-done.4 = f32[16,1024]{1,0:T(8,128)S(1)} collective-permute-done((f32[16,1024]{1,0:T(8,128)S(1)}, f32[16,1024]{1,0:T(8,128)S(1)}, u32[]{:S(2)}, u32[]{:S(2)}) %collective-permute-start.4) | collective-permute-done | bytes 65568 | tf_op jit(solution)/shard_map/ppermute | solution.py:10
  77.5 2.8 %collective-permute-done.5 = f32[16,1024]{1,0:T(8,128)S(1)} collective-permute-done((f32[16,1024]{1,0:T(8,128)S(1)}, f32[16,1024]{1,0:T(8,128)S(1)}, u32[]{:S(2)}, u32[]{:S(2)}) %collective-permute-start.5) | collective-permute-done | bytes 65568 | tf_op jit(solution)/shard_map/ppermute | solution.py:10
  80.2 2.8 %collective-permute-done.6 = f32[16,1024]{1,0:T(8,128)S(1)} collective-permute-done((f32[16,1024]{1,0:T(8,128)S(1)}, f32[16,1024]{1,0:T(8,128)S(1)}, u32[]{:S(2)}, u32[]{:S(2)}) %collective-permute-start.6) | collective-permute-done | bytes 65568 | tf_op jit(solution)/shard_map/ppermute | solution.py:10
  83.8 16.1 %all-reduce.2.cloned.1.call-done = f32[16,1024]{1,0:T(8,128)} async-done(((f32[16,1024]{1,0:T(8,128)}), f32[16,1024]{1,0:T(8,128)}) %all-reduce.2.cloned.1.call-update) | async-done | bytes 65552 | tf_op jit(solution)/shard_map/psum | solution.py:63
  99.9 1.5 %multiply_add_fusion = f32[16,1024]{1,0:T(8,128)} fusion(f32[16,1024]{1,0:T(8,128)} %all-reduce.2.cloned.1.call-done, f32[16,1024]{1,0:T(8,128)S(1)} %copy-done.2, f32[16,1024]{1,0:T(8,128)S(1)} %copy-done.1), kind=kLoop, calls=%fused_computation.28 | loop fusion | flops 32768 | bytes 262144 | tf_op jit(solution)/shard_map/add | solution.py:64
  (33 shorter events, 6.8 us)
Async XLA Ops:
  7.2 41.6 %copy-start = (f32[32,64]{1,0:T(8,128)S(1)}, f32[32,64]{1,0:T(8,128)}, u32[]{:S(2)}) copy-start(f32[32,64]{1,0:T(8,128)} %param.11) | copy-start | bytes 24580
  7.2 92.7 %all-reduce.2.cloned.1.call-start = ((), (), s32[]{:S(2)}) async-start(), calls=%async_computation | async-start | bytes 131072 | tf_op jit(solution)/shard_map/psum | solution.py:63
  8.1 6.5 %collective-permute-start = (bf16[16,1024]{1,0:T(8,128)(2,1)S(1)}, bf16[16,1024]{1,0:T(8,128)(2,1)S(1)}, u32[]{:S(2)}, u32[]{:S(2)}) collective-permute-start(bf16[16,1024]{1,0:T(8,128)(2,1)S(1)} %convert_element_type.16), channel_id=1, source_target_pairs={{0,4},{4,8},{8,12},{1,5},{5,9},{9,13},{2,6},{6,10},{10,14},{3,7},{... | collective-permute-start | bytes 98312 | tf_op jit(solution)/shard_map/ppermute | solution.py:10
  14.6 5.8 %collective-permute-start.1 = (bf16[16,1024]{1,0:T(8,128)(2,1)S(1)}, bf16[16,1024]{1,0:T(8,128)(2,1)S(1)}, u32[]{:S(2)}, u32[]{:S(2)}) collective-permute-start(bf16[16,1024]{1,0:T(8,128)(2,1)S(1)} %collective-permute-done), channel_id=1, source_target_pairs={{0,4},{4,8},{8,12},{1,5},{5,9},{9,13},{2,6},{6,10},{10,14},{3,7},{... | collective-permute-start | bytes 98312 | tf_op jit(solution)/shard_map/ppermute | solution.py:10
  18.9 19.4 %copy-start.3 = (s32[48,8]{0,1:T(8,128)S(1)}, s32[48,8]{0,1:T(8,128)}, u32[]{:S(2)}) copy-start(s32[48,8]{0,1:T(8,128)} %param.12) | copy-start | bytes 4612
  20.4 5.8 %collective-permute-start.2 = (bf16[16,1024]{1,0:T(8,128)(2,1)S(1)}, bf16[16,1024]{1,0:T(8,128)(2,1)S(1)}, u32[]{:S(2)}, u32[]{:S(2)}) collective-permute-start(bf16[16,1024]{1,0:T(8,128)(2,1)S(1)} %collective-permute-done.1), channel_id=1, source_target_pairs={{0,4},{4,8},{8,12},{1,5},{5,9},{9,13},{2,6},{6,10},{10,14},{3,7},{... | collective-permute-start | bytes 98312 | tf_op jit(solution)/shard_map/ppermute | solution.py:10
  26.2 5.8 %collective-permute-start.3 = (bf16[16,1024]{1,0:T(8,128)(2,1)S(1)}, bf16[16,1024]{1,0:T(8,128)(2,1)S(1)}, u32[]{:S(2)}, u32[]{:S(2)}) collective-permute-start(bf16[16,1024]{1,0:T(8,128)(2,1)S(1)} %collective-permute-done.2), channel_id=1, source_target_pairs={{0,4},{4,8},{8,12},{1,5},{5,9},{9,13},{2,6},{6,10},{10,14},{3,7},{... | collective-permute-start | bytes 98312 | tf_op jit(solution)/shard_map/ppermute | solution.py:10
  55.5 5.4 %copy-start.5 = (f32[48,8]{0,1:T(8,128)}, f32[48,8]{0,1:T(8,128)S(1)}, u32[]{:S(2)}) copy-start(f32[48,8]{0,1:T(8,128)S(1)} %subtract_multiply_fusion) | copy-start | bytes 4612
  56.1 4.8 %copy-start.4 = (s32[48,8]{0,1:T(8,128)S(1)}, s32[48,8]{0,1:T(8,128)}, u32[]{:S(2)}) copy-start(s32[48,8]{0,1:T(8,128)} %param.12) | copy-start | bytes 4612
  60.9 38.9 %copy-start.1 = (f32[16,1024]{1,0:T(8,128)S(1)}, f32[16,1024]{1,0:T(8,128)}, u32[]{:S(2)}) copy-start(f32[16,1024]{1,0:T(8,128)} %param.8) | copy-start | bytes 196612
  60.9 38.9 %copy-start.2 = (f32[16,1024]{1,0:T(8,128)S(1)}, f32[16,1024]{1,0:T(8,128)}, u32[]{:S(2)}) copy-start(f32[16,1024]{1,0:T(8,128)} %param.9) | copy-start | bytes 196612
  71.0 6.5 %collective-permute-start.4 = (f32[16,1024]{1,0:T(8,128)S(1)}, f32[16,1024]{1,0:T(8,128)S(1)}, u32[]{:S(2)}, u32[]{:S(2)}) collective-permute-start(f32[16,1024]{1,0:T(8,128)S(1)} %get-tuple-element.2), channel_id=1, source_target_pairs={{4,0},{8,4},{12,8},{5,1},{9,5},{13,9},{6,2},{10,6},{14,10},{7,3},{... | collective-permute-start | bytes 196616 | tf_op jit(solution)/shard_map/ppermute | solution.py:10
  72.3 7.9 %collective-permute-start.5 = (f32[16,1024]{1,0:T(8,128)S(1)}, f32[16,1024]{1,0:T(8,128)S(1)}, u32[]{:S(2)}, u32[]{:S(2)}) collective-permute-start(f32[16,1024]{1,0:T(8,128)S(1)} %get-tuple-element.5), channel_id=1, source_target_pairs={{8,0},{12,4},{9,1},{13,5},{10,2},{14,6},{11,3},{15,7},{24,16},{28,... | collective-permute-start | bytes 196616 | tf_op jit(solution)/shard_map/ppermute | solution.py:10
  73.6 9.4 %collective-permute-start.6 = (f32[16,1024]{1,0:T(8,128)S(1)}, f32[16,1024]{1,0:T(8,128)S(1)}, u32[]{:S(2)}, u32[]{:S(2)}) collective-permute-start(f32[16,1024]{1,0:T(8,128)S(1)} %get-tuple-element.4), channel_id=1, source_target_pairs={{12,0},{13,1},{14,2},{15,3},{28,16},{29,17},{30,18},{31,19}} | collective-permute-start | bytes 196616 | tf_op jit(solution)/shard_map/ppermute | solution.py:10
  74.9 8.1 %collective-permute-start.7 = (f32[16,1024]{1,0:T(8,128)S(1)}, f32[16,1024]{1,0:T(8,128)S(1)}, u32[]{:S(2)}, u32[]{:S(2)}) collective-permute-start(f32[16,1024]{1,0:T(8,128)S(1)} %get-tuple-element.3), channel_id=1, source_target_pairs={} | collective-permute-start | bytes 196616 | tf_op jit(solution)/shard_map/ppermute | solution.py:10
Sparse Core Ops, SparseCore 0:
  83.9 15.9 all-reduce.1
where the time goes:
time: 109 us; the launch traced here: 108 us
  waiting for transfers between devices  28 us (26%)
  matrix products  24.3 us (22%)
  starting transfers between devices  22.1 us (20%)
  between operations  14.2 us (13%)
  other arithmetic  11.3 us (10%)
  blocking collectives  4.95 us (5%)
  local copies, waits for them, and re-layouts  3.3 us (3%)
    ppermute x8, starting transfers between devices, shifted(): return lax.ppermute(x, axis, pairs)  22.1 us
    psum x1, waiting for transfers between devices, on_device(): summed = lax.psum(total, 'stn')  16.1 us
    ppermute x8, waiting for transfers between devices, shifted(): return lax.ppermute(x, axis, pairs)  11.9 us
    dot_general x1, matrix products, on_device(): jnp.einsum('kj,kc->jc', spread.reshape(block_count * lag_count, width), t...  10.1 us
    dot_general x1, matrix products, on_device(): along = jnp.einsum('hslj,hlj->hsl', per_row, choose)  7.75 us
    psum x1, blocking collectives, on_device(): modeled = lax.psum(partial_model, 'space')  4.95 us
    transpose x1, other arithmetic, on_device(): jnp.einsum('hsl,hlj->hslj', weights_lag * resid[:, :, None], choose)  4.81 us
    dot_general x1, matrix products, on_device(): jnp.einsum('kc,jc->kj', table_rows, window_low, preferred_element_type=jn...  3.58 us
  transfers between devices with their start and end apart: 9, of which 8 were waited for; matrix products, arithmetic and copies ran while one was open for 2% of the time, Pallas kernels for 0%

commit v1 on v0

v1 whole, which is shorter than its diff:
```python
import functools

import jax
import jax.numpy as jnp
from jax import lax
from jax.experimental import pallas as pl
from jax.experimental.pallas import tpu as pltpu
from jax.sharding import PartitionSpec as P

F32 = jnp.float32
BF16 = jnp.bfloat16
GROUP = 4


def shifted(x, by):
    devices = lax.axis_size("tm")
    pairs = [(i, i + by) for i in range(devices) if 0 <= i + by < devices]
    return lax.ppermute(x, "tm", pairs)


def reach_mask(len_ref, lags, stations):
    shape = (GROUP * lags, GROUP * stations)
    lengths = jnp.concatenate([len_ref[...]] * GROUP, axis=1)
    row = lax.broadcasted_iota(jnp.int32, shape, 0)
    col = lax.broadcasted_iota(jnp.int32, shape, 1)
    same = (row // lags) == (col // stations)
    return jnp.where(same & ((row % lags) < lengths), 1.0, 0.0).astype(BF16)


def lane_scale(scale_ref, groups):
    return jnp.concatenate(
        [scale_ref[pl.ds(i, groups, stride=GROUP), :] for i in range(GROUP)], axis=1
    )


def lag_bits(lags, rows):
    lag = lax.broadcasted_iota(jnp.int32, (rows, GROUP * lags), 1) % lags
    return lag


def two_term_dot(x, mask, contract):
    high = x.astype(BF16)
    low = (x - high.astype(F32)).astype(BF16)
    dims = (((1,), (contract,)), ((), ()))
    return lax.dot_general(high, mask, dims, preferred_element_type=F32) + lax.dot_general(
        low, mask, dims, preferred_element_type=F32
    )


def skew_down(x, lags, slots):
    need = slots + lags
    rows = x.shape[0]
    if rows < need:
        x = jnp.concatenate([jnp.zeros((need - rows, x.shape[1]), x.dtype), x], 0)
    step = lags // 2
    while step >= 8:
        keep = x.shape[0] - step
        bit = (lag_bits(lags, keep) & step) != 0
        x = jnp.where(bit, x[:keep], x[step:])
        step //= 2
    while step >= 1:
        bit = (lag_bits(lags, x.shape[0]) & step) != 0
        x = jnp.where(bit, pltpu.roll(x, step, 0), x)
        step //= 2
    return x[x.shape[0] - slots :]


def skew_up(x, lags, rows):
    slots, lanes = x.shape
    x = jnp.concatenate([jnp.zeros((8, lanes), x.dtype), x], 0)
    step = 1
    while step < 8:
        bit = (lag_bits(lags, x.shape[0]) & step) != 0
        x = jnp.where(bit, pltpu.roll(x, x.shape[0] - step, 0), x)
        step *= 2
    while step < lags:
        gap = jnp.zeros((step, lanes), x.dtype)
        bit = (lag_bits(lags, x.shape[0] + step) & step) != 0
        x = jnp.where(bit, jnp.concatenate([x, gap], 0), jnp.concatenate([gap, x], 0))
        step *= 2
    return x[x.shape[0] - rows :]


def model_kernel(*refs):
    *piece_refs, table_ref, scale_ref, index_ref, len_ref, out_ref = refs
    blocks, lags, cells = table_ref.shape
    slots = piece_refs[0].shape[0]
    hours, stations = index_ref.shape
    per = hours // slots
    groups = blocks // GROUP
    window = jnp.concatenate([r[...].astype(BF16) for r in piece_refs], 0)
    scale = lane_scale(scale_ref, groups)
    mask = reach_mask(len_ref, lags, stations)
    terms = []
    for g in range(groups):
        table = table_ref[g * GROUP : (g + 1) * GROUP].reshape(GROUP * lags, cells)
        products = lax.dot_general(
            window, table, (((1,), (1,)), ((), ())), preferred_element_type=F32
        )
        terms.append(skew_down(products, lags, slots) * scale[g : g + 1])
    sums = two_term_dot(jnp.concatenate(terms, 0), mask, 0)
    lane_block = lax.broadcasted_iota(jnp.int32, (slots, GROUP * stations), 1) // stations
    for k in range(per):
        index = index_ref[pl.ds(k, slots, stride=per), :]
        first = jnp.concatenate([index] * GROUP, axis=1) - lane_block
        picked = jnp.zeros((slots, GROUP * stations), F32)
        for g in range(groups):
            picked = jnp.where(first == g * GROUP, sums[g * slots : (g + 1) * slots], picked)
        total = picked[:, :stations]
        for i in range(1, GROUP):
            total = total + picked[:, i * stations : (i + 1) * stations]
        out_ref[pl.ds(k, slots, stride=per), :] = total


def return_kernel(*refs):
    (mine_ref, other_ref, seen_ref, weight_ref, flux_ref, prior_ref, table_ref, scale_ref,
     index_ref, len_ref, resid_ref, own_ref, *rest) = refs
    *sent_refs, spread_ref = rest
    blocks, lags, cells = table_ref.shape
    slots = flux_ref.shape[0]
    hours, stations = index_ref.shape
    per = hours // slots
    groups = blocks // GROUP
    rows = spread_ref.shape[0]
    scale = lane_scale(scale_ref, groups)
    mask = reach_mask(len_ref, lags, stations)
    lane_block = lax.broadcasted_iota(jnp.int32, (slots, GROUP * stations), 1) // stations
    firsts, resids = [], []
    for k in range(per):
        at = (pl.ds(k, slots, stride=per), slice(None))
        resid = weight_ref[at] * (mine_ref[at] + other_ref[at] - seen_ref[at])
        resid_ref[at] = resid
        resids.append(jnp.concatenate([resid] * GROUP, axis=1))
        firsts.append(jnp.concatenate([index_ref[at]] * GROUP, axis=1) - lane_block)
    placed = []
    for g in range(groups):
        total = jnp.where(firsts[0] == g * GROUP, resids[0], 0.0)
        for k in range(1, per):
            total = total + jnp.where(firsts[k] == g * GROUP, resids[k], 0.0)
        placed.append(total)
    lagged = two_term_dot(jnp.concatenate(placed, 0), mask, 1)
    for g in range(groups):
        term = lagged[g * slots : (g + 1) * slots] * scale[g : g + 1]
        spread = skew_up(term, lags, rows).astype(BF16)
        spread_ref[:, g * GROUP * lags : (g + 1) * GROUP * lags] = spread
    table = table_ref[...].reshape(blocks * lags, cells)
    returned = jnp.dot(spread_ref[...], table, preferred_element_type=F32)
    own_ref[...] = returned[rows - slots :] + 0.5 * prior_ref[...] * flux_ref[...]
    for i, ref in enumerate(sent_refs):
        start = rows - slots * (i + 2)
        ref[...] = returned[start : start + slots].astype(ref.dtype)


VMEM = pl.BlockSpec(memory_space=pltpu.VMEM)


def on_device(
    fluxes, prior_weight, footprint, block_scale, block_index, foot_length, observed, obs_weight
):
    slots, cells = fluxes.shape
    blocks, lags, _ = footprint.shape
    hours, stations = block_index.shape
    far = min(lags // slots, lax.axis_size("tm") - 1)
    rows = slots * (far + 1)
    own = fluxes.astype(BF16)
    pieces = [shifted(own, d) for d in range(far, 0, -1)] + [own]
    lengths = foot_length.reshape(1, stations)
    flops = 2 * blocks * lags * cells * rows
    nbytes = blocks * lags * cells * 2
    cost = pl.CostEstimate(flops=flops, bytes_accessed=nbytes, transcendentals=0)
    params = pltpu.CompilerParams(vmem_limit_bytes=24 * 1024 * 1024)
    mine = pl.pallas_call(
        model_kernel,
        out_shape=jax.ShapeDtypeStruct((hours, stations), F32),
        in_specs=[VMEM] * (len(pieces) + 4),
        out_specs=VMEM,
        compiler_params=params,
        cost_estimate=cost,
    )(*pieces, footprint, block_scale, block_index, lengths)
    other = swapped_sum(mine, "space")
    piece = jax.ShapeDtypeStruct((slots, cells), F32)
    sent = jax.ShapeDtypeStruct((slots, cells), BF16)
    resid, total, *back = pl.pallas_call(
        return_kernel,
        out_shape=[jax.ShapeDtypeStruct((hours, stations), F32), piece] + [sent] * far,
        in_specs=[VMEM] * 10,
        out_specs=[VMEM] * (2 + far),
        scratch_shapes=[pltpu.VMEM((rows, blocks * lags), BF16)],
        compiler_params=params,
        cost_estimate=cost,
    )(mine, other, observed, obs_weight, fluxes, prior_weight, footprint, block_scale, block_index, lengths)
    for d in range(far, 0, -1):
        total = total + shifted(back[d - 1], -d).astype(F32)
    gradient = total + swapped_sum(total, "stn")
    return (resid, gradient)


def swapped_sum(x, axis):
    devices = lax.axis_size(axis)
    total = None
    for by in range(1, devices):
        moved = lax.ppermute(x, axis, [(i, (i + by) % devices) for i in range(devices)])
        total = moved if total is None else total + moved
    return total


def solution(mesh):
    placed = (
        P("tm", ("parts", "space")),
        P("tm", ("parts", "space")),
        P(("tm", "stn"), None, ("parts", "space")),
        P(("parts", "tm", "stn"), None),
        P(("parts", "tm"), "stn"),
        P(("parts", "stn")),
        P(("parts", "tm"), "stn"),
        P(("parts", "tm"), "stn"),
    )
    return jax.shard_map(
        on_device,
        mesh=mesh,
        in_specs=placed,
        out_specs=(P(("parts", "tm"), "stn"), P("tm", ("parts", "space"))),
        check_vma=False,
    )
```

time: 109 us -> 37.2 us (0.34)
  matrix products: 24.3 us -> 0 us
  waiting for transfers between devices: 28 us -> 8.09 us
  between operations: 14.2 us -> 0.77 us
  other arithmetic: 11.3 us -> 1.54 us
  starting transfers between devices: 22.1 us -> 16.2 us
  blocking collectives: 4.95 us -> 0 us
  local copies, waits for them, and re-layouts: 3.3 us -> 7.36 us
  Pallas kernels: 0 us -> 2.78 us
    dot_general x5 -> x0, matrix products: 24.3 us -> none  [the longest x1 10.1 us: on_device(): jnp.einsum('kj,kc->jc', spread.reshape(block_count * lag_count, width), t...]
    psum x1 -> x0, waiting for transfers between devices: 16.1 us -> none  [on_device(): summed = lax.psum(total, 'stn')]
    unnamed x16 -> x24, local copies, waits for them, and re-layouts: 0.05 us -> 7.36 us
    ppermute x8, starting transfers between devices: 22.1 us -> 16.2 us  [the longest x6 14.6 us: shifted(): return lax.ppermute(x, 'tm', pairs)]
    psum x1 -> x0, blocking collectives: 4.95 us -> none  [on_device(): modeled = lax.psum(partial_model, 'space')]
    transpose x1 -> x0, other arithmetic: 4.81 us -> none  [on_device(): jnp.einsum('hsl,hlj->hslj', weights_lag * resid[:, :, None], choose)]
    ppermute x8, waiting for transfers between devices: 11.9 us -> 8.09 us  [the longest x6 5.34 us: shifted(): return lax.ppermute(x, 'tm', pairs)]
    pallas_call x0 -> x2, Pallas kernels: none -> 2.78 us  [the longest x1 1.64 us: on_device(): pl.pallas_call(model_kernel, out_shape=jax.ShapeDtypeStruct((hours, stati...]
  transfers between devices with their start and end apart: 9 -> 8, of which waited for: 8 -> 6; matrix products, arithmetic and copies ran while one was open for 2% -> 4% of each run, Pallas kernels for 0% -> 0%
where the time goes in v1:
time: 37.2 us; the launch traced here: 36.8 us
  starting transfers between devices  16.2 us (44%)
  waiting for transfers between devices  8.09 us (22%)
  local copies, waits for them, and re-layouts  7.36 us (20%)
  Pallas kernels  2.78 us (7%)
  other arithmetic  1.54 us (4%)
  between operations  0.77 us (2%)
    ppermute x6, starting transfers between devices, shifted(): return lax.ppermute(x, 'tm', pairs)  14.6 us
    unnamed x24, local copies, waits for them, and re-layouts  7.36 us
    ppermute x6, waiting for transfers between devices, shifted(): return lax.ppermute(x, 'tm', pairs)  5.34 us
    ppermute x2, waiting for transfers between devices, swapped_sum(): lax.ppermute(x, axis, [(i, (i + by) % devices) for i in range(devices)])  2.75 us
    pallas_call x1, Pallas kernels, on_device(): pl.pallas_call(model_kernel, out_shape=jax.ShapeDtypeStruct((hours, stati...  1.64 us
    ppermute x2, starting transfers between devices, swapped_sum(): lax.ppermute(x, axis, [(i, (i + by) % devices) for i in range(devices)])  1.63 us
    pallas_call x1, Pallas kernels, on_device(): pl.pallas_call(return_kernel, out_shape=[jax.ShapeDtypeStruct((hours, sta...  1.14 us
    convert_element_type x1, other arithmetic, on_device(): own = fluxes.astype(BF16)  0.88 us
  transfers between devices with their start and end apart: 8, of which 6 were waited for; matrix products, arithmetic and copies ran while one was open for 4% of the time, Pallas kernels for 0%

profile of v1, /device:TPU:0, one launch (start us, length us, event | category | flops | bytes accessed | tf_op | source)
XLA Modules:
  0.0 36.8 jit_solution(2786936377749738984)
XLA Ops:
  0.7 0.9 %convert_element_type.12.refs_3_ = bf16[16,1024]{1,0:T(8,128)(2,1)S(1)} convert(f32[16,1024]{1,0:T(8,128)} %refs_4_.3) | non-fusion elementwise | flops 16384 | bytes 98304 | tf_op jit(solution)/shard_map/convert_element_type | solution.py:165
  1.6 4.9 %collective-permute-start.2 = (bf16[16,1024]{1,0:T(8,128)(2,1)S(1)}, bf16[16,1024]{1,0:T(8,128)(2,1)S(1)}, u32[]{:S(2)}, u32[]{:S(2)}) collective-permute-start(bf16[16,1024]{1,0:T(8,128)(2,1)S(1)} %convert_element_type.12.refs_3_), channel_id=1, source_target_pairs={{0,4},{4,8},{8,12},{1,5},{5,9},{9,13},{2,6},{6,10},{10,14},{3,7},{... | collective-permute-start | bytes 98312 | tf_op jit(solution)/shard_map/ppermute | solution.py:18
  6.5 4.5 %collective-permute-start.1 = (bf16[16,1024]{1,0:T(8,128)(2,1)S(1)}, bf16[16,1024]{1,0:T(8,128)(2,1)S(1)}, u32[]{:S(2)}, u32[]{:S(2)}) collective-permute-start(bf16[16,1024]{1,0:T(8,128)(2,1)S(1)} %convert_element_type.12.refs_3_), channel_id=1, source_target_pairs={{0,8},{4,12},{1,9},{5,13},{2,10},{6,14},{3,11},{7,15},{16,24},{20,... | collective-permute-start | bytes 98312 | tf_op jit(solution)/shard_map/ppermute | solution.py:18
  11.0 1.3 %collective-permute-start = (bf16[16,1024]{1,0:T(8,128)(2,1)S(1)}, bf16[16,1024]{1,0:T(8,128)(2,1)S(1)}, u32[]{:S(2)}, u32[]{:S(2)}) collective-permute-start(bf16[16,1024]{1,0:T(8,128)(2,1)S(1)} %convert_element_type.12.refs_3_), channel_id=1, source_target_pairs={{0,12},{1,13},{2,14},{3,15},{16,28},{17,29},{18,30},{19,31}} | collective-permute-start | bytes 98312 | tf_op jit(solution)/shard_map/ppermute | solution.py:18
  12.3 0.8 %copy.10.refs_6_.refs_8_ = s32[48,8]{1,0:T(8,128)S(1)} copy(s32[48,8]{0,1:T(8,128)} %param.12) | data formatting | bytes 3072 | tf_op args[4]
  13.1 0.8 %collective-permute-done.refs_0_ = bf16[16,1024]{1,0:T(8,128)(2,1)S(1)} collective-permute-done((bf16[16,1024]{1,0:T(8,128)(2,1)S(1)}, bf16[16,1024]{1,0:T(8,128)(2,1)S(1)}, u32[]{:S(2)}, u32[]{:S(2)}) %collective-permute-start) | collective-permute-done | bytes 32800 | tf_op jit(solution)/shard_map/ppermute | solution.py:18
  13.9 2.2 %copy-done = bf16[32,64,1024]{2,1,0:T(8,128)(2,1)S(1)} copy-done((bf16[32,64,1024]{2,1,0:T(8,128)(2,1)S(1)}, bf16[32,64,1024]{2,1,0:T(8,128)(2,1)}, u32[]{:S(2)}) %copy-start) | copy-done | bytes 4194328
  16.1 0.7 %copy-done.4 = f32[32,64]{1,0:T(8,128)S(1)} copy-done((f32[32,64]{1,0:T(8,128)S(1)}, f32[32,64]{1,0:T(8,128)}, u32[]{:S(2)}) %copy-start.4) | copy-done | bytes 8216
  16.8 0.7 %copy-done.6 = s32[8]{0:T(128)S(1)} copy-done((s32[8]{0:T(128)S(1)}, s32[8]{0:T(128)}, u32[]{:S(2)}) %copy-start.6) | copy-done | bytes 56
  17.4 1.6 %shard_map.95.refs_0_ = f32[48,8]{1,0:T(8,128)S(1)} custom-call(bf16[16,1024]{1,0:T(8,128)(2,1)S(1)} %collective-permute-done.refs_0_, bf16[16,1024]{1,0:T(8,128)(2,1)S(1)} %collective-permute-done.1.refs_1_, bf16[16,1024]{1,0:T(8,128)(2,1)S(1)} %collective-permute-done.2.refs_2_, bf16[16,1024]{1,0:T(8,128)(2,1)S(1)} %convert_element_type.12.refs_3_, ...), custom_call_target="tpu_custom_call" | custom-call | flops 268435456 | bytes 4194304 | tf_op jit(solution)/shard_map/pallas_call | solution.py:172
  19.1 1.6 %collective-permute-start.3 = (f32[48,8]{1,0:T(8,128)S(1)}, f32[48,8]{1,0:T(8,128)S(1)}, u32[]{:S(2)}, u32[]{:S(2)}) collective-permute-start(f32[48,8]{1,0:T(8,128)S(1)} %shard_map.95.refs_0_), channel_id=1, source_target_pairs={{0,2},{2,0},{1,3},{3,1},{4,6},{6,4},{5,7},{7,5},{8,10},{10,8},{9,1... | collective-permute-start | bytes 4616 | tf_op jit(solution)/shard_map/ppermute | solution.py:202
  20.7 0.1 copy.12.refs_3_
  20.8 2.2 %collective-permute-done.3.refs_1_ = f32[48,8]{1,0:T(8,128)S(1)} collective-permute-done((f32[48,8]{1,0:T(8,128)S(1)}, f32[48,8]{1,0:T(8,128)S(1)}, u32[]{:S(2)}, u32[]{:S(2)}) %collective-permute-start.3) | collective-permute-done | bytes 1568 | tf_op jit(solution)/shard_map/ppermute | solution.py:202
  23.0 2.2 %copy-done.1 = bf16[32,64,1024]{2,1,0:T(8,128)(2,1)S(1)} copy-done((bf16[32,64,1024]{2,1,0:T(8,128)(2,1)S(1)}, bf16[32,64,1024]{2,1,0:T(8,128)(2,1)}, u32[]{:S(2)}) %copy-start.1) | copy-done | bytes 4194328
  25.2 1.1 %shard_map.96 = (f32[48,8]{1,0:T(8,128)S(1)}, f32[16,1024]{1,0:T(8,128)S(1)}, bf16[16,1024]{1,0:T(8,128)(2,1)S(1)}, bf16[16,1024]{1,0:T(8,128)(2,1)S(1)}, bf16[16,1024]{1,0:T(8,128)(2,1)S(1)}) custom-call(f32[48,8]{1,0:T(8,128)S(1)} %shard_map.95.refs_0_, f32[48,8]{1,0:T(8,128)S(1)} %collective-permute-done.3.refs_1_, f32[48,8]{1,0:T(8,128)S(1)} %copy.11.refs_2_, ...), custom_call_target="tpu_custom_call" | custom-call | flops 268435456 | bytes 4194304 | tf_op jit(solution)/shard_map/pallas_call | solution.py:183
  26.3 1.3 %collective-permute-start.4 = (bf16[16,1024]{1,0:T(8,128)(2,1)S(1)}, bf16[16,1024]{1,0:T(8,128)(2,1)S(1)}, u32[]{:S(2)}, u32[]{:S(2)}) collective-permute-start(bf16[16,1024]{1,0:T(8,128)(2,1)S(1)} %get-tuple-element.9), channel_id=1, source_target_pairs={{12,0},{13,1},{14,2},{15,3},{28,16},{29,17},{30,18},{31,19}} | collective-permute-start | bytes 98312 | tf_op jit(solution)/shard_map/ppermute | solution.py:18
  27.6 1.3 %collective-permute-start.5 = (bf16[16,1024]{1,0:T(8,128)(2,1)S(1)}, bf16[16,1024]{1,0:T(8,128)(2,1)S(1)}, u32[]{:S(2)}, u32[]{:S(2)}) collective-permute-start(bf16[16,1024]{1,0:T(8,128)(2,1)S(1)} %get-tuple-element.10), channel_id=1, source_target_pairs={{8,0},{12,4},{9,1},{13,5},{10,2},{14,6},{11,3},{15,7},{24,16},{28,... | collective-permute-start | bytes 98312 | tf_op jit(solution)/shard_map/ppermute | solution.py:18
  28.9 1.3 %collective-permute-start.6 = (bf16[16,1024]{1,0:T(8,128)(2,1)S(1)}, bf16[16,1024]{1,0:T(8,128)(2,1)S(1)}, u32[]{:S(2)}, u32[]{:S(2)}) collective-permute-start(bf16[16,1024]{1,0:T(8,128)(2,1)S(1)} %get-tuple-element.11), channel_id=1, source_target_pairs={{4,0},{8,4},{12,8},{5,1},{9,5},{13,9},{6,2},{10,6},{14,10},{7,3},{... | collective-permute-start | bytes 98312 | tf_op jit(solution)/shard_map/ppermute | solution.py:18
  30.2 3.9 %collective-permute-done.4 = bf16[16,1024]{1,0:T(8,128)(2,1)S(1)} collective-permute-done((bf16[16,1024]{1,0:T(8,128)(2,1)S(1)}, bf16[16,1024]{1,0:T(8,128)(2,1)S(1)}, u32[]{:S(2)}, u32[]{:S(2)}) %collective-permute-start.4) | collective-permute-done | bytes 32800 | tf_op jit(solution)/shard_map/ppermute | solution.py:18
  34.1 0.3 collective-permute-done.5
  34.4 0.4 collective-permute-done.6
  34.9 0.7 %copy.14 = f32[48,8]{0,1:T(8,128)} copy(f32[48,8]{1,0:T(8,128)S(1)} %get-tuple-element.12) | data formatting | bytes 3072
  35.5 0.6 %collective-permute-done.7 = f32[16,1024]{1,0:T(8,128)S(1)} collective-permute-done((f32[16,1024]{1,0:T(8,128)S(1)}, f32[16,1024]{1,0:T(8,128)S(1)}, u32[]{:S(2)}, u32[]{:S(2)}) %collective-permute-start.7) | collective-permute-done | bytes 65568 | tf_op jit(solution)/shard_map/ppermute | solution.py:202
  36.1 0.6 %add.15 = f32[16,1024]{1,0:T(8,128)} add(f32[16,1024]{1,0:T(8,128)S(1)} %convert_add_fusion, f32[16,1024]{1,0:T(8,128)S(1)} %collective-permute-done.7) | non-fusion elementwise | flops 16384 | bytes 196608 | tf_op jit(solution)/shard_map/add | solution.py:194
  (21 shorter events, 0.2 us)
Async XLA Ops:
  0.6 22.4 %copy-start.2 = (f32[16,1024]{1,0:T(8,128)S(1)}, f32[16,1024]{1,0:T(8,128)}, u32[]{:S(2)}) copy-start(f32[16,1024]{1,0:T(8,128)} %refs_4_.3) | copy-start | bytes 196612
  0.6 22.3 %copy-start.5 = (f32[32,64]{1,0:T(8,128)S(1)}, f32[32,64]{1,0:T(8,128)}, u32[]{:S(2)}) copy-start(f32[32,64]{1,0:T(8,128)} %refs_7_.1) | copy-start | bytes 24580
  0.7 22.3 %copy-start.7 = (s32[8]{0:T(128)S(1)}, s32[8]{0:T(128)}, u32[]{:S(2)}) copy-start(s32[8]{0:T(128)} %param.13) | copy-start | bytes 100
  0.7 20.0 %copy-start.8 = (f32[48,8]{0,1:T(8,128)S(1)}, f32[48,8]{0,1:T(8,128)}, u32[]{:S(2)}) copy-start(f32[48,8]{0,1:T(8,128)} %param.14) | copy-start | bytes 4612
  0.7 20.1 %copy-start.9 = (f32[48,8]{0,1:T(8,128)S(1)}, f32[48,8]{0,1:T(8,128)}, u32[]{:S(2)}) copy-start(f32[48,8]{0,1:T(8,128)} %param.15) | copy-start | bytes 4612
  1.6 11.5 %collective-permute-start.2 = (bf16[16,1024]{1,0:T(8,128)(2,1)S(1)}, bf16[16,1024]{1,0:T(8,128)(2,1)S(1)}, u32[]{:S(2)}, u32[]{:S(2)}) collective-permute-start(bf16[16,1024]{1,0:T(8,128)(2,1)S(1)} %convert_element_type.12.refs_3_), channel_id=1, source_target_pairs={{0,4},{4,8},{8,12},{1,5},{5,9},{9,13},{2,6},{6,10},{10,14},{3,7},{... | collective-permute-start | bytes 98312 | tf_op jit(solution)/shard_map/ppermute | solution.py:18
  6.5 6.6 %collective-permute-start.1 = (bf16[16,1024]{1,0:T(8,128)(2,1)S(1)}, bf16[16,1024]{1,0:T(8,128)(2,1)S(1)}, u32[]{:S(2)}, u32[]{:S(2)}) collective-permute-start(bf16[16,1024]{1,0:T(8,128)(2,1)S(1)} %convert_element_type.12.refs_3_), channel_id=1, source_target_pairs={{0,8},{4,12},{1,9},{5,13},{2,10},{6,14},{3,11},{7,15},{16,24},{20,... | collective-permute-start | bytes 98312 | tf_op jit(solution)/shard_map/ppermute | solution.py:18
  11.0 2.9 %collective-permute-start = (bf16[16,1024]{1,0:T(8,128)(2,1)S(1)}, bf16[16,1024]{1,0:T(8,128)(2,1)S(1)}, u32[]{:S(2)}, u32[]{:S(2)}) collective-permute-start(bf16[16,1024]{1,0:T(8,128)(2,1)S(1)} %convert_element_type.12.refs_3_), channel_id=1, source_target_pairs={{0,12},{1,13},{2,14},{3,15},{16,28},{17,29},{18,30},{19,31}} | collective-permute-start | bytes 98312 | tf_op jit(solution)/shard_map/ppermute | solution.py:18
  13.9 2.2 %copy-start = (bf16[32,64,1024]{2,1,0:T(8,128)(2,1)S(1)}, bf16[32,64,1024]{2,1,0:T(8,128)(2,1)}, u32[]{:S(2)}) copy-start(bf16[32,64,1024]{2,1,0:T(8,128)(2,1)} %refs_6_.2) | copy-start | bytes 12582916
  16.1 0.7 %copy-start.4 = (f32[32,64]{1,0:T(8,128)S(1)}, f32[32,64]{1,0:T(8,128)}, u32[]{:S(2)}) copy-start(f32[32,64]{1,0:T(8,128)} %refs_7_.1) | copy-start | bytes 24580
  16.8 0.7 %copy-start.6 = (s32[8]{0:T(128)S(1)}, s32[8]{0:T(128)}, u32[]{:S(2)}) copy-start(s32[8]{0:T(128)} %param.13) | copy-start | bytes 100
  17.4 5.6 %copy-start.3 = (f32[16,1024]{1,0:T(8,128)S(1)}, f32[16,1024]{1,0:T(8,128)}, u32[]{:S(2)}) copy-start(f32[16,1024]{1,0:T(8,128)} %refs_5_.3) | copy-start | bytes 196612
  19.1 3.9 %collective-permute-start.3 = (f32[48,8]{1,0:T(8,128)S(1)}, f32[48,8]{1,0:T(8,128)S(1)}, u32[]{:S(2)}, u32[]{:S(2)}) collective-permute-start(f32[48,8]{1,0:T(8,128)S(1)} %shard_map.95.refs_0_), channel_id=1, source_target_pairs={{0,2},{2,0},{1,3},{3,1},{4,6},{6,4},{5,7},{7,5},{8,10},{10,8},{9,1... | collective-permute-start | bytes 4616 | tf_op jit(solution)/shard_map/ppermute | solution.py:202
  23.0 2.2 %copy-start.1 = (bf16[32,64,1024]{2,1,0:T(8,128)(2,1)S(1)}, bf16[32,64,1024]{2,1,0:T(8,128)(2,1)}, u32[]{:S(2)}) copy-start(bf16[32,64,1024]{2,1,0:T(8,128)(2,1)} %refs_6_.2) | copy-start | bytes 12582916
  26.3 7.8 %collective-permute-start.4 = (bf16[16,1024]{1,0:T(8,128)(2,1)S(1)}, bf16[16,1024]{1,0:T(8,128)(2,1)S(1)}, u32[]{:S(2)}, u32[]{:S(2)}) collective-permute-start(bf16[16,1024]{1,0:T(8,128)(2,1)S(1)} %get-tuple-element.9), channel_id=1, source_target_pairs={{12,0},{13,1},{14,2},{15,3},{28,16},{29,17},{30,18},{31,19}} | collective-permute-start | bytes 98312 | tf_op jit(solution)/shard_map/ppermute | solution.py:18
  27.6 6.8 %collective-permute-start.5 = (bf16[16,1024]{1,0:T(8,128)(2,1)S(1)}, bf16[16,1024]{1,0:T(8,128)(2,1)S(1)}, u32[]{:S(2)}, u32[]{:S(2)}) collective-permute-start(bf16[16,1024]{1,0:T(8,128)(2,1)S(1)} %get-tuple-element.10), channel_id=1, source_target_pairs={{8,0},{12,4},{9,1},{13,5},{10,2},{14,6},{11,3},{15,7},{24,16},{28,... | collective-permute-start | bytes 98312 | tf_op jit(solution)/shard_map/ppermute | solution.py:18
  28.9 5.8 %collective-permute-start.6 = (bf16[16,1024]{1,0:T(8,128)(2,1)S(1)}, bf16[16,1024]{1,0:T(8,128)(2,1)S(1)}, u32[]{:S(2)}, u32[]{:S(2)}) collective-permute-start(bf16[16,1024]{1,0:T(8,128)(2,1)S(1)} %get-tuple-element.11), channel_id=1, source_target_pairs={{4,0},{8,4},{12,8},{5,1},{9,5},{13,9},{6,2},{10,6},{14,10},{7,3},{... | collective-permute-start | bytes 98312 | tf_op jit(solution)/shard_map/ppermute | solution.py:18
  34.8 1.3 %collective-permute-start.7 = (f32[16,1024]{1,0:T(8,128)S(1)}, f32[16,1024]{1,0:T(8,128)S(1)}, u32[]{:S(2)}, u32[]{:S(2)}) collective-permute-start(f32[16,1024]{1,0:T(8,128)S(1)} %convert_add_fusion), channel_id=1, source_target_pairs={{0,1},{1,0},{2,3},{3,2},{4,5},{5,4},{6,7},{7,6},{8,9},{9,8},{10,11... | collective-permute-start | bytes 196616 | tf_op jit(solution)/shard_map/ppermute | solution.py:202

commit v2 on v1

--- a/solution.py
+++ b/solution.py
@@ -16,6 +16,17 @@
     devices = lax.axis_size("tm")
     pairs = [(i, i + by) for i in range(devices) if 0 <= i + by < devices]
     return lax.ppermute(x, "tm", pairs)
+
+
+def shared(x, near, far):
+    devices = lax.axis_size("tm")
+    pairs = [
+        (t * 2 + core, (t + by) * 2 + core)
+        for core, by in ((0, near + 1), (1, near))
+        for t in range(devices - by)
+        if by <= far
+    ]
+    return lax.ppermute(x, ("tm", "stn"), pairs)
 
 
 def reach_mask(len_ref, lags, stations):
@@ -81,16 +92,52 @@
     return x[x.shape[0] - rows :]
 
 
-def model_kernel(*refs):
-    *piece_refs, table_ref, scale_ref, index_ref, len_ref, out_ref = refs
+def prepare_kernel(
+    scale_hbm, index_hbm, len_hbm, seen_hbm, weight_hbm,
+    lane_scale_ref, mask_ref, first_ref, slot_seen_ref, slot_weight_ref,
+    scale_ref, index_ref, len_ref, seen_ref, weight_ref, swap_int, swap_float, sems
+):
+    sources = (scale_hbm, index_hbm, len_hbm, seen_hbm, weight_hbm)
+    targets = (scale_ref, index_ref, len_ref, seen_ref, weight_ref)
+    copies = [
+        pltpu.make_async_copy(source, target, sems.at[i])
+        for i, (source, target) in enumerate(zip(sources, targets))
+    ]
+    for copy in copies:
+        copy.start()
+    for copy in copies:
+        copy.wait()
+    groups, width = lane_scale_ref.shape
+    stations = index_ref.shape[0]
+    per, slots, _ = first_ref.shape
+    lane_scale_ref[...] = lane_scale(scale_ref, groups)
+    mask_ref[...] = reach_mask(len_ref, width // GROUP, stations)
+    lane_block = lax.broadcasted_iota(jnp.int32, (slots, GROUP * stations), 1) // stations
+    swap_int[...] = index_ref[...].T
+    for k in range(per):
+        index = swap_int[pl.ds(k, slots, stride=per), :]
+        first_ref[k] = jnp.concatenate([index] * GROUP, axis=1) - lane_block
+    for source, target in ((seen_ref, slot_seen_ref), (weight_ref, slot_weight_ref)):
+        swap_float[...] = source[...].T
+        for k in range(per):
+            target[k] = swap_float[pl.ds(k, slots, stride=per), :]
+
+
+def model_kernel(far, *refs):
+    *moved_refs, own_ref, table_ref, scale_ref, mask_ref, first_ref, out_ref = refs
     blocks, lags, cells = table_ref.shape
-    slots = piece_refs[0].shape[0]
-    hours, stations = index_ref.shape
-    per = hours // slots
+    per, slots, stations = out_ref.shape
     groups = blocks // GROUP
-    window = jnp.concatenate([r[...].astype(BF16) for r in piece_refs], 0)
-    scale = lane_scale(scale_ref, groups)
-    mask = reach_mask(len_ref, lags, stations)
+    core = lax.axis_index("stn")
+    got, swapped = moved_refs[: len(moved_refs) // 2], moved_refs[len(moved_refs) // 2 :]
+    pieces = [own_ref[...]]
+    for mine, other in zip(got, swapped):
+        pieces.append(jnp.where(core == 1, mine[...], other[...]))
+        pieces.append(jnp.where(core == 0, mine[...], other[...]))
+    pieces = pieces[: far + 1][::-1]
+    window = jnp.concatenate([p.astype(BF16) for p in pieces], 0)
+    scale = scale_ref[...]
+    mask = mask_ref[...]
     terms = []
     for g in range(groups):
         table = table_ref[g * GROUP : (g + 1) * GROUP].reshape(GROUP * lags, cells)
@@ -99,39 +146,33 @@
         )
         terms.append(skew_down(products, lags, slots) * scale[g : g + 1])
     sums = two_term_dot(jnp.concatenate(terms, 0), mask, 0)
-    lane_block = lax.broadcasted_iota(jnp.int32, (slots, GROUP * stations), 1) // stations
     for k in range(per):
-        index = index_ref[pl.ds(k, slots, stride=per), :]
-        first = jnp.concatenate([index] * GROUP, axis=1) - lane_block
+        first = first_ref[k]
         picked = jnp.zeros((slots, GROUP * stations), F32)
         for g in range(groups):
             picked = jnp.where(first == g * GROUP, sums[g * slots : (g + 1) * slots], picked)
         total = picked[:, :stations]
         for i in range(1, GROUP):
             total = total + picked[:, i * stations : (i + 1) * stations]
-        out_ref[pl.ds(k, slots, stride=per), :] = total
+        out_ref[k] = total
 
 
 def return_kernel(*refs):
     (mine_ref, other_ref, seen_ref, weight_ref, flux_ref, prior_ref, table_ref, scale_ref,
-     index_ref, len_ref, resid_ref, own_ref, *rest) = refs
-    *sent_refs, spread_ref = rest
+     mask_ref, first_ref, resid_ref, own_ref, *rest) = refs
+    *sent_refs, spread_ref, swap_float = rest
     blocks, lags, cells = table_ref.shape
-    slots = flux_ref.shape[0]
-    hours, stations = index_ref.shape
-    per = hours // slots
+    per, slots, stations = mine_ref.shape
     groups = blocks // GROUP
     rows = spread_ref.shape[0]
-    scale = lane_scale(scale_ref, groups)
-    mask = reach_mask(len_ref, lags, stations)
-    lane_block = lax.broadcasted_iota(jnp.int32, (slots, GROUP * stations), 1) // stations
+    scale = scale_ref[...]
+    mask = mask_ref[...]
     firsts, resids = [], []
     for k in range(per):
-        at = (pl.ds(k, slots, stride=per), slice(None))
-        resid = weight_ref[at] * (mine_ref[at] + other_ref[at] - seen_ref[at])
-        resid_ref[at] = resid
+        resid = weight_ref[k] * (mine_ref[k] + other_ref[k] - seen_ref[k])
+        swap_float[pl.ds(k, slots, stride=per), :] = resid
         resids.append(jnp.concatenate([resid] * GROUP, axis=1))
-        firsts.append(jnp.concatenate([index_ref[at]] * GROUP, axis=1) - lane_block)
+        firsts.append(first_ref[k])
     placed = []
     for g in range(groups):
         total = jnp.where(firsts[0] == g * GROUP, resids[0], 0.0)
@@ -145,12 +186,14 @@
         spread_ref[:, g * GROUP * lags : (g + 1) * GROUP * lags] = spread
     table = table_ref[...].reshape(blocks * lags, cells)
     returned = jnp.dot(spread_ref[...], table, preferred_element_type=F32)
+    resid_ref[...] = swap_float[...].T
     own_ref[...] = returned[rows - slots :] + 0.5 * prior_ref[...] * flux_ref[...]
     for i, ref in enumerate(sent_refs):
         start = rows - slots * (i + 2)
         ref[...] = returned[start : start + slots].astype(ref.dtype)
 
 
+PARAMS = pltpu.CompilerParams(vmem_limit_bytes=12 * 1024 * 1024)
 VMEM = pl.BlockSpec(memory_space=pltpu.VMEM)
 
 
@@ -162,37 +205,67 @@
     hours, stations = block_index.shape
     far = min(lags // slots, lax.axis_size("tm") - 1)
     rows = slots * (far + 1)
-    own = fluxes.astype(BF16)
-    pieces = [shifted(own, d) for d in range(far, 0, -1)] + [own]
-    lengths = foot_length.reshape(1, stations)
+    own = fluxes
+    got = [shared(own, d, far) for d in range(1, far + 1, 2)]
+    per = hours // slots
+    groups = blocks // GROUP
+    by_hour = jax.ShapeDtypeStruct((per, slots, stations), F32)
+    scale, mask, first, seen, weight = pl.pallas_call(
+        prepare_kernel,
+        out_shape=[
+            jax.ShapeDtypeStruct((groups, GROUP * lags), F32),
+            jax.ShapeDtypeStruct((GROUP * lags, GROUP * stations), BF16),
+            jax.ShapeDtypeStruct((per, slots, GROUP * stations), jnp.int32),
+            by_hour,
+            by_hour,
+        ],
+        in_specs=[pl.BlockSpec(memory_space=pltpu.HBM)] * 5,
+        out_specs=[VMEM] * 5,
+        scratch_shapes=[
+            pltpu.VMEM((blocks, lags), F32),
+            pltpu.VMEM((stations, hours), jnp.int32),
+            pltpu.VMEM((1, stations), jnp.int32),
+            pltpu.VMEM((stations, hours), F32),
+            pltpu.VMEM((stations, hours), F32),
+            pltpu.VMEM((hours, stations), jnp.int32),
+            pltpu.VMEM((hours, stations), F32),
+            pltpu.SemaphoreType.DMA((5,)),
+        ],
+        compiler_params=PARAMS,
+        cost_estimate=pl.CostEstimate(flops=2 * 10**10, bytes_accessed=10**5, transcendentals=0),
+    )(*[pltpu.with_memory_space_constraint(x, pltpu.HBM) for x in (block_scale, block_index.T, foot_length.reshape(1, stations), observed.T, obs_weight.T)])
+    got, scale, mask, first, seen, weight = lax.optimization_barrier(
+        (got, scale, mask, first, seen, weight)
+    )
+    both = swapped_sum(jnp.concatenate(got, 0), "stn")
+    pieces = got + [both[i * slots : (i + 1) * slots] for i in range(len(got))] + [own]
     flops = 2 * blocks * lags * cells * rows
     nbytes = blocks * lags * cells * 2
     cost = pl.CostEstimate(flops=flops, bytes_accessed=nbytes, transcendentals=0)
-    params = pltpu.CompilerParams(vmem_limit_bytes=24 * 1024 * 1024)
     mine = pl.pallas_call(
-        model_kernel,
-        out_shape=jax.ShapeDtypeStruct((hours, stations), F32),
+        functools.partial(model_kernel, far),
+        out_shape=by_hour,
         in_specs=[VMEM] * (len(pieces) + 4),
         out_specs=VMEM,
-        compiler_params=params,
+        compiler_params=PARAMS,
         cost_estimate=cost,
-    )(*pieces, footprint, block_scale, block_index, lengths)
+    )(*pieces, footprint, scale, mask, first)
     other = swapped_sum(mine, "space")
     piece = jax.ShapeDtypeStruct((slots, cells), F32)
     sent = jax.ShapeDtypeStruct((slots, cells), BF16)
     resid, total, *back = pl.pallas_call(
         return_kernel,
-        out_shape=[jax.ShapeDtypeStruct((hours, stations), F32), piece] + [sent] * far,
+        out_shape=[jax.ShapeDtypeStruct((stations, hours), F32), piece] + [sent] * far,
         in_specs=[VMEM] * 10,
         out_specs=[VMEM] * (2 + far),
-        scratch_shapes=[pltpu.VMEM((rows, blocks * lags), BF16)],
-        compiler_params=params,
+        scratch_shapes=[pltpu.VMEM((rows, blocks * lags), BF16), pltpu.VMEM((hours, stations), F32)],
+        compiler_params=PARAMS,
         cost_estimate=cost,
-    )(mine, other, observed, obs_weight, fluxes, prior_weight, footprint, block_scale, block_index, lengths)
+    )(mine, other, seen, weight, fluxes, prior_weight, footprint, scale, mask, first)
     for d in range(far, 0, -1):
         total = total + shifted(back[d - 1], -d).astype(F32)
     gradient = total + swapped_sum(total, "stn")
-    return (resid, gradient)
+    return (resid.T, gradient)
 
 
 def swapped_sum(x, axis):

time: 37.2 us -> 29.1 us (0.78)
  local copies, waits for them, and re-layouts: 7.36 us -> 0.02 us
  starting transfers between devices: 16.2 us -> 12.7 us
  waiting for transfers between devices: 8.09 us -> 10.3 us
  Pallas kernels: 2.78 us -> 4.4 us
  other arithmetic: 1.54 us -> 0.67 us
    ppermute x6 -> x3, starting transfers between devices: 14.6 us -> 3.86 us  [shifted(): return lax.ppermute(x, 'tm', pairs)]
    unnamed x24 -> x6, local copies, waits for them, and re-layouts: 7.36 us -> 0.01 us
    ppermute x0 -> x2, starting transfers between devices: none -> 6.61 us  [shared(): return lax.ppermute(x, ('tm', 'stn'), pairs)]
    ppermute x2 -> x3, waiting for transfers between devices: 2.75 us -> 4.57 us  [swapped_sum(): lax.ppermute(x, axis, [(i, (i + by) % devices) for i in range(devices)])]
    pallas_call x2 -> x3, Pallas kernels: 2.78 us -> 4.4 us  [the longest x1 1.64 us: on_device(): pl.pallas_call(functools.partial(model_kernel, far), out_shape=by_hour, i...]
    ppermute x0 -> x2, waiting for transfers between devices: none -> 1.12 us  [shared(): return lax.ppermute(x, ('tm', 'stn'), pairs)]
    convert_element_type x1 -> x0, other arithmetic: 0.88 us -> none  [on_device(): own = fluxes.astype(BF16)]
    ppermute x6 -> x3, waiting for transfers between devices: 5.34 us -> 4.58 us  [shifted(): return lax.ppermute(x, 'tm', pairs)]
  transfers between devices with their start and end apart: 8 -> 8, of which waited for: 6 -> 7; matrix products, arithmetic and copies ran while one was open for 4% -> 0% of each run, Pallas kernels for 0% -> 4%
where the time goes in v2:
time: 29.1 us; the launch traced here: 28.8 us
  starting transfers between devices  12.7 us (44%)
  waiting for transfers between devices  10.3 us (35%)
  Pallas kernels  4.4 us (15%)
  between operations  0.76 us (3%)
  other arithmetic  0.67 us (2%)
    ppermute x2, starting transfers between devices, shared(): return lax.ppermute(x, ('tm', 'stn'), pairs)  6.61 us
    ppermute x3, waiting for transfers between devices, shifted(): return lax.ppermute(x, 'tm', pairs)  4.58 us
    ppermute x3, waiting for transfers between devices, swapped_sum(): lax.ppermute(x, axis, [(i, (i + by) % devices) for i in range(devices)])  4.57 us
    ppermute x3, starting transfers between devices, shifted(): return lax.ppermute(x, 'tm', pairs)  3.86 us
    ppermute x3, starting transfers between devices, swapped_sum(): lax.ppermute(x, axis, [(i, (i + by) % devices) for i in range(devices)])  2.26 us
    pallas_call x1, Pallas kernels, on_device(): pl.pallas_call(functools.partial(model_kernel, far), out_shape=by_hour, i...  1.64 us
    pallas_call x1, Pallas kernels, on_device(): pl.pallas_call(return_kernel, out_shape=[jax.ShapeDtypeStruct((stations,...  1.59 us
    pallas_call x1, Pallas kernels, on_device(): pl.pallas_call(prepare_kernel, out_shape=[jax.ShapeDtypeStruct((groups, G...  1.18 us
  transfers between devices with their start and end apart: 8, of which 7 were waited for; matrix products, arithmetic and copies ran while one was open for 0% of the time, Pallas kernels for 4%

profile of v2, /device:TPU:0, one launch (start us, length us, event | category | flops | bytes accessed | tf_op | source)
XLA Modules:
  0.0 28.8 jit_solution(9415581415891595241)
XLA Ops:
  0.6 0.7 %collective-permute-start.1 = (f32[16,1024]{1,0:T(8,128)}, f32[16,1024]{1,0:T(8,128)S(1)}, u32[]{:S(2)}, u32[]{:S(2)}) collective-permute-start(f32[16,1024]{1,0:T(8,128)} %refs_4_.3), channel_id=1, source_target_pairs={{1,13},{3,15},{17,29},{19,31}} | collective-permute-start | bytes 196616 | tf_op jit(solution)/shard_map/ppermute | solution.py:29
  1.3 5.9 %collective-permute-start = (f32[16,1024]{1,0:T(8,128)}, f32[16,1024]{1,0:T(8,128)S(1)}, u32[]{:S(2)}, u32[]{:S(2)}) collective-permute-start(f32[16,1024]{1,0:T(8,128)} %refs_4_.3), channel_id=1, source_target_pairs={{0,8},{4,12},{1,5},{5,9},{9,13},{2,10},{6,14},{3,7},{7,11},{11,15}... | collective-permute-start | bytes 196616 | tf_op jit(solution)/shard_map/ppermute | solution.py:29
  7.3 0.0 copy-start
  7.3 0.0 copy-start.1
  7.3 1.2 %shard_map.95 = (f32[8,256]{1,0:T(8,128)S(1)}, bf16[256,32]{1,0:T(8,128)(2,1)S(1)}, s32[3,16,32]{2,1,0:T(8,128)S(1)}, f32[3,16,8]{2,1,0:T(8,128)S(1)}, f32[3,16,8]{2,1,0:T(8,128)S(1)}) custom-call(f32[32,64]{1,0:T(8,128)} %scale_hbm.1, s32[8,48]{1,0:T(8,128)} %bitcast.5, s32[1,8]{1,0:T(1,128)} %bitcast.9, f32[8,48]{1,0:T(8,128)} %bitcast.6, f32[8,48]{1,0:T(8,128)} %bitcast.7), custom_call_target="tpu_custom_call" | custom-call | flops 20000000000 | bytes 100000 | tf_op jit(solution)/shard_map/pallas_call | solution.py:213
  8.5 0.0 copy-start.2
  8.5 0.0 collective-permute-done.1.refs_1_
  8.5 1.1 %collective-permute-done.refs_0_ = f32[16,1024]{1,0:T(8,128)S(1)} collective-permute-done((f32[16,1024]{1,0:T(8,128)}, f32[16,1024]{1,0:T(8,128)S(1)}, u32[]{:S(2)}, u32[]{:S(2)}) %collective-permute-start) | collective-permute-done | bytes 65568 | tf_op jit(solution)/shard_map/ppermute | solution.py:29
  9.6 0.6 %collective-permute-start.2 = (f32[32,1024]{1,0:T(8,128)S(1)}, f32[32,1024]{1,0:T(8,128)S(1)}, u32[]{:S(2)}, u32[]{:S(2)}) collective-permute-start(f32[32,1024]{1,0:T(8,128)S(1)} %pad_maximum_fusion), channel_id=1, source_target_pairs={{0,1},{1,0},{2,3},{3,2},{4,5},{5,4},{6,7},{7,6},{8,9},{9,8},{10,11... | collective-permute-start | bytes 393224 | tf_op jit(solution)/shard_map/ppermute | solution.py:275
  10.2 1.0 %collective-permute-done.2 = f32[32,1024]{1,0:T(8,128)S(1)} collective-permute-done((f32[32,1024]{1,0:T(8,128)S(1)}, f32[32,1024]{1,0:T(8,128)S(1)}, u32[]{:S(2)}, u32[]{:S(2)}) %collective-permute-start.2) | collective-permute-done | bytes 131104 | tf_op jit(solution)/shard_map/ppermute | solution.py:275
  11.2 0.0 copy-done
  11.3 1.6 %shard_map.96.refs_0_ = f32[3,16,8]{2,1,0:T(8,128)S(1)} custom-call(f32[16,1024]{1,0:T(8,128)S(1)} %collective-permute-done.refs_0_, f32[16,1024]{1,0:T(8,128)S(1)} %collective-permute-done.1.refs_1_, f32[16,1024]{1,0:T(8,128)S(1)} %get-tuple-element.37.refs_2_, f32[16,1024]{1,0:T(8,128)S(1)} %get-tuple-element.36.refs_3_, f32[16,1024]{1,0:T(8,128)S(1)} %copy-done.1, ...), custom_call_target="tpu_custom_call" | custom-call | flops 268435456 | bytes 4194304 | tf_op jit(solution)/shard_map/pallas_call | solution.py:245
  12.9 1.6 %collective-permute-start.3 = (f32[3,16,8]{2,1,0:T(8,128)S(1)}, f32[3,16,8]{2,1,0:T(8,128)S(1)}, u32[]{:S(2)}, u32[]{:S(2)}) collective-permute-start(f32[3,16,8]{2,1,0:T(8,128)S(1)} %shard_map.96.refs_0_), channel_id=1, source_target_pairs={{0,2},{2,0},{1,3},{3,1},{4,6},{6,4},{5,7},{7,5},{8,10},{10,8},{9,1... | collective-permute-start | bytes 4616 | tf_op jit(solution)/shard_map/ppermute | solution.py:275
  14.5 2.3 %collective-permute-done.3.refs_1_ = f32[3,16,8]{2,1,0:T(8,128)S(1)} collective-permute-done((f32[3,16,8]{2,1,0:T(8,128)S(1)}, f32[3,16,8]{2,1,0:T(8,128)S(1)}, u32[]{:S(2)}, u32[]{:S(2)}) %collective-permute-start.3) | collective-permute-done | bytes 1568 | tf_op jit(solution)/shard_map/ppermute | solution.py:275
  16.8 1.6 %shard_map.97 = (f32[8,48]{1,0:T(8,128)}, f32[16,1024]{1,0:T(8,128)S(1)}, bf16[16,1024]{1,0:T(8,128)(2,1)S(1)}, bf16[16,1024]{1,0:T(8,128)(2,1)S(1)}, bf16[16,1024]{1,0:T(8,128)(2,1)S(1)}) custom-call(f32[3,16,8]{2,1,0:T(8,128)S(1)} %shard_map.96.refs_0_, f32[3,16,8]{2,1,0:T(8,128)S(1)} %collective-permute-done.3.refs_1_, ...), custom_call_target="tpu_custom_call" | custom-call | flops 268435456 | bytes 4194304 | tf_op jit(solution)/shard_map/pallas_call | solution.py:256
  18.4 1.3 %collective-permute-start.4 = (bf16[16,1024]{1,0:T(8,128)(2,1)S(1)}, bf16[16,1024]{1,0:T(8,128)(2,1)S(1)}, u32[]{:S(2)}, u32[]{:S(2)}) collective-permute-start(bf16[16,1024]{1,0:T(8,128)(2,1)S(1)} %get-tuple-element.33), channel_id=1, source_target_pairs={{12,0},{13,1},{14,2},{15,3},{28,16},{29,17},{30,18},{31,19}} | collective-permute-start | bytes 98312 | tf_op jit(solution)/shard_map/ppermute | solution.py:18
  19.7 1.3 %collective-permute-start.5 = (bf16[16,1024]{1,0:T(8,128)(2,1)S(1)}, bf16[16,1024]{1,0:T(8,128)(2,1)S(1)}, u32[]{:S(2)}, u32[]{:S(2)}) collective-permute-start(bf16[16,1024]{1,0:T(8,128)(2,1)S(1)} %get-tuple-element.34), channel_id=1, source_target_pairs={{8,0},{12,4},{9,1},{13,5},{10,2},{14,6},{11,3},{15,7},{24,16},{28,... | collective-permute-start | bytes 98312 | tf_op jit(solution)/shard_map/ppermute | solution.py:18
  21.0 1.3 %collective-permute-start.6 = (bf16[16,1024]{1,0:T(8,128)(2,1)S(1)}, bf16[16,1024]{1,0:T(8,128)(2,1)S(1)}, u32[]{:S(2)}, u32[]{:S(2)}) collective-permute-start(bf16[16,1024]{1,0:T(8,128)(2,1)S(1)} %get-tuple-element.35), channel_id=1, source_target_pairs={{4,0},{8,4},{12,8},{5,1},{9,5},{13,9},{6,2},{10,6},{14,10},{7,3},{... | collective-permute-start | bytes 98312 | tf_op jit(solution)/shard_map/ppermute | solution.py:18
  22.3 3.7 %collective-permute-done.4 = bf16[16,1024]{1,0:T(8,128)(2,1)S(1)} collective-permute-done((bf16[16,1024]{1,0:T(8,128)(2,1)S(1)}, bf16[16,1024]{1,0:T(8,128)(2,1)S(1)}, u32[]{:S(2)}, u32[]{:S(2)}) %collective-permute-start.4) | collective-permute-done | bytes 32800 | tf_op jit(solution)/shard_map/ppermute | solution.py:18
  26.0 0.6 %collective-permute-done.5 = bf16[16,1024]{1,0:T(8,128)(2,1)S(1)} collective-permute-done((bf16[16,1024]{1,0:T(8,128)(2,1)S(1)}, bf16[16,1024]{1,0:T(8,128)(2,1)S(1)}, u32[]{:S(2)}, u32[]{:S(2)}) %collective-permute-start.5) | collective-permute-done | bytes 32800 | tf_op jit(solution)/shard_map/ppermute | solution.py:18
  26.6 0.3 collective-permute-done.6
  26.9 0.1 collective-permute-start.7
  27.0 1.2 %collective-permute-done.7 = f32[16,1024]{1,0:T(8,128)S(1)} collective-permute-done((f32[16,1024]{1,0:T(8,128)S(1)}, f32[16,1024]{1,0:T(8,128)S(1)}, u32[]{:S(2)}, u32[]{:S(2)}) %collective-permute-start.7) | collective-permute-done | bytes 65568 | tf_op jit(solution)/shard_map/ppermute | solution.py:275
  28.2 0.6 %add.15 = f32[16,1024]{1,0:T(8,128)} add(f32[16,1024]{1,0:T(8,128)S(1)} %convert_add_fusion, f32[16,1024]{1,0:T(8,128)S(1)} %collective-permute-done.7) | non-fusion elementwise | flops 16384 | bytes 196608 | tf_op jit(solution)/shard_map/add | solution.py:267
  (5 shorter events, 0.0 us)
Async XLA Ops:
  0.6 7.8 %collective-permute-start.1 = (f32[16,1024]{1,0:T(8,128)}, f32[16,1024]{1,0:T(8,128)S(1)}, u32[]{:S(2)}, u32[]{:S(2)}) collective-permute-start(f32[16,1024]{1,0:T(8,128)} %refs_4_.3), channel_id=1, source_target_pairs={{1,13},{3,15},{17,29},{19,31}} | collective-permute-start | bytes 196616 | tf_op jit(solution)/shard_map/ppermute | solution.py:29
  1.3 8.3 %collective-permute-start = (f32[16,1024]{1,0:T(8,128)}, f32[16,1024]{1,0:T(8,128)S(1)}, u32[]{:S(2)}, u32[]{:S(2)}) collective-permute-start(f32[16,1024]{1,0:T(8,128)} %refs_4_.3), channel_id=1, source_target_pairs={{0,8},{4,12},{1,5},{5,9},{9,13},{2,10},{6,14},{3,7},{7,11},{11,15}... | collective-permute-start | bytes 196616 | tf_op jit(solution)/shard_map/ppermute | solution.py:29
  7.3 4.0 %copy-start = (bf16[32,64,1024]{2,1,0:T(8,128)(2,1)S(1)}, bf16[32,64,1024]{2,1,0:T(8,128)(2,1)}, u32[]{:S(2)}) copy-start(bf16[32,64,1024]{2,1,0:T(8,128)(2,1)} %refs_6_.1) | copy-start | bytes 12582916
  7.3 4.0 %copy-start.1 = (f32[16,1024]{1,0:T(8,128)S(1)}, f32[16,1024]{1,0:T(8,128)}, u32[]{:S(2)}) copy-start(f32[16,1024]{1,0:T(8,128)} %refs_4_.3) | copy-start | bytes 196612
  8.5 8.3 %copy-start.2 = (f32[16,1024]{1,0:T(8,128)S(1)}, f32[16,1024]{1,0:T(8,128)}, u32[]{:S(2)}) copy-start(f32[16,1024]{1,0:T(8,128)} %refs_5_.3) | copy-start | bytes 196612
  9.6 1.6 %collective-permute-start.2 = (f32[32,1024]{1,0:T(8,128)S(1)}, f32[32,1024]{1,0:T(8,128)S(1)}, u32[]{:S(2)}, u32[]{:S(2)}) collective-permute-start(f32[32,1024]{1,0:T(8,128)S(1)} %pad_maximum_fusion), channel_id=1, source_target_pairs={{0,1},{1,0},{2,3},{3,2},{4,5},{5,4},{6,7},{7,6},{8,9},{9,8},{10,11... | collective-permute-start | bytes 393224 | tf_op jit(solution)/shard_map/ppermute | solution.py:275
  12.9 3.9 %collective-permute-start.3 = (f32[3,16,8]{2,1,0:T(8,128)S(1)}, f32[3,16,8]{2,1,0:T(8,128)S(1)}, u32[]{:S(2)}, u32[]{:S(2)}) collective-permute-start(f32[3,16,8]{2,1,0:T(8,128)S(1)} %shard_map.96.refs_0_), channel_id=1, source_target_pairs={{0,2},{2,0},{1,3},{3,1},{4,6},{6,4},{5,7},{7,5},{8,10},{10,8},{9,1... | collective-permute-start | bytes 4616 | tf_op jit(solution)/shard_map/ppermute | solution.py:275
  18.4 7.6 %collective-permute-start.4 = (bf16[16,1024]{1,0:T(8,128)(2,1)S(1)}, bf16[16,1024]{1,0:T(8,128)(2,1)S(1)}, u32[]{:S(2)}, u32[]{:S(2)}) collective-permute-start(bf16[16,1024]{1,0:T(8,128)(2,1)S(1)} %get-tuple-element.33), channel_id=1, source_target_pairs={{12,0},{13,1},{14,2},{15,3},{28,16},{29,17},{30,18},{31,19}} | collective-permute-start | bytes 98312 | tf_op jit(solution)/shard_map/ppermute | solution.py:18
  19.7 6.9 %collective-permute-start.5 = (bf16[16,1024]{1,0:T(8,128)(2,1)S(1)}, bf16[16,1024]{1,0:T(8,128)(2,1)S(1)}, u32[]{:S(2)}, u32[]{:S(2)}) collective-permute-start(bf16[16,1024]{1,0:T(8,128)(2,1)S(1)} %get-tuple-element.34), channel_id=1, source_target_pairs={{8,0},{12,4},{9,1},{13,5},{10,2},{14,6},{11,3},{15,7},{24,16},{28,... | collective-permute-start | bytes 98312 | tf_op jit(solution)/shard_map/ppermute | solution.py:18
  21.0 5.9 %collective-permute-start.6 = (bf16[16,1024]{1,0:T(8,128)(2,1)S(1)}, bf16[16,1024]{1,0:T(8,128)(2,1)S(1)}, u32[]{:S(2)}, u32[]{:S(2)}) collective-permute-start(bf16[16,1024]{1,0:T(8,128)(2,1)S(1)} %get-tuple-element.35), channel_id=1, source_target_pairs={{4,0},{8,4},{12,8},{5,1},{9,5},{13,9},{6,2},{10,6},{14,10},{7,3},{... | collective-permute-start | bytes 98312 | tf_op jit(solution)/shard_map/ppermute | solution.py:18
  26.9 1.3 %collective-permute-start.7 = (f32[16,1024]{1,0:T(8,128)S(1)}, f32[16,1024]{1,0:T(8,128)S(1)}, u32[]{:S(2)}, u32[]{:S(2)}) collective-permute-start(f32[16,1024]{1,0:T(8,128)S(1)} %convert_add_fusion), channel_id=1, source_target_pairs={{0,1},{1,0},{2,3},{3,2},{4,5},{5,4},{6,7},{7,6},{8,9},{9,8},{10,11... | collective-permute-start | bytes 196616 | tf_op jit(solution)/shard_map/ppermute | solution.py:275

commit v3 on v1

--- a/solution.py
+++ b/solution.py
@@ -12,10 +12,19 @@
 GROUP = 4
 
 
-def shifted(x, by):
+def rolled(x, by):
     devices = lax.axis_size("tm")
-    pairs = [(i, i + by) for i in range(devices) if 0 <= i + by < devices]
-    return lax.ppermute(x, "tm", pairs)
+    return lax.ppermute(x, "tm", [(t, (t + by) % devices) for t in range(devices)])
+
+
+def shared(x, near):
+    devices = lax.axis_size("tm")
+    pairs = [
+        (t * 2 + core, (t + near + 1 - core) % devices * 2 + core)
+        for t in range(devices)
+        for core in (0, 1)
+    ]
+    return lax.ppermute(x, ("tm", "stn"), pairs)
 
 
 def reach_mask(len_ref, lags, stations):
@@ -81,16 +90,45 @@
     return x[x.shape[0] - rows :]
 
 
-def model_kernel(*refs):
-    *piece_refs, table_ref, scale_ref, index_ref, len_ref, out_ref = refs
+def round_kernel(flux_hbm, out_ref, flux_ref, sem):
+    copy = pltpu.make_async_copy(flux_hbm, flux_ref, sem)
+    copy.start()
+    copy.wait()
+    out_ref[...] = flux_ref[...].astype(out_ref.dtype)
+
+
+def model_kernel(far, *refs):
+    moved_refs = refs[: far]
+    (own_ref, table_ref, block_scale_ref, index_ref, len_ref, seen_ref, weight_ref,
+     out_ref, scale_ref, mask_ref, first_ref, slot_seen_ref, slot_weight_ref,
+     swap_int, swap_float) = refs[far:]
     blocks, lags, cells = table_ref.shape
-    slots = piece_refs[0].shape[0]
-    hours, stations = index_ref.shape
-    per = hours // slots
+    per, slots, stations = out_ref.shape
     groups = blocks // GROUP
-    window = jnp.concatenate([r[...].astype(BF16) for r in piece_refs], 0)
-    scale = lane_scale(scale_ref, groups)
+    core, shard = lax.axis_index("stn"), lax.axis_index("tm")
+    pieces = [own_ref[...]]
+    for near in range(1, far + 1, 2):
+        if near == far:
+            both = [moved_refs[near - 1][...]]
+        else:
+            mine, other = moved_refs[near - 1][...], moved_refs[near][...]
+            both = [jnp.where(core == 1, mine, other), jnp.where(core == 0, mine, other)]
+        for distance, piece in enumerate(both, near):
+            pieces.append(jnp.where(shard >= distance, piece, jnp.zeros_like(piece)))
+    window = jnp.concatenate(pieces[::-1], 0)
+    scale = lane_scale(block_scale_ref, groups)
+    scale_ref[...] = scale
     mask = reach_mask(len_ref, lags, stations)
+    mask_ref[...] = mask
+    lane_block = lax.broadcasted_iota(jnp.int32, (slots, GROUP * stations), 1) // stations
+    swap_int[...] = index_ref[...].T
+    for k in range(per):
+        index = swap_int[pl.ds(k, slots, stride=per), :]
+        first_ref[k] = jnp.concatenate([index] * GROUP, axis=1) - lane_block
+    for i, (source, target) in enumerate(((seen_ref, slot_seen_ref), (weight_ref, slot_weight_ref))):
+        swap_float[i] = source[...].T
+        for k in range(per):
+            target[k] = swap_float[i, pl.ds(k, slots, stride=per), :]
     terms = []
     for g in range(groups):
         table = table_ref[g * GROUP : (g + 1) * GROUP].reshape(GROUP * lags, cells)
@@ -99,39 +137,34 @@
         )
         terms.append(skew_down(products, lags, slots) * scale[g : g + 1])
     sums = two_term_dot(jnp.concatenate(terms, 0), mask, 0)
-    lane_block = lax.broadcasted_iota(jnp.int32, (slots, GROUP * stations), 1) // stations
-    for k in range(per):
-        index = index_ref[pl.ds(k, slots, stride=per), :]
-        first = jnp.concatenate([index] * GROUP, axis=1) - lane_block
+    for k in range(per):
+        first = first_ref[k]
         picked = jnp.zeros((slots, GROUP * stations), F32)
         for g in range(groups):
             picked = jnp.where(first == g * GROUP, sums[g * slots : (g + 1) * slots], picked)
         total = picked[:, :stations]
         for i in range(1, GROUP):
             total = total + picked[:, i * stations : (i + 1) * stations]
-        out_ref[pl.ds(k, slots, stride=per), :] = total
+        out_ref[k] = total
 
 
 def return_kernel(*refs):
     (mine_ref, other_ref, seen_ref, weight_ref, flux_ref, prior_ref, table_ref, scale_ref,
-     index_ref, len_ref, resid_ref, own_ref, *rest) = refs
+     mask_ref, first_ref, resid_ref, own_ref, *rest) = refs
     *sent_refs, spread_ref = rest
     blocks, lags, cells = table_ref.shape
-    slots = flux_ref.shape[0]
-    hours, stations = index_ref.shape
-    per = hours // slots
+    per, slots, stations = mine_ref.shape
     groups = blocks // GROUP
     rows = spread_ref.shape[0]
-    scale = lane_scale(scale_ref, groups)
-    mask = reach_mask(len_ref, lags, stations)
-    lane_block = lax.broadcasted_iota(jnp.int32, (slots, GROUP * stations), 1) // stations
+    shard = lax.axis_index("tm")
+    scale = scale_ref[...]
+    mask = mask_ref[...]
     firsts, resids = [], []
     for k in range(per):
-        at = (pl.ds(k, slots, stride=per), slice(None))
-        resid = weight_ref[at] * (mine_ref[at] + other_ref[at] - seen_ref[at])
-        resid_ref[at] = resid
+        resid = weight_ref[k] * (mine_ref[k] + other_ref[k] - seen_ref[k])
+        resid_ref[k] = resid
         resids.append(jnp.concatenate([resid] * GROUP, axis=1))
-        firsts.append(jnp.concatenate([index_ref[at]] * GROUP, axis=1) - lane_block)
+        firsts.append(first_ref[k])
     placed = []
     for g in range(groups):
         total = jnp.where(firsts[0] == g * GROUP, resids[0], 0.0)
@@ -148,9 +181,18 @@
     own_ref[...] = returned[rows - slots :] + 0.5 * prior_ref[...] * flux_ref[...]
     for i, ref in enumerate(sent_refs):
         start = rows - slots * (i + 2)
-        ref[...] = returned[start : start + slots].astype(ref.dtype)
-
-
+        piece = returned[start : start + slots].astype(ref.dtype)
+        ref[...] = jnp.where(shard > i, piece, jnp.zeros_like(piece))
+
+
+def order_kernel(slot_resid_ref, resid_ref, swap_float):
+    per, slots, _ = slot_resid_ref.shape
+    for k in range(per):
+        swap_float[pl.ds(k, slots, stride=per), :] = slot_resid_ref[k]
+    resid_ref[...] = swap_float[...].T
+
+
+PARAMS = pltpu.CompilerParams(vmem_limit_bytes=12 * 1024 * 1024)
 VMEM = pl.BlockSpec(memory_space=pltpu.VMEM)
 
 
@@ -162,37 +204,69 @@
     hours, stations = block_index.shape
     far = min(lags // slots, lax.axis_size("tm") - 1)
     rows = slots * (far + 1)
-    own = fluxes.astype(BF16)
-    pieces = [shifted(own, d) for d in range(far, 0, -1)] + [own]
-    lengths = foot_length.reshape(1, stations)
+    own = pl.pallas_call(
+        round_kernel,
+        out_shape=jax.ShapeDtypeStruct((slots, cells), BF16),
+        in_specs=[pl.BlockSpec(memory_space=pltpu.HBM)],
+        out_specs=VMEM,
+        scratch_shapes=[pltpu.VMEM((slots, cells), F32), pltpu.SemaphoreType.DMA],
+        compiler_params=pltpu.CompilerParams(vmem_limit_bytes=2 * 1024 * 1024),
+        cost_estimate=pl.CostEstimate(flops=2 * 10**10, bytes_accessed=10**5, transcendentals=0),
+    )(pltpu.with_memory_space_constraint(fluxes, pltpu.HBM))
+    moved = []
+    for near in range(1, far + 1, 2):
+        if near == far:
+            moved.append(rolled(own, near))
+        else:
+            got = shared(own, near)
+            moved += [got, swapped_sum(got, "stn")]
+    per = hours // slots
+    groups = blocks // GROUP
+    by_hour = jax.ShapeDtypeStruct((per, slots, stations), F32)
     flops = 2 * blocks * lags * cells * rows
     nbytes = blocks * lags * cells * 2
     cost = pl.CostEstimate(flops=flops, bytes_accessed=nbytes, transcendentals=0)
-    params = pltpu.CompilerParams(vmem_limit_bytes=24 * 1024 * 1024)
-    mine = pl.pallas_call(
-        model_kernel,
-        out_shape=jax.ShapeDtypeStruct((hours, stations), F32),
-        in_specs=[VMEM] * (len(pieces) + 4),
-        out_specs=VMEM,
-        compiler_params=params,
+    mine, scale, mask, first, seen, weight = pl.pallas_call(
+        functools.partial(model_kernel, far),
+        out_shape=[
+            by_hour,
+            jax.ShapeDtypeStruct((groups, GROUP * lags), F32),
+            jax.ShapeDtypeStruct((GROUP * lags, GROUP * stations), BF16),
+            jax.ShapeDtypeStruct((per, slots, GROUP * stations), jnp.int32),
+            by_hour,
+            by_hour,
+        ],
+        in_specs=[VMEM] * (far + 7),
+        out_specs=[VMEM] * 6,
+        scratch_shapes=[pltpu.VMEM((hours, stations), jnp.int32), pltpu.VMEM((2, hours, stations), F32)],
+        compiler_params=PARAMS,
         cost_estimate=cost,
-    )(*pieces, footprint, block_scale, block_index, lengths)
+    )(*moved, own, footprint, block_scale, block_index.T, foot_length.reshape(1, stations), observed.T, obs_weight.T)
     other = swapped_sum(mine, "space")
     piece = jax.ShapeDtypeStruct((slots, cells), F32)
     sent = jax.ShapeDtypeStruct((slots, cells), BF16)
     resid, total, *back = pl.pallas_call(
         return_kernel,
-        out_shape=[jax.ShapeDtypeStruct((hours, stations), F32), piece] + [sent] * far,
+        out_shape=[by_hour, piece] + [sent] * far,
         in_specs=[VMEM] * 10,
         out_specs=[VMEM] * (2 + far),
         scratch_shapes=[pltpu.VMEM((rows, blocks * lags), BF16)],
-        compiler_params=params,
+        compiler_params=PARAMS,
         cost_estimate=cost,
-    )(mine, other, observed, obs_weight, fluxes, prior_weight, footprint, block_scale, block_index, lengths)
+    )(mine, other, seen, weight, fluxes, prior_weight, footprint, scale, mask, first)
     for d in range(far, 0, -1):
-        total = total + shifted(back[d - 1], -d).astype(F32)
+        total = total + rolled(back[d - 1], -d).astype(F32)
+    resid = pl.pallas_call(
+        order_kernel,
+        out_shape=jax.ShapeDtypeStruct((stations, hours), F32),
+        in_specs=[VMEM],
+        out_specs=VMEM,
+        scratch_shapes=[pltpu.VMEM((hours, stations), F32)],
+        compiler_params=pltpu.CompilerParams(vmem_limit_bytes=2 * 1024 * 1024),
+        cost_estimate=pl.CostEstimate(flops=10**6, bytes_accessed=10**4, transcendentals=0),
+    )(resid)
     gradient = total + swapped_sum(total, "stn")
-    return (resid, gradient)
+    return (resid.T, gradient)
 
 
 def swapped_sum(x, axis):

time: 37.2 us -> 26.8 us (0.72)
  local copies, waits for them, and re-layouts: 7.36 us -> 0.04 us
  starting transfers between devices: 16.2 us -> 12.5 us
  Pallas kernels: 2.78 us -> 4.46 us
  other arithmetic: 1.54 us -> 0.66 us
    unnamed x24 -> x16, local copies, waits for them, and re-layouts: 7.36 us -> 0.04 us
    ppermute x6 -> x5, starting transfers between devices: 14.6 us -> 10.9 us  [the longest x4 6.77 us: rolled(): lax.ppermute(x, 'tm', [(t, (t + by) % devices) for t in range(devices)])]
    pallas_call x2 -> x4, Pallas kernels: 2.78 us -> 4.46 us  [the longest x1 1.66 us: on_device(): pl.pallas_call(functools.partial(model_kernel, far), out_shape=[by_hour,...]
    convert_element_type x1 -> x0, other arithmetic: 0.88 us -> none  [on_device(): own = fluxes.astype(BF16)]
    ppermute x2 -> x3, waiting for transfers between devices: 2.75 us -> 2.91 us  [swapped_sum(): lax.ppermute(x, axis, [(i, (i + by) % devices) for i in range(devices)])]
    ppermute x6 -> x5, waiting for transfers between devices: 5.34 us -> 5.31 us  [the longest x4 4.32 us: rolled(): lax.ppermute(x, 'tm', [(t, (t + by) % devices) for t in range(devices)])]
    ppermute x2 -> x3, starting transfers between devices: 1.63 us -> 1.63 us  [swapped_sum(): lax.ppermute(x, axis, [(i, (i + by) % devices) for i in range(devices)])]
  transfers between devices with their start and end apart: 8 -> 8, of which waited for: 6 -> 7; matrix products, arithmetic and copies ran while one was open for 4% -> 0% of each run, Pallas kernels for 0% -> 3%
where the time goes in v3:
time: 26.8 us; the launch traced here: 26.6 us
  starting transfers between devices  12.5 us (47%)
  waiting for transfers between devices  8.22 us (31%)
  Pallas kernels  4.46 us (17%)
  between operations  0.77 us (3%)
  other arithmetic  0.66 us (2%)
    ppermute x4, starting transfers between devices, rolled(): lax.ppermute(x, 'tm', [(t, (t + by) % devices) for t in range(devices)])  6.77 us
    ppermute x4, waiting for transfers between devices, rolled(): lax.ppermute(x, 'tm', [(t, (t + by) % devices) for t in range(devices)])  4.32 us
    ppermute x1, starting transfers between devices, shared(): return lax.ppermute(x, ('tm', 'stn'), pairs)  4.09 us
    ppermute x3, waiting for transfers between devices, swapped_sum(): lax.ppermute(x, axis, [(i, (i + by) % devices) for i in range(devices)])  2.91 us
    pallas_call x1, Pallas kernels, on_device(): pl.pallas_call(functools.partial(model_kernel, far), out_shape=[by_hour,...  1.66 us
    ppermute x3, starting transfers between devices, swapped_sum(): lax.ppermute(x, axis, [(i, (i + by) % devices) for i in range(devices)])  1.63 us
    pallas_call x1, Pallas kernels, on_device(): pl.pallas_call(return_kernel, out_shape=[by_hour, piece] + [sent] * far,...  1.13 us
    pallas_call x1, Pallas kernels, on_device(): pl.pallas_call(round_kernel, out_shape=jax.ShapeDtypeStruct((slots, cells...  1 us
  transfers between devices with their start and end apart: 8, of which 7 were waited for; matrix products, arithmetic and copies ran while one was open for 0% of the time, Pallas kernels for 3%

profile of v3, /device:TPU:0, one launch (start us, length us, event | category | flops | bytes accessed | tf_op | source)
XLA Modules:
  0.0 26.6 jit_solution(450937641754660204)
XLA Ops:
  0.6 0.0 copy-start
  0.7 1.0 %shard_map.95.refs_3_ = bf16[16,1024]{1,0:T(8,128)(2,1)S(1)} custom-call(f32[16,1024]{1,0:T(8,128)} %refs_4_.3), custom_call_target="tpu_custom_call" | custom-call | flops 20000000000 | bytes 100000 | tf_op jit(solution)/shard_map/pallas_call | solution.py:207
  1.7 0.0 copy-start.1
  1.7 0.0 copy-start.2
  1.7 4.1 %collective-permute-start = (bf16[16,1024]{1,0:T(8,128)(2,1)S(1)}, bf16[16,1024]{1,0:T(8,128)(2,1)S(1)}, u32[]{:S(2)}, u32[]{:S(2)}) collective-permute-start(bf16[16,1024]{1,0:T(8,128)(2,1)S(1)} %shard_map.95.refs_3_), channel_id=1, source_target_pairs={{0,8},{1,5},{4,12},{5,9},{8,0},{9,13},{12,4},{13,1},{2,10},{3,7},{... | collective-permute-start | bytes 98312 | tf_op jit(solution)/shard_map/ppermute | solution.py:27
  5.8 1.3 %collective-permute-start.2 = (bf16[16,1024]{1,0:T(8,128)(2,1)S(1)}, bf16[16,1024]{1,0:T(8,128)(2,1)S(1)}, u32[]{:S(2)}, u32[]{:S(2)}) collective-permute-start(bf16[16,1024]{1,0:T(8,128)(2,1)S(1)} %shard_map.95.refs_3_), channel_id=1, source_target_pairs={{0,12},{4,0},{8,4},{12,8},{1,13},{5,1},{9,5},{13,9},{2,14},{6,2},{... | collective-permute-start | bytes 98312 | tf_op jit(solution)/shard_map/ppermute | solution.py:17
  7.2 1.0 %collective-permute-done.refs_0_ = bf16[16,1024]{1,0:T(8,128)(2,1)S(1)} collective-permute-done((bf16[16,1024]{1,0:T(8,128)(2,1)S(1)}, bf16[16,1024]{1,0:T(8,128)(2,1)S(1)}, u32[]{:S(2)}, u32[]{:S(2)}) %collective-permute-start) | collective-permute-done | bytes 32800 | tf_op jit(solution)/shard_map/ppermute | solution.py:27
  8.2 0.0 collective-permute-start.1
  8.2 1.6 %collective-permute-done.2.refs_2_ = bf16[16,1024]{1,0:T(8,128)(2,1)S(1)} collective-permute-done((bf16[16,1024]{1,0:T(8,128)(2,1)S(1)}, bf16[16,1024]{1,0:T(8,128)(2,1)S(1)}, u32[]{:S(2)}, u32[]{:S(2)}) %collective-permute-start.2) | collective-permute-done | bytes 32800 | tf_op jit(solution)/shard_map/ppermute | solution.py:17
  9.7 0.0 collective-permute-done.1.refs_1_
  9.8 1.7 %shard_map.96 = (f32[3,16,8]{2,1,0:T(8,128)S(1)}, f32[8,256]{1,0:T(8,128)S(1)}, bf16[256,32]{1,0:T(8,128)(2,1)S(1)}, s32[3,16,32]{2,1,0:T(8,128)S(1)}, f32[3,16,8]{2,1,0:T(8,128)S(1)}, /*index=5*/f32[3,16,8]{2,1,0:T(8,128)S(1)}) custom-call(bf16[16,1024]{1,0:T(8,128)(2,1)S(1)} %collective-permute-done.refs_0_, ...), custom_call_target="tpu_custom_call" | custom-call | flops 268435456 | bytes 4194304 | tf_op jit(solution)/shard_map/pallas_call | solution.py:229
  11.4 1.6 %collective-permute-start.3 = (f32[3,16,8]{2,1,0:T(8,128)S(1)}, f32[3,16,8]{2,1,0:T(8,128)S(1)}, u32[]{:S(2)}, u32[]{:S(2)}) collective-permute-start(f32[3,16,8]{2,1,0:T(8,128)S(1)} %get-tuple-element.13.refs_0_), channel_id=1, source_target_pairs={{0,2},{2,0},{1,3},{3,1},{4,6},{6,4},{5,7},{7,5},{8,10},{10,8},{9,1... | collective-permute-start | bytes 4616 | tf_op jit(solution)/shard_map/ppermute | solution.py:276
  13.0 2.3 %collective-permute-done.3.refs_1_ = f32[3,16,8]{2,1,0:T(8,128)S(1)} collective-permute-done((f32[3,16,8]{2,1,0:T(8,128)S(1)}, f32[3,16,8]{2,1,0:T(8,128)S(1)}, u32[]{:S(2)}, u32[]{:S(2)}) %collective-permute-start.3) | collective-permute-done | bytes 1568 | tf_op jit(solution)/shard_map/ppermute | solution.py:276
  15.3 1.1 %shard_map.97 = (f32[3,16,8]{2,1,0:T(8,128)S(1)}, f32[16,1024]{1,0:T(8,128)S(1)}, bf16[16,1024]{1,0:T(8,128)(2,1)S(1)}, bf16[16,1024]{1,0:T(8,128)(2,1)S(1)}, bf16[16,1024]{1,0:T(8,128)(2,1)S(1)}) custom-call(f32[3,16,8]{2,1,0:T(8,128)S(1)} %get-tuple-element.13.refs_0_, f32[3,16,8]{2,1,0:T(8,128)S(1)} %collective-permute-done.3.refs_1_, ...), custom_call_target="tpu_custom_call" | custom-call | flops 268435456 | bytes 4194304 | tf_op jit(solution)/shard_map/pallas_call | solution.py:248
  16.5 1.6 %collective-permute-start.4 = (bf16[16,1024]{1,0:T(8,128)(2,1)S(1)}, bf16[16,1024]{1,0:T(8,128)(2,1)S(1)}, u32[]{:S(2)}, u32[]{:S(2)}) collective-permute-start(bf16[16,1024]{1,0:T(8,128)(2,1)S(1)} %get-tuple-element.21), channel_id=1, source_target_pairs={{0,4},{4,8},{8,12},{12,0},{1,5},{5,9},{9,13},{13,1},{2,6},{6,10},{... | collective-permute-start | bytes 98312 | tf_op jit(solution)/shard_map/ppermute | solution.py:17
  18.1 2.6 %collective-permute-start.5 = (bf16[16,1024]{1,0:T(8,128)(2,1)S(1)}, bf16[16,1024]{1,0:T(8,128)(2,1)S(1)}, u32[]{:S(2)}, u32[]{:S(2)}) collective-permute-start(bf16[16,1024]{1,0:T(8,128)(2,1)S(1)} %get-tuple-element.22), channel_id=1, source_target_pairs={{0,8},{4,12},{8,0},{12,4},{1,9},{5,13},{9,1},{13,5},{2,10},{6,14},... | collective-permute-start | bytes 98312 | tf_op jit(solution)/shard_map/ppermute | solution.py:17
  20.7 1.2 %collective-permute-start.6 = (bf16[16,1024]{1,0:T(8,128)(2,1)S(1)}, bf16[16,1024]{1,0:T(8,128)(2,1)S(1)}, u32[]{:S(2)}, u32[]{:S(2)}) collective-permute-start(bf16[16,1024]{1,0:T(8,128)(2,1)S(1)} %get-tuple-element.23), channel_id=1, source_target_pairs={{0,12},{4,0},{8,4},{12,8},{1,13},{5,1},{9,5},{13,9},{2,14},{6,2},{... | collective-permute-start | bytes 98312 | tf_op jit(solution)/shard_map/ppermute | solution.py:17
  21.9 0.5 %collective-permute-done.4 = bf16[16,1024]{1,0:T(8,128)(2,1)S(1)} collective-permute-done((bf16[16,1024]{1,0:T(8,128)(2,1)S(1)}, bf16[16,1024]{1,0:T(8,128)(2,1)S(1)}, u32[]{:S(2)}, u32[]{:S(2)}) %collective-permute-start.4) | collective-permute-done | bytes 32800 | tf_op jit(solution)/shard_map/ppermute | solution.py:17
  22.4 0.6 %collective-permute-done.5 = bf16[16,1024]{1,0:T(8,128)(2,1)S(1)} collective-permute-done((bf16[16,1024]{1,0:T(8,128)(2,1)S(1)}, bf16[16,1024]{1,0:T(8,128)(2,1)S(1)}, u32[]{:S(2)}, u32[]{:S(2)}) %collective-permute-start.5) | collective-permute-done | bytes 32800 | tf_op jit(solution)/shard_map/ppermute | solution.py:17
  22.9 1.7 %collective-permute-done.6 = bf16[16,1024]{1,0:T(8,128)(2,1)S(1)} collective-permute-done((bf16[16,1024]{1,0:T(8,128)(2,1)S(1)}, bf16[16,1024]{1,0:T(8,128)(2,1)S(1)}, u32[]{:S(2)}, u32[]{:S(2)}) %collective-permute-start.6) | collective-permute-done | bytes 32800 | tf_op jit(solution)/shard_map/ppermute | solution.py:17
  24.7 0.1 collective-permute-start.7
  24.7 0.7 %shard_map.98 = f32[8,48]{1,0:T(8,128)} custom-call(f32[3,16,8]{2,1,0:T(8,128)S(1)} %get-tuple-element.19.slot_resid_ref), custom_call_target="tpu_custom_call" | custom-call | flops 1000000 | bytes 10000 | tf_op jit(solution)/shard_map/pallas_call | solution.py:259
  25.4 0.6 %collective-permute-done.7 = f32[16,1024]{1,0:T(8,128)S(1)} collective-permute-done((f32[16,1024]{1,0:T(8,128)S(1)}, f32[16,1024]{1,0:T(8,128)S(1)}, u32[]{:S(2)}, u32[]{:S(2)}) %collective-permute-start.7) | collective-permute-done | bytes 65568 | tf_op jit(solution)/shard_map/ppermute | solution.py:276
  26.0 0.6 %add.15 = f32[16,1024]{1,0:T(8,128)} add(f32[16,1024]{1,0:T(8,128)S(1)} %convert_add_fusion, f32[16,1024]{1,0:T(8,128)S(1)} %collective-permute-done.7) | non-fusion elementwise | flops 16384 | bytes 196608 | tf_op jit(solution)/shard_map/add | solution.py:268
  (14 shorter events, 0.0 us)
Async XLA Ops:
  0.6 9.1 %copy-start = (bf16[32,64,1024]{2,1,0:T(8,128)(2,1)S(1)}, bf16[32,64,1024]{2,1,0:T(8,128)(2,1)}, u32[]{:S(2)}) copy-start(bf16[32,64,1024]{2,1,0:T(8,128)(2,1)} %refs_6_.1) | copy-start | bytes 12582916
  0.6 9.1 %copy-start.6 = (f32[48,8]{0,1:T(8,128)S(1)}, f32[48,8]{0,1:T(8,128)}, u32[]{:S(2)}) copy-start(f32[48,8]{0,1:T(8,128)} %param.15) | copy-start | bytes 4612
  0.7 9.1 %copy-start.5 = (f32[48,8]{0,1:T(8,128)S(1)}, f32[48,8]{0,1:T(8,128)}, u32[]{:S(2)}) copy-start(f32[48,8]{0,1:T(8,128)} %param.14) | copy-start | bytes 4612
  0.7 9.1 %copy-start.7 = (s32[8]{0:T(128)S(1)}, s32[8]{0:T(128)}, u32[]{:S(2)}) copy-start(s32[8]{0:T(128)} %param.13) | copy-start | bytes 100
  0.7 9.1 %copy-start.4 = (s32[48,8]{0,1:T(8,128)S(1)}, s32[48,8]{0,1:T(8,128)}, u32[]{:S(2)}) copy-start(s32[48,8]{0,1:T(8,128)} %param.12) | copy-start | bytes 4612
  0.7 9.1 %copy-start.3 = (f32[32,64]{1,0:T(8,128)S(1)}, f32[32,64]{1,0:T(8,128)}, u32[]{:S(2)}) copy-start(f32[32,64]{1,0:T(8,128)} %refs_5_.2) | copy-start | bytes 24580
  1.7 13.6 %copy-start.1 = (f32[16,1024]{1,0:T(8,128)S(1)}, f32[16,1024]{1,0:T(8,128)}, u32[]{:S(2)}) copy-start(f32[16,1024]{1,0:T(8,128)} %refs_4_.3) | copy-start | bytes 196612
  1.7 13.6 %copy-start.2 = (f32[16,1024]{1,0:T(8,128)S(1)}, f32[16,1024]{1,0:T(8,128)}, u32[]{:S(2)}) copy-start(f32[16,1024]{1,0:T(8,128)} %refs_5_.3) | copy-start | bytes 196612
  1.7 6.4 %collective-permute-start = (bf16[16,1024]{1,0:T(8,128)(2,1)S(1)}, bf16[16,1024]{1,0:T(8,128)(2,1)S(1)}, u32[]{:S(2)}, u32[]{:S(2)}) collective-permute-start(bf16[16,1024]{1,0:T(8,128)(2,1)S(1)} %shard_map.95.refs_3_), channel_id=1, source_target_pairs={{0,8},{1,5},{4,12},{5,9},{8,0},{9,13},{12,4},{13,1},{2,10},{3,7},{... | collective-permute-start | bytes 98312 | tf_op jit(solution)/shard_map/ppermute | solution.py:27
  5.8 3.9 %collective-permute-start.2 = (bf16[16,1024]{1,0:T(8,128)(2,1)S(1)}, bf16[16,1024]{1,0:T(8,128)(2,1)S(1)}, u32[]{:S(2)}, u32[]{:S(2)}) collective-permute-start(bf16[16,1024]{1,0:T(8,128)(2,1)S(1)} %shard_map.95.refs_3_), channel_id=1, source_target_pairs={{0,12},{4,0},{8,4},{12,8},{1,13},{5,1},{9,5},{13,9},{2,14},{6,2},{... | collective-permute-start | bytes 98312 | tf_op jit(solution)/shard_map/ppermute | solution.py:17
  8.2 1.6 %collective-permute-start.1 = (bf16[16,1024]{1,0:T(8,128)(2,1)S(1)}, bf16[16,1024]{1,0:T(8,128)(2,1)S(1)}, u32[]{:S(2)}, u32[]{:S(2)}) collective-permute-start(bf16[16,1024]{1,0:T(8,128)(2,1)S(1)} %collective-permute-done.refs_0_), channel_id=1, source_target_pairs={{0,1},{1,0},{2,3},{3,2},{4,5},{5,4},{6,7},{7,6},{8,9},{9,8},{10,11... | collective-permute-start | bytes 98312 | tf_op jit(solution)/shard_map/ppermute | solution.py:276
  11.4 3.9 %collective-permute-start.3 = (f32[3,16,8]{2,1,0:T(8,128)S(1)}, f32[3,16,8]{2,1,0:T(8,128)S(1)}, u32[]{:S(2)}, u32[]{:S(2)}) collective-permute-start(f32[3,16,8]{2,1,0:T(8,128)S(1)} %get-tuple-element.13.refs_0_), channel_id=1, source_target_pairs={{0,2},{2,0},{1,3},{3,1},{4,6},{6,4},{5,7},{7,5},{8,10},{10,8},{9,1... | collective-permute-start | bytes 4616 | tf_op jit(solution)/shard_map/ppermute | solution.py:276
  16.5 5.9 %collective-permute-start.4 = (bf16[16,1024]{1,0:T(8,128)(2,1)S(1)}, bf16[16,1024]{1,0:T(8,128)(2,1)S(1)}, u32[]{:S(2)}, u32[]{:S(2)}) collective-permute-start(bf16[16,1024]{1,0:T(8,128)(2,1)S(1)} %get-tuple-element.21), channel_id=1, source_target_pairs={{0,4},{4,8},{8,12},{12,0},{1,5},{5,9},{9,13},{13,1},{2,6},{6,10},{... | collective-permute-start | bytes 98312 | tf_op jit(solution)/shard_map/ppermute | solution.py:17
  18.1 4.8 %collective-permute-start.5 = (bf16[16,1024]{1,0:T(8,128)(2,1)S(1)}, bf16[16,1024]{1,0:T(8,128)(2,1)S(1)}, u32[]{:S(2)}, u32[]{:S(2)}) collective-permute-start(bf16[16,1024]{1,0:T(8,128)(2,1)S(1)} %get-tuple-element.22), channel_id=1, source_target_pairs={{0,8},{4,12},{8,0},{12,4},{1,9},{5,13},{9,1},{13,5},{2,10},{6,14},... | collective-permute-start | bytes 98312 | tf_op jit(solution)/shard_map/ppermute | solution.py:17
  20.7 3.9 %collective-permute-start.6 = (bf16[16,1024]{1,0:T(8,128)(2,1)S(1)}, bf16[16,1024]{1,0:T(8,128)(2,1)S(1)}, u32[]{:S(2)}, u32[]{:S(2)}) collective-permute-start(bf16[16,1024]{1,0:T(8,128)(2,1)S(1)} %get-tuple-element.23), channel_id=1, source_target_pairs={{0,12},{4,0},{8,4},{12,8},{1,13},{5,1},{9,5},{13,9},{2,14},{6,2},{... | collective-permute-start | bytes 98312 | tf_op jit(solution)/shard_map/ppermute | solution.py:17
  24.7 1.3 %collective-permute-start.7 = (f32[16,1024]{1,0:T(8,128)S(1)}, f32[16,1024]{1,0:T(8,128)S(1)}, u32[]{:S(2)}, u32[]{:S(2)}) collective-permute-start(f32[16,1024]{1,0:T(8,128)S(1)} %convert_add_fusion), channel_id=1, source_target_pairs={{0,1},{1,0},{2,3},{3,2},{4,5},{5,4},{6,7},{7,6},{8,9},{9,8},{10,11... | collective-permute-start | bytes 196616 | tf_op jit(solution)/shard_map/ppermute | solution.py:276

commit v4 on v3

--- a/solution.py
+++ b/solution.py
@@ -17,10 +17,10 @@
     return lax.ppermute(x, "tm", [(t, (t + by) % devices) for t in range(devices)])
 
 
-def shared(x, near):
+def shared(x, near, sign=1):
     devices = lax.axis_size("tm")
     pairs = [
-        (t * 2 + core, (t + near + 1 - core) % devices * 2 + core)
+        (t * 2 + core, (t + sign * (near + 1 - core)) % devices * 2 + core)
         for t in range(devices)
         for core in (0, 1)
     ]
@@ -133,8 +133,8 @@
     for g in range(groups):
         table = table_ref[g * GROUP : (g + 1) * GROUP].reshape(GROUP * lags, cells)
         products = lax.dot_general(
-            window, table, (((1,), (1,)), ((), ())), preferred_element_type=F32
-        )
+            table, window, (((1,), (1,)), ((), ())), preferred_element_type=F32
+        ).T
         terms.append(skew_down(products, lags, slots) * scale[g : g + 1])
     sums = two_term_dot(jnp.concatenate(terms, 0), mask, 0)
     for k in range(per):
@@ -179,10 +179,18 @@
     table = table_ref[...].reshape(blocks * lags, cells)
     returned = jnp.dot(spread_ref[...], table, preferred_element_type=F32)
     own_ref[...] = returned[rows - slots :] + 0.5 * prior_ref[...] * flux_ref[...]
-    for i, ref in enumerate(sent_refs):
-        start = rows - slots * (i + 2)
-        piece = returned[start : start + slots].astype(ref.dtype)
-        ref[...] = jnp.where(shard > i, piece, jnp.zeros_like(piece))
+    core = lax.axis_index("stn")
+    near = []
+    for distance in range(1, rows // slots):
+        start = rows - slots * (distance + 1)
+        piece = returned[start : start + slots]
+        near.append(jnp.where(shard >= distance, piece, jnp.zeros_like(piece)))
+    for first in range(0, len(near), 2):
+        if first + 1 < len(near):
+            sent_refs[first][...] = jnp.where(core == 0, near[first + 1], near[first])
+            sent_refs[first + 1][...] = jnp.where(core == 1, near[first + 1], near[first])
+        else:
+            sent_refs[first][...] = near[first].astype(sent_refs[first].dtype)
 
 
 def order_kernel(slot_resid_ref, resid_ref, swap_float):
@@ -247,15 +255,22 @@
     sent = jax.ShapeDtypeStruct((slots, cells), BF16)
     resid, total, *back = pl.pallas_call(
         return_kernel,
-        out_shape=[by_hour, piece] + [sent] * far,
+        out_shape=[by_hour, piece] + [piece] * (far // 2 * 2) + [sent] * (far % 2),
         in_specs=[VMEM] * 10,
         out_specs=[VMEM] * (2 + far),
         scratch_shapes=[pltpu.VMEM((rows, blocks * lags), BF16)],
         compiler_params=PARAMS,
         cost_estimate=cost,
     )(mine, other, seen, weight, fluxes, prior_weight, footprint, scale, mask, first)
-    for d in range(far, 0, -1):
-        total = total + rolled(back[d - 1], -d).astype(F32)
+    arrived = []
+    for near in range(1, far + 1, 2):
+        if near == far:
+            arrived.append(rolled(back[near - 1], -near))
+        else:
+            both = back[near - 1] + swapped_sum(back[near], "stn")
+            arrived.append(shared(both.astype(BF16), near, -1))
+    for piece in arrived[::-1]:
+        total = total + piece
     resid = pl.pallas_call(
         order_kernel,
         out_shape=jax.ShapeDtypeStruct((stations, hours), F32),

time: 26.8 us -> 25.1 us (0.937)
  starting transfers between devices: 12.5 us -> 11.5 us
  waiting for transfers between devices: 8.22 us -> 7.63 us
    ppermute x4 -> x2, starting transfers between devices: 6.77 us -> 2.97 us  [rolled(): lax.ppermute(x, 'tm', [(t, (t + by) % devices) for t in range(devices)])]
    ppermute x1 -> x2, starting transfers between devices: 4.09 us -> 6.78 us  [shared(): return lax.ppermute(x, ('tm', 'stn'), pairs)]
    ppermute x4 -> x2, waiting for transfers between devices: 4.32 us -> 3.12 us  [rolled(): lax.ppermute(x, 'tm', [(t, (t + by) % devices) for t in range(devices)])]
    ppermute x1 -> x2, waiting for transfers between devices: 0.99 us -> 1.62 us  [shared(): return lax.ppermute(x, ('tm', 'stn'), pairs)]
    ppermute x3 -> x4, starting transfers between devices: 1.63 us -> 1.71 us  [swapped_sum(): lax.ppermute(x, axis, [(i, (i + by) % devices) for i in range(devices)])]
    ppermute x3 -> x4, waiting for transfers between devices: 2.91 us -> 2.9 us  [swapped_sum(): lax.ppermute(x, axis, [(i, (i + by) % devices) for i in range(devices)])]
  transfers between devices with their start and end apart: 8 -> 8, of which waited for: 7 -> 6; matrix products, arithmetic and copies ran while one was open for 0% -> 0% of each run, Pallas kernels for 3% -> 3%
where the time goes in v4:
time: 25.1 us; the launch traced here: 24.9 us
  starting transfers between devices  11.5 us (46%)
  waiting for transfers between devices  7.63 us (30%)
  Pallas kernels  4.36 us (17%)
  between operations  0.78 us (3%)
  other arithmetic  0.66 us (3%)
    ppermute x2, starting transfers between devices, shared(): return lax.ppermute(x, ('tm', 'stn'), pairs)  6.78 us
    ppermute x2, waiting for transfers between devices, rolled(): lax.ppermute(x, 'tm', [(t, (t + by) % devices) for t in range(devices)])  3.12 us
    ppermute x2, starting transfers between devices, rolled(): lax.ppermute(x, 'tm', [(t, (t + by) % devices) for t in range(devices)])  2.97 us
    ppermute x4, waiting for transfers between devices, swapped_sum(): lax.ppermute(x, axis, [(i, (i + by) % devices) for i in range(devices)])  2.9 us
    ppermute x4, starting transfers between devices, swapped_sum(): lax.ppermute(x, axis, [(i, (i + by) % devices) for i in range(devices)])  1.71 us
    ppermute x2, waiting for transfers between devices, shared(): return lax.ppermute(x, ('tm', 'stn'), pairs)  1.62 us
    pallas_call x1, Pallas kernels, on_device(): pl.pallas_call(functools.partial(model_kernel, far), out_shape=[by_hour,...  1.55 us
    pallas_call x1, Pallas kernels, on_device(): pl.pallas_call(return_kernel, out_shape=[by_hour, piece] + [piece] * (far...  1.13 us
  transfers between devices with their start and end apart: 8, of which 6 were waited for; matrix products, arithmetic and copies ran while one was open for 0% of the time, Pallas kernels for 3%

profile of v4, /device:TPU:0, one launch (start us, length us, event | category | flops | bytes accessed | tf_op | source)
XLA Modules:
  0.0 24.9 jit_solution(5868387956977700923)
XLA Ops:
  0.6 0.0 copy-start
  0.7 1.0 %shard_map.95.refs_3_ = bf16[16,1024]{1,0:T(8,128)(2,1)S(1)} custom-call(f32[16,1024]{1,0:T(8,128)} %refs_4_.3), custom_call_target="tpu_custom_call" | custom-call | flops 20000000000 | bytes 100000 | tf_op jit(solution)/shard_map/pallas_call | solution.py:215
  1.7 0.0 copy-start.1
  1.7 0.0 copy-start.2
  1.7 4.1 %collective-permute-start = (bf16[16,1024]{1,0:T(8,128)(2,1)S(1)}, bf16[16,1024]{1,0:T(8,128)(2,1)S(1)}, u32[]{:S(2)}, u32[]{:S(2)}) collective-permute-start(bf16[16,1024]{1,0:T(8,128)(2,1)S(1)} %shard_map.95.refs_3_), channel_id=1, source_target_pairs={{0,8},{1,5},{4,12},{5,9},{8,0},{9,13},{12,4},{13,1},{2,10},{3,7},{... | collective-permute-start | bytes 98312 | tf_op jit(solution)/shard_map/ppermute | solution.py:27
  5.8 1.3 %collective-permute-start.2 = (bf16[16,1024]{1,0:T(8,128)(2,1)S(1)}, bf16[16,1024]{1,0:T(8,128)(2,1)S(1)}, u32[]{:S(2)}, u32[]{:S(2)}) collective-permute-start(bf16[16,1024]{1,0:T(8,128)(2,1)S(1)} %shard_map.95.refs_3_), channel_id=1, source_target_pairs={{0,12},{4,0},{8,4},{12,8},{1,13},{5,1},{9,5},{13,9},{2,14},{6,2},{... | collective-permute-start | bytes 98312 | tf_op jit(solution)/shard_map/ppermute | solution.py:17
  7.2 1.0 %collective-permute-done.refs_0_ = bf16[16,1024]{1,0:T(8,128)(2,1)S(1)} collective-permute-done((bf16[16,1024]{1,0:T(8,128)(2,1)S(1)}, bf16[16,1024]{1,0:T(8,128)(2,1)S(1)}, u32[]{:S(2)}, u32[]{:S(2)}) %collective-permute-start) | collective-permute-done | bytes 32800 | tf_op jit(solution)/shard_map/ppermute | solution.py:27
  8.2 0.0 collective-permute-start.1
  8.2 1.6 %collective-permute-done.2.refs_2_ = bf16[16,1024]{1,0:T(8,128)(2,1)S(1)} collective-permute-done((bf16[16,1024]{1,0:T(8,128)(2,1)S(1)}, bf16[16,1024]{1,0:T(8,128)(2,1)S(1)}, u32[]{:S(2)}, u32[]{:S(2)}) %collective-permute-start.2) | collective-permute-done | bytes 32800 | tf_op jit(solution)/shard_map/ppermute | solution.py:17
  9.7 0.0 collective-permute-done.1.refs_1_
  9.8 1.6 %shard_map.96 = (f32[3,16,8]{2,1,0:T(8,128)S(1)}, f32[8,256]{1,0:T(8,128)S(1)}, bf16[256,32]{1,0:T(8,128)(2,1)S(1)}, s32[3,16,32]{2,1,0:T(8,128)S(1)}, f32[3,16,8]{2,1,0:T(8,128)S(1)}, /*index=5*/f32[3,16,8]{2,1,0:T(8,128)S(1)}) custom-call(bf16[16,1024]{1,0:T(8,128)(2,1)S(1)} %collective-permute-done.refs_0_, ...), custom_call_target="tpu_custom_call" | custom-call | flops 268435456 | bytes 4194304 | tf_op jit(solution)/shard_map/pallas_call | solution.py:237
  11.3 1.6 %collective-permute-start.3 = (f32[3,16,8]{2,1,0:T(8,128)S(1)}, f32[3,16,8]{2,1,0:T(8,128)S(1)}, u32[]{:S(2)}, u32[]{:S(2)}) collective-permute-start(f32[3,16,8]{2,1,0:T(8,128)S(1)} %get-tuple-element.13.refs_0_), channel_id=1, source_target_pairs={{0,2},{2,0},{1,3},{3,1},{4,6},{6,4},{5,7},{7,5},{8,10},{10,8},{9,1... | collective-permute-start | bytes 4616 | tf_op jit(solution)/shard_map/ppermute | solution.py:291
  12.9 2.3 %collective-permute-done.3.refs_1_ = f32[3,16,8]{2,1,0:T(8,128)S(1)} collective-permute-done((f32[3,16,8]{2,1,0:T(8,128)S(1)}, f32[3,16,8]{2,1,0:T(8,128)S(1)}, u32[]{:S(2)}, u32[]{:S(2)}) %collective-permute-start.3) | collective-permute-done | bytes 1568 | tf_op jit(solution)/shard_map/ppermute | solution.py:291
  15.2 1.1 %shard_map.97 = (f32[3,16,8]{2,1,0:T(8,128)S(1)}, f32[16,1024]{1,0:T(8,128)S(1)}, f32[16,1024]{1,0:T(8,128)S(1)}, f32[16,1024]{1,0:T(8,128)S(1)}, bf16[16,1024]{1,0:T(8,128)(2,1)S(1)}) custom-call(f32[3,16,8]{2,1,0:T(8,128)S(1)} %get-tuple-element.13.refs_0_, f32[3,16,8]{2,1,0:T(8,128)S(1)} %collective-permute-done.3.refs_1_, ...), custom_call_target="tpu_custom_call" | custom-call | flops 268435456 | bytes 4194304 | tf_op jit(solution)/shard_map/pallas_call | solution.py:256
  16.4 0.1 collective-permute-start.5
  16.4 1.6 %collective-permute-start.4 = (bf16[16,1024]{1,0:T(8,128)(2,1)S(1)}, bf16[16,1024]{1,0:T(8,128)(2,1)S(1)}, u32[]{:S(2)}, u32[]{:S(2)}) collective-permute-start(bf16[16,1024]{1,0:T(8,128)(2,1)S(1)} %get-tuple-element.21), channel_id=1, source_target_pairs={{0,4},{4,8},{8,12},{12,0},{1,5},{5,9},{9,13},{13,1},{2,6},{6,10},{... | collective-permute-start | bytes 98312 | tf_op jit(solution)/shard_map/ppermute | solution.py:17
  18.1 0.0 collective-permute-done.5
  18.1 2.7 %collective-permute-start.6 = (bf16[16,1024]{1,0:T(8,128)(2,1)S(1)}, bf16[16,1024]{1,0:T(8,128)(2,1)S(1)}, u32[]{:S(2)}, u32[]{:S(2)}) collective-permute-start(bf16[16,1024]{1,0:T(8,128)(2,1)S(1)} %add_convert_fusion), channel_id=1, source_target_pairs={{0,8},{1,13},{4,12},{5,1},{8,0},{9,5},{12,4},{13,9},{2,10},{3,15},... | collective-permute-start | bytes 98312 | tf_op jit(solution)/shard_map/ppermute | solution.py:27
  20.8 1.5 %collective-permute-done.4 = bf16[16,1024]{1,0:T(8,128)(2,1)S(1)} collective-permute-done((bf16[16,1024]{1,0:T(8,128)(2,1)S(1)}, bf16[16,1024]{1,0:T(8,128)(2,1)S(1)}, u32[]{:S(2)}, u32[]{:S(2)}) %collective-permute-start.4) | collective-permute-done | bytes 32800 | tf_op jit(solution)/shard_map/ppermute | solution.py:17
  22.3 0.6 %collective-permute-done.6 = bf16[16,1024]{1,0:T(8,128)(2,1)S(1)} collective-permute-done((bf16[16,1024]{1,0:T(8,128)(2,1)S(1)}, bf16[16,1024]{1,0:T(8,128)(2,1)S(1)}, u32[]{:S(2)}, u32[]{:S(2)}) %collective-permute-start.6) | collective-permute-done | bytes 32800 | tf_op jit(solution)/shard_map/ppermute | solution.py:27
  23.0 0.1 collective-permute-start.7
  23.0 0.7 %shard_map.98 = f32[8,48]{1,0:T(8,128)} custom-call(f32[3,16,8]{2,1,0:T(8,128)S(1)} %get-tuple-element.19.slot_resid_ref), custom_call_target="tpu_custom_call" | custom-call | flops 1000000 | bytes 10000 | tf_op jit(solution)/shard_map/pallas_call | solution.py:274
  23.7 0.6 %collective-permute-done.7 = f32[16,1024]{1,0:T(8,128)S(1)} collective-permute-done((f32[16,1024]{1,0:T(8,128)S(1)}, f32[16,1024]{1,0:T(8,128)S(1)}, u32[]{:S(2)}, u32[]{:S(2)}) %collective-permute-start.7) | collective-permute-done | bytes 65568 | tf_op jit(solution)/shard_map/ppermute | solution.py:291
  24.3 0.6 %add.15 = f32[16,1024]{1,0:T(8,128)} add(f32[16,1024]{1,0:T(8,128)S(1)} %convert_add_fusion, f32[16,1024]{1,0:T(8,128)S(1)} %collective-permute-done.7) | non-fusion elementwise | flops 16384 | bytes 196608 | tf_op jit(solution)/shard_map/add | solution.py:283
  (15 shorter events, 0.0 us)
Async XLA Ops:
  0.6 9.1 %copy-start = (bf16[32,64,1024]{2,1,0:T(8,128)(2,1)S(1)}, bf16[32,64,1024]{2,1,0:T(8,128)(2,1)}, u32[]{:S(2)}) copy-start(bf16[32,64,1024]{2,1,0:T(8,128)(2,1)} %refs_6_.1) | copy-start | bytes 12582916
  0.6 9.1 %copy-start.6 = (f32[48,8]{0,1:T(8,128)S(1)}, f32[48,8]{0,1:T(8,128)}, u32[]{:S(2)}) copy-start(f32[48,8]{0,1:T(8,128)} %param.15) | copy-start | bytes 4612
  0.7 9.1 %copy-start.5 = (f32[48,8]{0,1:T(8,128)S(1)}, f32[48,8]{0,1:T(8,128)}, u32[]{:S(2)}) copy-start(f32[48,8]{0,1:T(8,128)} %param.14) | copy-start | bytes 4612
  0.7 9.1 %copy-start.7 = (s32[8]{0:T(128)S(1)}, s32[8]{0:T(128)}, u32[]{:S(2)}) copy-start(s32[8]{0:T(128)} %param.13) | copy-start | bytes 100
  0.7 9.1 %copy-start.4 = (s32[48,8]{0,1:T(8,128)S(1)}, s32[48,8]{0,1:T(8,128)}, u32[]{:S(2)}) copy-start(s32[48,8]{0,1:T(8,128)} %param.12) | copy-start | bytes 4612
  0.7 9.1 %copy-start.3 = (f32[32,64]{1,0:T(8,128)S(1)}, f32[32,64]{1,0:T(8,128)}, u32[]{:S(2)}) copy-start(f32[32,64]{1,0:T(8,128)} %refs_5_.2) | copy-start | bytes 24580
  1.7 13.5 %copy-start.1 = (f32[16,1024]{1,0:T(8,128)S(1)}, f32[16,1024]{1,0:T(8,128)}, u32[]{:S(2)}) copy-start(f32[16,1024]{1,0:T(8,128)} %refs_4_.3) | copy-start | bytes 196612
  1.7 13.5 %copy-start.2 = (f32[16,1024]{1,0:T(8,128)S(1)}, f32[16,1024]{1,0:T(8,128)}, u32[]{:S(2)}) copy-start(f32[16,1024]{1,0:T(8,128)} %refs_5_.3) | copy-start | bytes 196612
  1.7 6.4 %collective-permute-start = (bf16[16,1024]{1,0:T(8,128)(2,1)S(1)}, bf16[16,1024]{1,0:T(8,128)(2,1)S(1)}, u32[]{:S(2)}, u32[]{:S(2)}) collective-permute-start(bf16[16,1024]{1,0:T(8,128)(2,1)S(1)} %shard_map.95.refs_3_), channel_id=1, source_target_pairs={{0,8},{1,5},{4,12},{5,9},{8,0},{9,13},{12,4},{13,1},{2,10},{3,7},{... | collective-permute-start | bytes 98312 | tf_op jit(solution)/shard_map/ppermute | solution.py:27
  5.8 3.9 %collective-permute-start.2 = (bf16[16,1024]{1,0:T(8,128)(2,1)S(1)}, bf16[16,1024]{1,0:T(8,128)(2,1)S(1)}, u32[]{:S(2)}, u32[]{:S(2)}) collective-permute-start(bf16[16,1024]{1,0:T(8,128)(2,1)S(1)} %shard_map.95.refs_3_), channel_id=1, source_target_pairs={{0,12},{4,0},{8,4},{12,8},{1,13},{5,1},{9,5},{13,9},{2,14},{6,2},{... | collective-permute-start | bytes 98312 | tf_op jit(solution)/shard_map/ppermute | solution.py:17
  8.2 1.6 %collective-permute-start.1 = (bf16[16,1024]{1,0:T(8,128)(2,1)S(1)}, bf16[16,1024]{1,0:T(8,128)(2,1)S(1)}, u32[]{:S(2)}, u32[]{:S(2)}) collective-permute-start(bf16[16,1024]{1,0:T(8,128)(2,1)S(1)} %collective-permute-done.refs_0_), channel_id=1, source_target_pairs={{0,1},{1,0},{2,3},{3,2},{4,5},{5,4},{6,7},{7,6},{8,9},{9,8},{10,11... | collective-permute-start | bytes 98312 | tf_op jit(solution)/shard_map/ppermute | solution.py:291
  11.3 3.9 %collective-permute-start.3 = (f32[3,16,8]{2,1,0:T(8,128)S(1)}, f32[3,16,8]{2,1,0:T(8,128)S(1)}, u32[]{:S(2)}, u32[]{:S(2)}) collective-permute-start(f32[3,16,8]{2,1,0:T(8,128)S(1)} %get-tuple-element.13.refs_0_), channel_id=1, source_target_pairs={{0,2},{2,0},{1,3},{3,1},{4,6},{6,4},{5,7},{7,5},{8,10},{10,8},{9,1... | collective-permute-start | bytes 4616 | tf_op jit(solution)/shard_map/ppermute | solution.py:291
  16.4 1.7 %collective-permute-start.5 = (f32[16,1024]{1,0:T(8,128)S(1)}, f32[16,1024]{1,0:T(8,128)S(1)}, u32[]{:S(2)}, u32[]{:S(2)}) collective-permute-start(f32[16,1024]{1,0:T(8,128)S(1)} %get-tuple-element.23), channel_id=1, source_target_pairs={{0,1},{1,0},{2,3},{3,2},{4,5},{5,4},{6,7},{7,6},{8,9},{9,8},{10,11... | collective-permute-start | bytes 196616 | tf_op jit(solution)/shard_map/ppermute | solution.py:291
  16.4 5.9 %collective-permute-start.4 = (bf16[16,1024]{1,0:T(8,128)(2,1)S(1)}, bf16[16,1024]{1,0:T(8,128)(2,1)S(1)}, u32[]{:S(2)}, u32[]{:S(2)}) collective-permute-start(bf16[16,1024]{1,0:T(8,128)(2,1)S(1)} %get-tuple-element.21), channel_id=1, source_target_pairs={{0,4},{4,8},{8,12},{12,0},{1,5},{5,9},{9,13},{13,1},{2,6},{6,10},{... | collective-permute-start | bytes 98312 | tf_op jit(solution)/shard_map/ppermute | solution.py:17
  18.1 4.9 %collective-permute-start.6 = (bf16[16,1024]{1,0:T(8,128)(2,1)S(1)}, bf16[16,1024]{1,0:T(8,128)(2,1)S(1)}, u32[]{:S(2)}, u32[]{:S(2)}) collective-permute-start(bf16[16,1024]{1,0:T(8,128)(2,1)S(1)} %add_convert_fusion), channel_id=1, source_target_pairs={{0,8},{1,13},{4,12},{5,1},{8,0},{9,5},{12,4},{13,9},{2,10},{3,15},... | collective-permute-start | bytes 98312 | tf_op jit(solution)/shard_map/ppermute | solution.py:27
  23.0 1.3 %collective-permute-start.7 = (f32[16,1024]{1,0:T(8,128)S(1)}, f32[16,1024]{1,0:T(8,128)S(1)}, u32[]{:S(2)}, u32[]{:S(2)}) collective-permute-start(f32[16,1024]{1,0:T(8,128)S(1)} %convert_add_fusion), channel_id=1, source_target_pairs={{0,1},{1,0},{2,3},{3,2},{4,5},{5,4},{6,7},{7,6},{8,9},{9,8},{10,11... | collective-permute-start | bytes 196616 | tf_op jit(solution)/shard_map/ppermute | solution.py:291

commit v5 on v4

--- a/solution.py
+++ b/solution.py
@@ -14,13 +14,34 @@
 
 def rolled(x, by):
     devices = lax.axis_size("tm")
-    return lax.ppermute(x, "tm", [(t, (t + by) % devices) for t in range(devices)])
-
-
-def shared(x, near, sign=1):
+    pairs = [(t * 2 + c, (t + by) % devices * 2 + 1 - c) for t in range(devices) for c in (0, 1)]
+    return lax.ppermute(x, ("tm", "stn"), pairs)
+
+
+def grouped(far, single):
+    rest = [d for d in range(1, far + 1) if d != single or far % 2 == 0]
+    groups = [(rest[i + 1], rest[i]) for i in range(0, len(rest), 2)]
+    return groups + [(single,)] * (far % 2)
+
+
+def grouped_fwd(far, single):
+    return [g[::-1] for g in grouped(far, single)]
+
+
+def shared(x, by):
     devices = lax.axis_size("tm")
     pairs = [
-        (t * 2 + core, (t + sign * (near + 1 - core)) % devices * 2 + core)
+        (t * 2 + 1 - core, (t + by[core]) % devices * 2 + core)
+        for t in range(devices)
+        for core in (0, 1)
+    ]
+    return lax.ppermute(x, ("tm", "stn"), pairs)
+
+
+def shared_back(x, by):
+    devices = lax.axis_size("tm")
+    pairs = [
+        (t * 2 + core, (t + by[core]) % devices * 2 + core)
         for t in range(devices)
         for core in (0, 1)
     ]
@@ -106,15 +127,17 @@
     per, slots, stations = out_ref.shape
     groups = blocks // GROUP
     core, shard = lax.axis_index("stn"), lax.axis_index("tm")
-    pieces = [own_ref[...]]
-    for near in range(1, far + 1, 2):
-        if near == far:
-            both = [moved_refs[near - 1][...]]
-        else:
-            mine, other = moved_refs[near - 1][...], moved_refs[near][...]
-            both = [jnp.where(core == 1, mine, other), jnp.where(core == 0, mine, other)]
-        for distance, piece in enumerate(both, near):
-            pieces.append(jnp.where(shard >= distance, piece, jnp.zeros_like(piece)))
+    pieces = {0: own_ref[...]}
+    moved_refs = list(moved_refs)
+    for group in grouped_fwd(far, 3):
+        got = moved_refs.pop(0)[...]
+        both = [got]
+        if len(group) == 2:
+            other = moved_refs.pop(0)[...]
+            both = [jnp.where(core == i, got, other) for i in (0, 1)]
+        for distance, piece in zip(group, both):
+            pieces[distance] = jnp.where(shard >= distance, piece, jnp.zeros_like(piece))
+    pieces = [pieces[d] for d in range(far + 1)]
     window = jnp.concatenate(pieces[::-1], 0)
     scale = lane_scale(block_scale_ref, groups)
     scale_ref[...] = scale
@@ -185,12 +208,15 @@
         start = rows - slots * (distance + 1)
         piece = returned[start : start + slots]
         near.append(jnp.where(shard >= distance, piece, jnp.zeros_like(piece)))
-    for first in range(0, len(near), 2):
-        if first + 1 < len(near):
-            sent_refs[first][...] = jnp.where(core == 0, near[first + 1], near[first])
-            sent_refs[first + 1][...] = jnp.where(core == 1, near[first + 1], near[first])
+    sent_refs = list(sent_refs)
+    for group in grouped(len(near), 3):
+        if len(group) == 1:
+            sent = sent_refs.pop(0)
+            sent[...] = near[group[0] - 1].astype(sent.dtype)
         else:
-            sent_refs[first][...] = near[first].astype(sent_refs[first].dtype)
+            first, second = near[group[0] - 1], near[group[1] - 1]
+            sent_refs.pop(0)[...] = jnp.where(core == 0, first, second)
+            sent_refs.pop(0)[...] = jnp.where(core == 1, first, second)
 
 
 def order_kernel(slot_resid_ref, resid_ref, swap_float):
@@ -222,11 +248,11 @@
         cost_estimate=pl.CostEstimate(flops=2 * 10**10, bytes_accessed=10**5, transcendentals=0),
     )(pltpu.with_memory_space_constraint(fluxes, pltpu.HBM))
     moved = []
-    for near in range(1, far + 1, 2):
-        if near == far:
-            moved.append(rolled(own, near))
+    for group in grouped_fwd(far, 3):
+        if len(group) == 1:
+            moved.append(rolled(own, group[0]))
         else:
-            got = shared(own, near)
+            got = shared(own, group)
             moved += [got, swapped_sum(got, "stn")]
     per = hours // slots
     groups = blocks // GROUP
@@ -263,12 +289,12 @@
         cost_estimate=cost,
     )(mine, other, seen, weight, fluxes, prior_weight, footprint, scale, mask, first)
     arrived = []
-    for near in range(1, far + 1, 2):
-        if near == far:
-            arrived.append(rolled(back[near - 1], -near))
+    for group in grouped(far, 3):
+        if len(group) == 1:
+            arrived.append(rolled(back.pop(0), -group[0]))
         else:
-            both = back[near - 1] + swapped_sum(back[near], "stn")
-            arrived.append(shared(both.astype(BF16), near, -1))
+            both = back.pop(0) + swapped_sum(back.pop(0), "stn")
+            arrived.append(shared_back(both.astype(BF16), [-d for d in group]))
     for piece in arrived[::-1]:
         total = total + piece
     resid = pl.pallas_call(

time: 25.1 us -> 24.3 us (0.968)
  starting transfers between devices: 11.5 us -> 10.6 us
    ppermute x2 -> x1, starting transfers between devices: 6.78 us -> 3.53 us  [shared(): return lax.ppermute(x, ('tm', 'stn'), pairs)]
    ppermute x2 -> x3, starting transfers between devices: 2.97 us -> 5 us  [the longest x1 2.62 us: shared_back(): return lax.ppermute(x, ('tm', 'stn'), pairs)]
    ppermute x4, starting transfers between devices: 1.71 us -> 2.11 us  [swapped_sum(): lax.ppermute(x, axis, [(i, (i + by) % devices) for i in range(devices)])]
    ppermute x2 -> x1, waiting for transfers between devices: 1.62 us -> 1.63 us  [shared(): return lax.ppermute(x, ('tm', 'stn'), pairs)]
    ppermute x2 -> x3, waiting for transfers between devices: 3.12 us -> 3.13 us  [the longest x2 2.11 us: rolled(): return lax.ppermute(x, ('tm', 'stn'), pairs)]
  transfers between devices with their start and end apart: 8 -> 8, of which waited for: 6 -> 7; matrix products, arithmetic and copies ran while one was open for 0% -> 0% of each run, Pallas kernels for 3% -> 3%
where the time goes in v5:
time: 24.3 us; the launch traced here: 24.1 us
  starting transfers between devices  10.6 us (44%)
  waiting for transfers between devices  7.64 us (31%)
  Pallas kernels  4.37 us (18%)
  between operations  0.77 us (3%)
  other arithmetic  0.66 us (3%)
    ppermute x1, starting transfers between devices, shared(): return lax.ppermute(x, ('tm', 'stn'), pairs)  3.53 us
    ppermute x4, waiting for transfers between devices, swapped_sum(): lax.ppermute(x, axis, [(i, (i + by) % devices) for i in range(devices)])  2.87 us
    ppermute x1, starting transfers between devices, shared_back(): return lax.ppermute(x, ('tm', 'stn'), pairs)  2.62 us
    ppermute x2, starting transfers between devices, rolled(): return lax.ppermute(x, ('tm', 'stn'), pairs)  2.38 us
    ppermute x2, waiting for transfers between devices, rolled(): return lax.ppermute(x, ('tm', 'stn'), pairs)  2.11 us
    ppermute x4, starting transfers between devices, swapped_sum(): lax.ppermute(x, axis, [(i, (i + by) % devices) for i in range(devices)])  2.11 us
    ppermute x1, waiting for transfers between devices, shared(): return lax.ppermute(x, ('tm', 'stn'), pairs)  1.63 us
    pallas_call x1, Pallas kernels, on_device(): pl.pallas_call(functools.partial(model_kernel, far), out_shape=[by_hour,...  1.56 us
  transfers between devices with their start and end apart: 8, of which 7 were waited for; matrix products, arithmetic and copies ran while one was open for 0% of the time, Pallas kernels for 3%

profile of v5, /device:TPU:0, one launch (start us, length us, event | category | flops | bytes accessed | tf_op | source)
XLA Modules:
  0.0 24.1 jit_solution(12246070870274393601)
XLA Ops:
  0.7 1.0 %shard_map.95.refs_3_ = bf16[16,1024]{1,0:T(8,128)(2,1)S(1)} custom-call(f32[16,1024]{1,0:T(8,128)} %refs_4_.3), custom_call_target="tpu_custom_call" | custom-call | flops 20000000000 | bytes 100000 | tf_op jit(solution)/shard_map/pallas_call | solution.py:241
  1.7 0.0 copy-start.1
  1.7 0.0 copy-start.2
  1.7 3.5 %collective-permute-start = (bf16[16,1024]{1,0:T(8,128)(2,1)S(1)}, bf16[16,1024]{1,0:T(8,128)(2,1)S(1)}, u32[]{:S(2)}, u32[]{:S(2)}) collective-permute-start(bf16[16,1024]{1,0:T(8,128)(2,1)S(1)} %shard_map.95.refs_3_), channel_id=1, source_target_pairs={{1,4},{0,9},{5,8},{4,13},{9,12},{8,1},{13,0},{12,5},{3,6},{2,11},{... | collective-permute-start | bytes 98312 | tf_op jit(solution)/shard_map/ppermute | solution.py:38
  5.3 1.1 %collective-permute-start.2 = (bf16[16,1024]{1,0:T(8,128)(2,1)S(1)}, bf16[16,1024]{1,0:T(8,128)(2,1)S(1)}, u32[]{:S(2)}, u32[]{:S(2)}) collective-permute-start(bf16[16,1024]{1,0:T(8,128)(2,1)S(1)} %shard_map.95.refs_3_), channel_id=1, source_target_pairs={{0,13},{1,12},{4,1},{5,0},{8,5},{9,4},{12,9},{13,8},{2,15},{3,14},... | collective-permute-start | bytes 98312 | tf_op jit(solution)/shard_map/ppermute | solution.py:18
  6.3 1.6 %collective-permute-done.refs_0_ = bf16[16,1024]{1,0:T(8,128)(2,1)S(1)} collective-permute-done((bf16[16,1024]{1,0:T(8,128)(2,1)S(1)}, bf16[16,1024]{1,0:T(8,128)(2,1)S(1)}, u32[]{:S(2)}, u32[]{:S(2)}) %collective-permute-start) | collective-permute-done | bytes 32800 | tf_op jit(solution)/shard_map/ppermute | solution.py:38
  8.0 0.0 collective-permute-start.1
  8.0 0.8 %collective-permute-done.2.refs_2_ = bf16[16,1024]{1,0:T(8,128)(2,1)S(1)} collective-permute-done((bf16[16,1024]{1,0:T(8,128)(2,1)S(1)}, bf16[16,1024]{1,0:T(8,128)(2,1)S(1)}, u32[]{:S(2)}, u32[]{:S(2)}) %collective-permute-start.2) | collective-permute-done | bytes 32800 | tf_op jit(solution)/shard_map/ppermute | solution.py:18
  8.8 0.4 %collective-permute-done.1.refs_1_ = bf16[16,1024]{1,0:T(8,128)(2,1)S(1)} collective-permute-done((bf16[16,1024]{1,0:T(8,128)(2,1)S(1)}, bf16[16,1024]{1,0:T(8,128)(2,1)S(1)}, u32[]{:S(2)}, u32[]{:S(2)}) %collective-permute-start.1) | collective-permute-done | bytes 32800 | tf_op jit(solution)/shard_map/ppermute | solution.py:317
  9.2 0.0 copy-done.5
  9.2 1.6 %shard_map.96 = (f32[3,16,8]{2,1,0:T(8,128)S(1)}, f32[8,256]{1,0:T(8,128)S(1)}, bf16[256,32]{1,0:T(8,128)(2,1)S(1)}, s32[3,16,32]{2,1,0:T(8,128)S(1)}, f32[3,16,8]{2,1,0:T(8,128)S(1)}, /*index=5*/f32[3,16,8]{2,1,0:T(8,128)S(1)}) custom-call(bf16[16,1024]{1,0:T(8,128)(2,1)S(1)} %collective-permute-done.refs_0_, ...), custom_call_target="tpu_custom_call" | custom-call | flops 268435456 | bytes 4194304 | tf_op jit(solution)/shard_map/pallas_call | solution.py:263
  10.8 2.0 %collective-permute-start.3 = (f32[3,16,8]{2,1,0:T(8,128)S(1)}, f32[3,16,8]{2,1,0:T(8,128)S(1)}, u32[]{:S(2)}, u32[]{:S(2)}) collective-permute-start(f32[3,16,8]{2,1,0:T(8,128)S(1)} %get-tuple-element.13.refs_0_), channel_id=1, source_target_pairs={{0,2},{2,0},{1,3},{3,1},{4,6},{6,4},{5,7},{7,5},{8,10},{10,8},{9,1... | collective-permute-start | bytes 4616 | tf_op jit(solution)/shard_map/ppermute | solution.py:317
  12.7 1.9 %collective-permute-done.3.refs_1_ = f32[3,16,8]{2,1,0:T(8,128)S(1)} collective-permute-done((f32[3,16,8]{2,1,0:T(8,128)S(1)}, f32[3,16,8]{2,1,0:T(8,128)S(1)}, u32[]{:S(2)}, u32[]{:S(2)}) %collective-permute-start.3) | collective-permute-done | bytes 1568 | tf_op jit(solution)/shard_map/ppermute | solution.py:317
  14.7 1.1 %shard_map.97 = (f32[3,16,8]{2,1,0:T(8,128)S(1)}, f32[16,1024]{1,0:T(8,128)S(1)}, f32[16,1024]{1,0:T(8,128)S(1)}, f32[16,1024]{1,0:T(8,128)S(1)}, bf16[16,1024]{1,0:T(8,128)(2,1)S(1)}) custom-call(f32[3,16,8]{2,1,0:T(8,128)S(1)} %get-tuple-element.13.refs_0_, f32[3,16,8]{2,1,0:T(8,128)S(1)} %collective-permute-done.3.refs_1_, ...), custom_call_target="tpu_custom_call" | custom-call | flops 268435456 | bytes 4194304 | tf_op jit(solution)/shard_map/pallas_call | solution.py:282
  15.8 0.1 collective-permute-start.5
  15.9 1.3 %collective-permute-start.4 = (bf16[16,1024]{1,0:T(8,128)(2,1)S(1)}, bf16[16,1024]{1,0:T(8,128)(2,1)S(1)}, u32[]{:S(2)}, u32[]{:S(2)}) collective-permute-start(bf16[16,1024]{1,0:T(8,128)(2,1)S(1)} %get-tuple-element.21), channel_id=1, source_target_pairs={{0,5},{1,4},{4,9},{5,8},{8,13},{9,12},{12,1},{13,0},{2,7},{3,6},{6... | collective-permute-start | bytes 98312 | tf_op jit(solution)/shard_map/ppermute | solution.py:18
  17.2 0.0 collective-permute-done.5
  17.2 2.6 %collective-permute-start.6 = (bf16[16,1024]{1,0:T(8,128)(2,1)S(1)}, bf16[16,1024]{1,0:T(8,128)(2,1)S(1)}, u32[]{:S(2)}, u32[]{:S(2)}) collective-permute-start(bf16[16,1024]{1,0:T(8,128)(2,1)S(1)} %add_convert_fusion), channel_id=1, source_target_pairs={{0,8},{1,13},{4,12},{5,1},{8,0},{9,5},{12,4},{13,9},{2,10},{3,15},... | collective-permute-start | bytes 98312 | tf_op jit(solution)/shard_map/ppermute | solution.py:48
  19.8 1.3 %collective-permute-done.4 = bf16[16,1024]{1,0:T(8,128)(2,1)S(1)} collective-permute-done((bf16[16,1024]{1,0:T(8,128)(2,1)S(1)}, bf16[16,1024]{1,0:T(8,128)(2,1)S(1)}, u32[]{:S(2)}, u32[]{:S(2)}) %collective-permute-start.4) | collective-permute-done | bytes 32800 | tf_op jit(solution)/shard_map/ppermute | solution.py:18
  21.1 1.0 %collective-permute-done.6 = bf16[16,1024]{1,0:T(8,128)(2,1)S(1)} collective-permute-done((bf16[16,1024]{1,0:T(8,128)(2,1)S(1)}, bf16[16,1024]{1,0:T(8,128)(2,1)S(1)}, u32[]{:S(2)}, u32[]{:S(2)}) %collective-permute-start.6) | collective-permute-done | bytes 32800 | tf_op jit(solution)/shard_map/ppermute | solution.py:48
  22.2 0.1 collective-permute-start.7
  22.2 0.7 %shard_map.98 = f32[8,48]{1,0:T(8,128)} custom-call(f32[3,16,8]{2,1,0:T(8,128)S(1)} %get-tuple-element.19.slot_resid_ref), custom_call_target="tpu_custom_call" | custom-call | flops 1000000 | bytes 10000 | tf_op jit(solution)/shard_map/pallas_call | solution.py:300
  22.9 0.6 %collective-permute-done.7 = f32[16,1024]{1,0:T(8,128)S(1)} collective-permute-done((f32[16,1024]{1,0:T(8,128)S(1)}, f32[16,1024]{1,0:T(8,128)S(1)}, u32[]{:S(2)}, u32[]{:S(2)}) %collective-permute-start.7) | collective-permute-done | bytes 65568 | tf_op jit(solution)/shard_map/ppermute | solution.py:317
  23.5 0.6 %add.15 = f32[16,1024]{1,0:T(8,128)} add(f32[16,1024]{1,0:T(8,128)S(1)} %convert_add_fusion, f32[16,1024]{1,0:T(8,128)S(1)} %collective-permute-done.7) | non-fusion elementwise | flops 16384 | bytes 196608 | tf_op jit(solution)/shard_map/add | solution.py:309
  (15 shorter events, 0.0 us)
Async XLA Ops:
  0.6 8.5 %copy-start = (bf16[32,64,1024]{2,1,0:T(8,128)(2,1)S(1)}, bf16[32,64,1024]{2,1,0:T(8,128)(2,1)}, u32[]{:S(2)}) copy-start(bf16[32,64,1024]{2,1,0:T(8,128)(2,1)} %refs_6_.1) | copy-start | bytes 12582916
  0.6 8.5 %copy-start.6 = (f32[48,8]{0,1:T(8,128)S(1)}, f32[48,8]{0,1:T(8,128)}, u32[]{:S(2)}) copy-start(f32[48,8]{0,1:T(8,128)} %param.15) | copy-start | bytes 4612
  0.7 8.5 %copy-start.5 = (f32[48,8]{0,1:T(8,128)S(1)}, f32[48,8]{0,1:T(8,128)}, u32[]{:S(2)}) copy-start(f32[48,8]{0,1:T(8,128)} %param.14) | copy-start | bytes 4612
  0.7 8.5 %copy-start.7 = (s32[8]{0:T(128)S(1)}, s32[8]{0:T(128)}, u32[]{:S(2)}) copy-start(s32[8]{0:T(128)} %param.13) | copy-start | bytes 100
  0.7 8.5 %copy-start.4 = (s32[48,8]{0,1:T(8,128)S(1)}, s32[48,8]{0,1:T(8,128)}, u32[]{:S(2)}) copy-start(s32[48,8]{0,1:T(8,128)} %param.12) | copy-start | bytes 4612
  0.7 8.5 %copy-start.3 = (f32[32,64]{1,0:T(8,128)S(1)}, f32[32,64]{1,0:T(8,128)}, u32[]{:S(2)}) copy-start(f32[32,64]{1,0:T(8,128)} %refs_5_.2) | copy-start | bytes 24580
  1.7 13.0 %copy-start.1 = (f32[16,1024]{1,0:T(8,128)S(1)}, f32[16,1024]{1,0:T(8,128)}, u32[]{:S(2)}) copy-start(f32[16,1024]{1,0:T(8,128)} %refs_4_.3) | copy-start | bytes 196612
  1.7 13.0 %copy-start.2 = (f32[16,1024]{1,0:T(8,128)S(1)}, f32[16,1024]{1,0:T(8,128)}, u32[]{:S(2)}) copy-start(f32[16,1024]{1,0:T(8,128)} %refs_5_.3) | copy-start | bytes 196612
  1.7 6.2 %collective-permute-start = (bf16[16,1024]{1,0:T(8,128)(2,1)S(1)}, bf16[16,1024]{1,0:T(8,128)(2,1)S(1)}, u32[]{:S(2)}, u32[]{:S(2)}) collective-permute-start(bf16[16,1024]{1,0:T(8,128)(2,1)S(1)} %shard_map.95.refs_3_), channel_id=1, source_target_pairs={{1,4},{0,9},{5,8},{4,13},{9,12},{8,1},{13,0},{12,5},{3,6},{2,11},{... | collective-permute-start | bytes 98312 | tf_op jit(solution)/shard_map/ppermute | solution.py:38
  5.3 3.6 %collective-permute-start.2 = (bf16[16,1024]{1,0:T(8,128)(2,1)S(1)}, bf16[16,1024]{1,0:T(8,128)(2,1)S(1)}, u32[]{:S(2)}, u32[]{:S(2)}) collective-permute-start(bf16[16,1024]{1,0:T(8,128)(2,1)S(1)} %shard_map.95.refs_3_), channel_id=1, source_target_pairs={{0,13},{1,12},{4,1},{5,0},{8,5},{9,4},{12,9},{13,8},{2,15},{3,14},... | collective-permute-start | bytes 98312 | tf_op jit(solution)/shard_map/ppermute | solution.py:18
  8.0 1.2 %collective-permute-start.1 = (bf16[16,1024]{1,0:T(8,128)(2,1)S(1)}, bf16[16,1024]{1,0:T(8,128)(2,1)S(1)}, u32[]{:S(2)}, u32[]{:S(2)}) collective-permute-start(bf16[16,1024]{1,0:T(8,128)(2,1)S(1)} %collective-permute-done.refs_0_), channel_id=1, source_target_pairs={{0,1},{1,0},{2,3},{3,2},{4,5},{5,4},{6,7},{7,6},{8,9},{9,8},{10,11... | collective-permute-start | bytes 98312 | tf_op jit(solution)/shard_map/ppermute | solution.py:317
  10.8 3.9 %collective-permute-start.3 = (f32[3,16,8]{2,1,0:T(8,128)S(1)}, f32[3,16,8]{2,1,0:T(8,128)S(1)}, u32[]{:S(2)}, u32[]{:S(2)}) collective-permute-start(f32[3,16,8]{2,1,0:T(8,128)S(1)} %get-tuple-element.13.refs_0_), channel_id=1, source_target_pairs={{0,2},{2,0},{1,3},{3,1},{4,6},{6,4},{5,7},{7,5},{8,10},{10,8},{9,1... | collective-permute-start | bytes 4616 | tf_op jit(solution)/shard_map/ppermute | solution.py:317
  15.8 1.4 %collective-permute-start.5 = (f32[16,1024]{1,0:T(8,128)S(1)}, f32[16,1024]{1,0:T(8,128)S(1)}, u32[]{:S(2)}, u32[]{:S(2)}) collective-permute-start(f32[16,1024]{1,0:T(8,128)S(1)} %get-tuple-element.23), channel_id=1, source_target_pairs={{0,1},{1,0},{2,3},{3,2},{4,5},{5,4},{6,7},{7,6},{8,9},{9,8},{10,11... | collective-permute-start | bytes 196616 | tf_op jit(solution)/shard_map/ppermute | solution.py:317
  15.9 5.2 %collective-permute-start.4 = (bf16[16,1024]{1,0:T(8,128)(2,1)S(1)}, bf16[16,1024]{1,0:T(8,128)(2,1)S(1)}, u32[]{:S(2)}, u32[]{:S(2)}) collective-permute-start(bf16[16,1024]{1,0:T(8,128)(2,1)S(1)} %get-tuple-element.21), channel_id=1, source_target_pairs={{0,5},{1,4},{4,9},{5,8},{8,13},{9,12},{12,1},{13,0},{2,7},{3,6},{6... | collective-permute-start | bytes 98312 | tf_op jit(solution)/shard_map/ppermute | solution.py:18
  17.2 4.9 %collective-permute-start.6 = (bf16[16,1024]{1,0:T(8,128)(2,1)S(1)}, bf16[16,1024]{1,0:T(8,128)(2,1)S(1)}, u32[]{:S(2)}, u32[]{:S(2)}) collective-permute-start(bf16[16,1024]{1,0:T(8,128)(2,1)S(1)} %add_convert_fusion), channel_id=1, source_target_pairs={{0,8},{1,13},{4,12},{5,1},{8,0},{9,5},{12,4},{13,9},{2,10},{3,15},... | collective-permute-start | bytes 98312 | tf_op jit(solution)/shard_map/ppermute | solution.py:48
  22.2 1.3 %collective-permute-start.7 = (f32[16,1024]{1,0:T(8,128)S(1)}, f32[16,1024]{1,0:T(8,128)S(1)}, u32[]{:S(2)}, u32[]{:S(2)}) collective-permute-start(f32[16,1024]{1,0:T(8,128)S(1)} %convert_add_fusion), channel_id=1, source_target_pairs={{0,1},{1,0},{2,3},{3,2},{4,5},{5,4},{6,7},{7,6},{8,9},{9,8},{10,11... | collective-permute-start | bytes 196616 | tf_op jit(solution)/shard_map/ppermute | solution.py:317

commit v6 on v5

--- a/solution.py
+++ b/solution.py
@@ -209,14 +209,14 @@
         piece = returned[start : start + slots]
         near.append(jnp.where(shard >= distance, piece, jnp.zeros_like(piece)))
     sent_refs = list(sent_refs)
-    for group in grouped(len(near), 3):
+    for group in grouped_fwd(len(near), 3):
         if len(group) == 1:
             sent = sent_refs.pop(0)
             sent[...] = near[group[0] - 1].astype(sent.dtype)
         else:
             first, second = near[group[0] - 1], near[group[1] - 1]
+            sent_refs.pop(0)[...] = jnp.where(core == 1, first, second)
             sent_refs.pop(0)[...] = jnp.where(core == 0, first, second)
-            sent_refs.pop(0)[...] = jnp.where(core == 1, first, second)
 
 
 def order_kernel(slot_resid_ref, resid_ref, swap_float):
@@ -289,12 +289,12 @@
         cost_estimate=cost,
     )(mine, other, seen, weight, fluxes, prior_weight, footprint, scale, mask, first)
     arrived = []
-    for group in grouped(far, 3):
+    for group in grouped_fwd(far, 3):
         if len(group) == 1:
             arrived.append(rolled(back.pop(0), -group[0]))
         else:
             both = back.pop(0) + swapped_sum(back.pop(0), "stn")
-            arrived.append(shared_back(both.astype(BF16), [-d for d in group]))
+            arrived.append(shared(both.astype(BF16), [-d for d in group]))
     for piece in arrived[::-1]:
         total = total + piece
     resid = pl.pallas_call(
@@ -316,7 +316,7 @@
     for by in range(1, devices):
         moved = lax.ppermute(x, axis, [(i, (i + by) % devices) for i in range(devices)])
         total = moved if total is None else total + moved
-    return total
+    return jnp.zeros_like(x) if total is None else total
 
 
 def solution(mesh):

time: 24.3 us -> 24 us (0.988)
  waiting for transfers between devices: 7.64 us -> 6.6 us
  starting transfers between devices: 10.6 us -> 11.4 us
    ppermute x1 -> x0, starting transfers between devices: 2.62 us -> none  [shared_back(): return lax.ppermute(x, ('tm', 'stn'), pairs)]
    ppermute x1 -> x2, starting transfers between devices: 3.53 us -> 5.83 us  [shared(): return lax.ppermute(x, ('tm', 'stn'), pairs)]
    ppermute x4, starting transfers between devices: 2.11 us -> 3.22 us  [swapped_sum(): lax.ppermute(x, axis, [(i, (i + by) % devices) for i in range(devices)])]
    ppermute x1 -> x0, waiting for transfers between devices: 1.02 us -> none  [shared_back(): return lax.ppermute(x, ('tm', 'stn'), pairs)]
    ppermute x4, waiting for transfers between devices: 2.87 us -> 2.53 us  [swapped_sum(): lax.ppermute(x, axis, [(i, (i + by) % devices) for i in range(devices)])]
    ppermute x2, waiting for transfers between devices: 2.11 us -> 2.43 us  [rolled(): return lax.ppermute(x, ('tm', 'stn'), pairs)]
    ppermute x1 -> x2, waiting for transfers between devices: 1.63 us -> 1.64 us  [shared(): return lax.ppermute(x, ('tm', 'stn'), pairs)]
  transfers between devices with their start and end apart: 8 -> 8, of which waited for: 7 -> 6; matrix products, arithmetic and copies ran while one was open for 0% -> 0% of each run, Pallas kernels for 3% -> 3%
where the time goes in v6:
time: 24 us; the launch traced here: 23.9 us
  starting transfers between devices  11.4 us (48%)
  waiting for transfers between devices  6.6 us (28%)
  Pallas kernels  4.37 us (18%)
  between operations  0.76 us (3%)
  other arithmetic  0.66 us (3%)
    ppermute x2, starting transfers between devices, shared(): return lax.ppermute(x, ('tm', 'stn'), pairs)  5.83 us
    ppermute x4, starting transfers between devices, swapped_sum(): lax.ppermute(x, axis, [(i, (i + by) % devices) for i in range(devices)])  3.22 us
    ppermute x4, waiting for transfers between devices, swapped_sum(): lax.ppermute(x, axis, [(i, (i + by) % devices) for i in range(devices)])  2.53 us
    ppermute x2, waiting for transfers between devices, rolled(): return lax.ppermute(x, ('tm', 'stn'), pairs)  2.43 us
    ppermute x2, starting transfers between devices, rolled(): return lax.ppermute(x, ('tm', 'stn'), pairs)  2.38 us
    ppermute x2, waiting for transfers between devices, shared(): return lax.ppermute(x, ('tm', 'stn'), pairs)  1.64 us
    pallas_call x1, Pallas kernels, on_device(): pl.pallas_call(functools.partial(model_kernel, far), out_shape=[by_hour,...  1.56 us
    pallas_call x1, Pallas kernels, on_device(): pl.pallas_call(return_kernel, out_shape=[by_hour, piece] + [piece] * (far...  1.13 us
  transfers between devices with their start and end apart: 8, of which 6 were waited for; matrix products, arithmetic and copies ran while one was open for 0% of the time, Pallas kernels for 3%

profile of v6, /device:TPU:0, one launch (start us, length us, event | category | flops | bytes accessed | tf_op | source)
XLA Modules:
  0.0 23.9 jit_solution(12074492476793031695)
XLA Ops:
  0.6 0.0 copy-start
  0.7 1.0 %shard_map.95.refs_3_ = bf16[16,1024]{1,0:T(8,128)(2,1)S(1)} custom-call(f32[16,1024]{1,0:T(8,128)} %refs_4_.3), custom_call_target="tpu_custom_call" | custom-call | flops 20000000000 | bytes 100000 | tf_op jit(solution)/shard_map/pallas_call | solution.py:241
  1.7 0.0 copy-start.1
  1.7 0.0 copy-start.2
  1.7 3.5 %collective-permute-start = (bf16[16,1024]{1,0:T(8,128)(2,1)S(1)}, bf16[16,1024]{1,0:T(8,128)(2,1)S(1)}, u32[]{:S(2)}, u32[]{:S(2)}) collective-permute-start(bf16[16,1024]{1,0:T(8,128)(2,1)S(1)} %shard_map.95.refs_3_), channel_id=1, source_target_pairs={{1,4},{0,9},{5,8},{4,13},{9,12},{8,1},{13,0},{12,5},{3,6},{2,11},{... | collective-permute-start | bytes 98312 | tf_op jit(solution)/shard_map/ppermute | solution.py:38
  5.3 1.1 %collective-permute-start.2 = (bf16[16,1024]{1,0:T(8,128)(2,1)S(1)}, bf16[16,1024]{1,0:T(8,128)(2,1)S(1)}, u32[]{:S(2)}, u32[]{:S(2)}) collective-permute-start(bf16[16,1024]{1,0:T(8,128)(2,1)S(1)} %shard_map.95.refs_3_), channel_id=1, source_target_pairs={{0,13},{1,12},{4,1},{5,0},{8,5},{9,4},{12,9},{13,8},{2,15},{3,14},... | collective-permute-start | bytes 98312 | tf_op jit(solution)/shard_map/ppermute | solution.py:18
  6.3 1.6 %collective-permute-done.refs_0_ = bf16[16,1024]{1,0:T(8,128)(2,1)S(1)} collective-permute-done((bf16[16,1024]{1,0:T(8,128)(2,1)S(1)}, bf16[16,1024]{1,0:T(8,128)(2,1)S(1)}, u32[]{:S(2)}, u32[]{:S(2)}) %collective-permute-start) | collective-permute-done | bytes 32800 | tf_op jit(solution)/shard_map/ppermute | solution.py:38
  8.0 0.0 collective-permute-start.1
  8.0 0.8 %collective-permute-done.2.refs_2_ = bf16[16,1024]{1,0:T(8,128)(2,1)S(1)} collective-permute-done((bf16[16,1024]{1,0:T(8,128)(2,1)S(1)}, bf16[16,1024]{1,0:T(8,128)(2,1)S(1)}, u32[]{:S(2)}, u32[]{:S(2)}) %collective-permute-start.2) | collective-permute-done | bytes 32800 | tf_op jit(solution)/shard_map/ppermute | solution.py:18
  8.8 0.4 %collective-permute-done.1.refs_1_ = bf16[16,1024]{1,0:T(8,128)(2,1)S(1)} collective-permute-done((bf16[16,1024]{1,0:T(8,128)(2,1)S(1)}, bf16[16,1024]{1,0:T(8,128)(2,1)S(1)}, u32[]{:S(2)}, u32[]{:S(2)}) %collective-permute-start.1) | collective-permute-done | bytes 32800 | tf_op jit(solution)/shard_map/ppermute | solution.py:317
  9.2 1.6 %shard_map.96 = (f32[3,16,8]{2,1,0:T(8,128)S(1)}, f32[8,256]{1,0:T(8,128)S(1)}, bf16[256,32]{1,0:T(8,128)(2,1)S(1)}, s32[3,16,32]{2,1,0:T(8,128)S(1)}, f32[3,16,8]{2,1,0:T(8,128)S(1)}, /*index=5*/f32[3,16,8]{2,1,0:T(8,128)S(1)}) custom-call(bf16[16,1024]{1,0:T(8,128)(2,1)S(1)} %collective-permute-done.refs_0_, ...), custom_call_target="tpu_custom_call" | custom-call | flops 268435456 | bytes 4194304 | tf_op jit(solution)/shard_map/pallas_call | solution.py:263
  10.8 2.0 %collective-permute-start.3 = (f32[3,16,8]{2,1,0:T(8,128)S(1)}, f32[3,16,8]{2,1,0:T(8,128)S(1)}, u32[]{:S(2)}, u32[]{:S(2)}) collective-permute-start(f32[3,16,8]{2,1,0:T(8,128)S(1)} %get-tuple-element.13.refs_0_), channel_id=1, source_target_pairs={{0,2},{2,0},{1,3},{3,1},{4,6},{6,4},{5,7},{7,5},{8,10},{10,8},{9,1... | collective-permute-start | bytes 4616 | tf_op jit(solution)/shard_map/ppermute | solution.py:317
  12.7 1.9 %collective-permute-done.3.refs_1_ = f32[3,16,8]{2,1,0:T(8,128)S(1)} collective-permute-done((f32[3,16,8]{2,1,0:T(8,128)S(1)}, f32[3,16,8]{2,1,0:T(8,128)S(1)}, u32[]{:S(2)}, u32[]{:S(2)}) %collective-permute-start.3) | collective-permute-done | bytes 1568 | tf_op jit(solution)/shard_map/ppermute | solution.py:317
  14.7 1.1 %shard_map.97 = (f32[3,16,8]{2,1,0:T(8,128)S(1)}, f32[16,1024]{1,0:T(8,128)S(1)}, f32[16,1024]{1,0:T(8,128)S(1)}, f32[16,1024]{1,0:T(8,128)S(1)}, bf16[16,1024]{1,0:T(8,128)(2,1)S(1)}) custom-call(f32[3,16,8]{2,1,0:T(8,128)S(1)} %get-tuple-element.13.refs_0_, f32[3,16,8]{2,1,0:T(8,128)S(1)} %collective-permute-done.3.refs_1_, ...), custom_call_target="tpu_custom_call" | custom-call | flops 268435456 | bytes 4194304 | tf_op jit(solution)/shard_map/pallas_call | solution.py:282
  15.8 0.1 collective-permute-start.5
  15.9 1.3 %collective-permute-start.4 = (bf16[16,1024]{1,0:T(8,128)(2,1)S(1)}, bf16[16,1024]{1,0:T(8,128)(2,1)S(1)}, u32[]{:S(2)}, u32[]{:S(2)}) collective-permute-start(bf16[16,1024]{1,0:T(8,128)(2,1)S(1)} %get-tuple-element.21), channel_id=1, source_target_pairs={{0,5},{1,4},{4,9},{5,8},{8,13},{9,12},{12,1},{13,0},{2,7},{3,6},{6... | collective-permute-start | bytes 98312 | tf_op jit(solution)/shard_map/ppermute | solution.py:18
  17.2 0.0 collective-permute-done.5
  17.2 2.3 %collective-permute-start.6 = (bf16[16,1024]{1,0:T(8,128)(2,1)S(1)}, bf16[16,1024]{1,0:T(8,128)(2,1)S(1)}, u32[]{:S(2)}, u32[]{:S(2)}) collective-permute-start(bf16[16,1024]{1,0:T(8,128)(2,1)S(1)} %add_convert_fusion), channel_id=1, source_target_pairs={{1,12},{0,9},{5,0},{4,13},{9,4},{8,1},{13,8},{12,5},{3,14},{2,11},... | collective-permute-start | bytes 98312 | tf_op jit(solution)/shard_map/ppermute | solution.py:38
  19.5 1.6 %collective-permute-done.4 = bf16[16,1024]{1,0:T(8,128)(2,1)S(1)} collective-permute-done((bf16[16,1024]{1,0:T(8,128)(2,1)S(1)}, bf16[16,1024]{1,0:T(8,128)(2,1)S(1)}, u32[]{:S(2)}, u32[]{:S(2)}) %collective-permute-start.4) | collective-permute-done | bytes 32800 | tf_op jit(solution)/shard_map/ppermute | solution.py:18
  21.1 0.0 collective-permute-done.6
  21.1 1.2 %collective-permute-start.7 = (f32[16,1024]{1,0:T(8,128)S(1)}, f32[16,1024]{1,0:T(8,128)S(1)}, u32[]{:S(2)}, u32[]{:S(2)}) collective-permute-start(f32[16,1024]{1,0:T(8,128)S(1)} %convert_add_fusion), channel_id=1, source_target_pairs={{0,1},{1,0},{2,3},{3,2},{4,5},{5,4},{6,7},{7,6},{8,9},{9,8},{10,11... | collective-permute-start | bytes 196616 | tf_op jit(solution)/shard_map/ppermute | solution.py:317
  22.3 0.7 %shard_map.98 = f32[8,48]{1,0:T(8,128)} custom-call(f32[3,16,8]{2,1,0:T(8,128)S(1)} %get-tuple-element.19.slot_resid_ref), custom_call_target="tpu_custom_call" | custom-call | flops 1000000 | bytes 10000 | tf_op jit(solution)/shard_map/pallas_call | solution.py:300
  23.0 0.2 collective-permute-done.7
  23.2 0.6 %add.15 = f32[16,1024]{1,0:T(8,128)} add(f32[16,1024]{1,0:T(8,128)S(1)} %convert_add_fusion, f32[16,1024]{1,0:T(8,128)S(1)} %collective-permute-done.7) | non-fusion elementwise | flops 16384 | bytes 196608 | tf_op jit(solution)/shard_map/add | solution.py:309
  (15 shorter events, 0.0 us)
Async XLA Ops:
  0.6 8.5 %copy-start = (bf16[32,64,1024]{2,1,0:T(8,128)(2,1)S(1)}, bf16[32,64,1024]{2,1,0:T(8,128)(2,1)}, u32[]{:S(2)}) copy-start(bf16[32,64,1024]{2,1,0:T(8,128)(2,1)} %refs_6_.1) | copy-start | bytes 12582916
  0.6 8.5 %copy-start.6 = (f32[48,8]{0,1:T(8,128)S(1)}, f32[48,8]{0,1:T(8,128)}, u32[]{:S(2)}) copy-start(f32[48,8]{0,1:T(8,128)} %param.15) | copy-start | bytes 4612
  0.7 8.5 %copy-start.5 = (f32[48,8]{0,1:T(8,128)S(1)}, f32[48,8]{0,1:T(8,128)}, u32[]{:S(2)}) copy-start(f32[48,8]{0,1:T(8,128)} %param.14) | copy-start | bytes 4612
  0.7 8.5 %copy-start.7 = (s32[8]{0:T(128)S(1)}, s32[8]{0:T(128)}, u32[]{:S(2)}) copy-start(s32[8]{0:T(128)} %param.13) | copy-start | bytes 100
  0.7 8.5 %copy-start.4 = (s32[48,8]{0,1:T(8,128)S(1)}, s32[48,8]{0,1:T(8,128)}, u32[]{:S(2)}) copy-start(s32[48,8]{0,1:T(8,128)} %param.12) | copy-start | bytes 4612
  0.7 8.5 %copy-start.3 = (f32[32,64]{1,0:T(8,128)S(1)}, f32[32,64]{1,0:T(8,128)}, u32[]{:S(2)}) copy-start(f32[32,64]{1,0:T(8,128)} %refs_5_.2) | copy-start | bytes 24580
  1.7 13.0 %copy-start.1 = (f32[16,1024]{1,0:T(8,128)S(1)}, f32[16,1024]{1,0:T(8,128)}, u32[]{:S(2)}) copy-start(f32[16,1024]{1,0:T(8,128)} %refs_4_.3) | copy-start | bytes 196612
  1.7 13.0 %copy-start.2 = (f32[16,1024]{1,0:T(8,128)S(1)}, f32[16,1024]{1,0:T(8,128)}, u32[]{:S(2)}) copy-start(f32[16,1024]{1,0:T(8,128)} %refs_5_.3) | copy-start | bytes 196612
  1.7 6.2 %collective-permute-start = (bf16[16,1024]{1,0:T(8,128)(2,1)S(1)}, bf16[16,1024]{1,0:T(8,128)(2,1)S(1)}, u32[]{:S(2)}, u32[]{:S(2)}) collective-permute-start(bf16[16,1024]{1,0:T(8,128)(2,1)S(1)} %shard_map.95.refs_3_), channel_id=1, source_target_pairs={{1,4},{0,9},{5,8},{4,13},{9,12},{8,1},{13,0},{12,5},{3,6},{2,11},{... | collective-permute-start | bytes 98312 | tf_op jit(solution)/shard_map/ppermute | solution.py:38
  5.3 3.6 %collective-permute-start.2 = (bf16[16,1024]{1,0:T(8,128)(2,1)S(1)}, bf16[16,1024]{1,0:T(8,128)(2,1)S(1)}, u32[]{:S(2)}, u32[]{:S(2)}) collective-permute-start(bf16[16,1024]{1,0:T(8,128)(2,1)S(1)} %shard_map.95.refs_3_), channel_id=1, source_target_pairs={{0,13},{1,12},{4,1},{5,0},{8,5},{9,4},{12,9},{13,8},{2,15},{3,14},... | collective-permute-start | bytes 98312 | tf_op jit(solution)/shard_map/ppermute | solution.py:18
  8.0 1.2 %collective-permute-start.1 = (bf16[16,1024]{1,0:T(8,128)(2,1)S(1)}, bf16[16,1024]{1,0:T(8,128)(2,1)S(1)}, u32[]{:S(2)}, u32[]{:S(2)}) collective-permute-start(bf16[16,1024]{1,0:T(8,128)(2,1)S(1)} %collective-permute-done.refs_0_), channel_id=1, source_target_pairs={{0,1},{1,0},{2,3},{3,2},{4,5},{5,4},{6,7},{7,6},{8,9},{9,8},{10,11... | collective-permute-start | bytes 98312 | tf_op jit(solution)/shard_map/ppermute | solution.py:317
  10.8 3.9 %collective-permute-start.3 = (f32[3,16,8]{2,1,0:T(8,128)S(1)}, f32[3,16,8]{2,1,0:T(8,128)S(1)}, u32[]{:S(2)}, u32[]{:S(2)}) collective-permute-start(f32[3,16,8]{2,1,0:T(8,128)S(1)} %get-tuple-element.13.refs_0_), channel_id=1, source_target_pairs={{0,2},{2,0},{1,3},{3,1},{4,6},{6,4},{5,7},{7,5},{8,10},{10,8},{9,1... | collective-permute-start | bytes 4616 | tf_op jit(solution)/shard_map/ppermute | solution.py:317
  15.8 1.4 %collective-permute-start.5 = (f32[16,1024]{1,0:T(8,128)S(1)}, f32[16,1024]{1,0:T(8,128)S(1)}, u32[]{:S(2)}, u32[]{:S(2)}) collective-permute-start(f32[16,1024]{1,0:T(8,128)S(1)} %get-tuple-element.23), channel_id=1, source_target_pairs={{0,1},{1,0},{2,3},{3,2},{4,5},{5,4},{6,7},{7,6},{8,9},{9,8},{10,11... | collective-permute-start | bytes 196616 | tf_op jit(solution)/shard_map/ppermute | solution.py:317
  15.9 5.2 %collective-permute-start.4 = (bf16[16,1024]{1,0:T(8,128)(2,1)S(1)}, bf16[16,1024]{1,0:T(8,128)(2,1)S(1)}, u32[]{:S(2)}, u32[]{:S(2)}) collective-permute-start(bf16[16,1024]{1,0:T(8,128)(2,1)S(1)} %get-tuple-element.21), channel_id=1, source_target_pairs={{0,5},{1,4},{4,9},{5,8},{8,13},{9,12},{12,1},{13,0},{2,7},{3,6},{6... | collective-permute-start | bytes 98312 | tf_op jit(solution)/shard_map/ppermute | solution.py:18
  17.2 3.9 %collective-permute-start.6 = (bf16[16,1024]{1,0:T(8,128)(2,1)S(1)}, bf16[16,1024]{1,0:T(8,128)(2,1)S(1)}, u32[]{:S(2)}, u32[]{:S(2)}) collective-permute-start(bf16[16,1024]{1,0:T(8,128)(2,1)S(1)} %add_convert_fusion), channel_id=1, source_target_pairs={{1,12},{0,9},{5,0},{4,13},{9,4},{8,1},{13,8},{12,5},{3,14},{2,11},... | collective-permute-start | bytes 98312 | tf_op jit(solution)/shard_map/ppermute | solution.py:38
  21.1 2.1 %collective-permute-start.7 = (f32[16,1024]{1,0:T(8,128)S(1)}, f32[16,1024]{1,0:T(8,128)S(1)}, u32[]{:S(2)}, u32[]{:S(2)}) collective-permute-start(f32[16,1024]{1,0:T(8,128)S(1)} %convert_add_fusion), channel_id=1, source_target_pairs={{0,1},{1,0},{2,3},{3,2},{4,5},{5,4},{6,7},{7,6},{8,9},{9,8},{10,11... | collective-permute-start | bytes 196616 | tf_op jit(solution)/shard_map/ppermute | solution.py:317

commit v7 on v6

--- a/solution.py
+++ b/solution.py
@@ -48,12 +48,13 @@
     return lax.ppermute(x, ("tm", "stn"), pairs)
 
 
-def reach_mask(len_ref, lags, stations):
-    shape = (GROUP * lags, GROUP * stations)
-    lengths = jnp.concatenate([len_ref[...]] * GROUP, axis=1)
+def reach_mask(len_ref, lags, stations, per, wide):
+    shape = (GROUP * lags, wide)
+    lengths = jnp.concatenate([len_ref[...]] * (wide // stations), axis=1)
     row = lax.broadcasted_iota(jnp.int32, shape, 0)
     col = lax.broadcasted_iota(jnp.int32, shape, 1)
-    same = (row // lags) == (col // stations)
+    part = GROUP * stations
+    same = ((row // lags) == (col % part // stations)) & (col < per * part)
     return jnp.where(same & ((row % lags) < lengths), 1.0, 0.0).astype(BF16)
 
 
@@ -111,10 +112,7 @@
     return x[x.shape[0] - rows :]
 
 
-def round_kernel(flux_hbm, out_ref, flux_ref, sem):
-    copy = pltpu.make_async_copy(flux_hbm, flux_ref, sem)
-    copy.start()
-    copy.wait()
+def round_kernel(flux_ref, out_ref):
     out_ref[...] = flux_ref[...].astype(out_ref.dtype)
 
 
@@ -124,7 +122,9 @@
      out_ref, scale_ref, mask_ref, first_ref, slot_seen_ref, slot_weight_ref,
      swap_int, swap_float) = refs[far:]
     blocks, lags, cells = table_ref.shape
-    per, slots, stations = out_ref.shape
+    slots, wide = out_ref.shape
+    stations, hours = index_ref.shape
+    per, part = hours // slots, GROUP * stations
     groups = blocks // GROUP
     core, shard = lax.axis_index("stn"), lax.axis_index("tm")
     pieces = {0: own_ref[...]}
@@ -141,17 +141,25 @@
     window = jnp.concatenate(pieces[::-1], 0)
     scale = lane_scale(block_scale_ref, groups)
     scale_ref[...] = scale
-    mask = reach_mask(len_ref, lags, stations)
+    mask = reach_mask(len_ref, lags, stations, per, wide)
     mask_ref[...] = mask
-    lane_block = lax.broadcasted_iota(jnp.int32, (slots, GROUP * stations), 1) // stations
+    lane = lax.broadcasted_iota(jnp.int32, (slots, wide), 1)
+    rest = wide - per * part
     swap_int[...] = index_ref[...].T
+    pieces = []
     for k in range(per):
-        index = swap_int[pl.ds(k, slots, stride=per), :]
-        first_ref[k] = jnp.concatenate([index] * GROUP, axis=1) - lane_block
+        pieces += [swap_int[pl.ds(k, slots, stride=per), :]] * GROUP
+    pieces += [jnp.zeros((slots, rest), jnp.int32)] if rest else []
+    first = jnp.concatenate(pieces, axis=1) - lane % part // stations
+    first_ref[...] = first
     for i, (source, target) in enumerate(((seen_ref, slot_seen_ref), (weight_ref, slot_weight_ref))):
         swap_float[i] = source[...].T
+        pieces = []
         for k in range(per):
-            target[k] = swap_float[i, pl.ds(k, slots, stride=per), :]
+            pieces.append(swap_float[i, pl.ds(k, slots, stride=per), :])
+            pieces.append(jnp.zeros((slots, part - stations), F32))
+        pieces += [jnp.zeros((slots, rest), F32)] if rest else []
+        target[...] = jnp.concatenate(pieces, axis=1)
     terms = []
     for g in range(groups):
         table = table_ref[g * GROUP : (g + 1) * GROUP].reshape(GROUP * lags, cells)
@@ -160,40 +168,36 @@
         ).T
         terms.append(skew_down(products, lags, slots) * scale[g : g + 1])
     sums = two_term_dot(jnp.concatenate(terms, 0), mask, 0)
-    for k in range(per):
-        first = first_ref[k]
-        picked = jnp.zeros((slots, GROUP * stations), F32)
-        for g in range(groups):
-            picked = jnp.where(first == g * GROUP, sums[g * slots : (g + 1) * slots], picked)
-        total = picked[:, :stations]
-        for i in range(1, GROUP):
-            total = total + picked[:, i * stations : (i + 1) * stations]
-        out_ref[k] = total
-
-
-def return_kernel(*refs):
+    picked = jnp.zeros((slots, wide), F32)
+    for g in range(groups):
+        picked = jnp.where(first == g * GROUP, sums[g * slots : (g + 1) * slots], picked)
+    total = picked
+    for i in range(1, GROUP):
+        total = total + pltpu.roll(picked, wide - i * stations, 1)
+    out_ref[...] = total
+
+
+def return_kernel(per, stations, *refs):
     (mine_ref, other_ref, seen_ref, weight_ref, flux_ref, prior_ref, table_ref, scale_ref,
      mask_ref, first_ref, resid_ref, own_ref, *rest) = refs
     *sent_refs, spread_ref = rest
     blocks, lags, cells = table_ref.shape
-    per, slots, stations = mine_ref.shape
+    slots, wide = mine_ref.shape
+    part = GROUP * stations
     groups = blocks // GROUP
     rows = spread_ref.shape[0]
     shard = lax.axis_index("tm")
     scale = scale_ref[...]
     mask = mask_ref[...]
-    firsts, resids = [], []
-    for k in range(per):
-        resid = weight_ref[k] * (mine_ref[k] + other_ref[k] - seen_ref[k])
-        resid_ref[k] = resid
-        resids.append(jnp.concatenate([resid] * GROUP, axis=1))
-        firsts.append(first_ref[k])
-    placed = []
-    for g in range(groups):
-        total = jnp.where(firsts[0] == g * GROUP, resids[0], 0.0)
-        for k in range(1, per):
-            total = total + jnp.where(firsts[k] == g * GROUP, resids[k], 0.0)
-        placed.append(total)
+    first = first_ref[...]
+    lane = lax.broadcasted_iota(jnp.int32, (slots, wide), 1)
+    held = (lane % part < stations) & (lane < per * part)
+    resid = jnp.where(held, weight_ref[...] * (mine_ref[...] + other_ref[...] - seen_ref[...]), 0.0)
+    resid_ref[...] = resid
+    spreading = resid
+    for i in range(1, GROUP):
+        spreading = spreading + pltpu.roll(resid, i * stations, 1)
+    placed = [jnp.where(first == g * GROUP, spreading, 0.0) for g in range(groups)]
     lagged = two_term_dot(jnp.concatenate(placed, 0), mask, 1)
     for g in range(groups):
         term = lagged[g * slots : (g + 1) * slots] * scale[g : g + 1]
@@ -220,9 +224,11 @@
 
 
 def order_kernel(slot_resid_ref, resid_ref, swap_float):
-    per, slots, _ = slot_resid_ref.shape
+    stations, hours = resid_ref.shape
+    slots, part = slot_resid_ref.shape[0], GROUP * stations
+    per = hours // slots
     for k in range(per):
-        swap_float[pl.ds(k, slots, stride=per), :] = slot_resid_ref[k]
+        swap_float[pl.ds(k, slots, stride=per), :] = slot_resid_ref[:, k * part : k * part + stations]
     resid_ref[...] = swap_float[...].T
 
 
@@ -238,15 +244,16 @@
     hours, stations = block_index.shape
     far = min(lags // slots, lax.axis_size("tm") - 1)
     rows = slots * (far + 1)
-    own = pl.pallas_call(
-        round_kernel,
-        out_shape=jax.ShapeDtypeStruct((slots, cells), BF16),
-        in_specs=[pl.BlockSpec(memory_space=pltpu.HBM)],
-        out_specs=VMEM,
-        scratch_shapes=[pltpu.VMEM((slots, cells), F32), pltpu.SemaphoreType.DMA],
-        compiler_params=pltpu.CompilerParams(vmem_limit_bytes=2 * 1024 * 1024),
-        cost_estimate=pl.CostEstimate(flops=2 * 10**10, bytes_accessed=10**5, transcendentals=0),
-    )(pltpu.with_memory_space_constraint(fluxes, pltpu.HBM))
+    own = fluxes
+    for flops in (10**4, 2 * 10**10):
+        own = pl.pallas_call(
+            round_kernel,
+            out_shape=jax.ShapeDtypeStruct((slots, cells), BF16),
+            in_specs=[VMEM],
+            out_specs=VMEM,
+            compiler_params=pltpu.CompilerParams(vmem_limit_bytes=2 * 1024 * 1024),
+            cost_estimate=pl.CostEstimate(flops=flops, bytes_accessed=10**5, transcendentals=0),
+        )(own)
     moved = []
     for group in grouped_fwd(far, 3):
         if len(group) == 1:
@@ -256,7 +263,8 @@
             moved += [got, swapped_sum(got, "stn")]
     per = hours // slots
     groups = blocks // GROUP
-    by_hour = jax.ShapeDtypeStruct((per, slots, stations), F32)
+    wide = -(-per * GROUP * stations // 128) * 128
+    by_hour = jax.ShapeDtypeStruct((slots, wide), F32)
     flops = 2 * blocks * lags * cells * rows
     nbytes = blocks * lags * cells * 2
     cost = pl.CostEstimate(flops=flops, bytes_accessed=nbytes, transcendentals=0)
@@ -265,8 +273,8 @@
         out_shape=[
             by_hour,
             jax.ShapeDtypeStruct((groups, GROUP * lags), F32),
-            jax.ShapeDtypeStruct((GROUP * lags, GROUP * stations), BF16),
-            jax.ShapeDtypeStruct((per, slots, GROUP * stations), jnp.int32),
+            jax.ShapeDtypeStruct((GROUP * lags, wide), BF16),
+            jax.ShapeDtypeStruct((slots, wide), jnp.int32),
             by_hour,
             by_hour,
         ],
@@ -280,7 +288,7 @@
     piece = jax.ShapeDtypeStruct((slots, cells), F32)
     sent = jax.ShapeDtypeStruct((slots, cells), BF16)
     resid, total, *back = pl.pallas_call(
-        return_kernel,
+        functools.partial(return_kernel, per, stations),
         out_shape=[by_hour, piece] + [piece] * (far // 2 * 2) + [sent] * (far % 2),
         in_specs=[VMEM] * 10,
         out_specs=[VMEM] * (2 + far),

time: 24 us -> 23.6 us (0.983)
  Pallas kernels: 4.37 us -> 3.4 us
  local copies, waits for them, and re-layouts: 0.04 us -> 0.88 us
    pallas_call x1 -> x2, Pallas kernels: 1 us -> 0.01 us  [on_device(): pl.pallas_call(round_kernel, out_shape=jax.ShapeDtypeStruct((slots, cells...]
    unnamed x16 -> x18, local copies, waits for them, and re-layouts: 0.04 us -> 0.88 us
    ppermute x4, waiting for transfers between devices: 2.53 us -> 2.28 us  [swapped_sum(): lax.ppermute(x, axis, [(i, (i + by) % devices) for i in range(devices)])]
where the time goes in v7:
time: 23.6 us; the launch traced here: 23.4 us
  starting transfers between devices  11.4 us (48%)
  waiting for transfers between devices  6.36 us (27%)
  Pallas kernels  3.4 us (14%)
  local copies, waits for them, and re-layouts  0.88 us (4%)
  between operations  0.75 us (3%)
  other arithmetic  0.66 us (3%)
    ppermute x2, starting transfers between devices, shared(): return lax.ppermute(x, ('tm', 'stn'), pairs)  5.82 us
    ppermute x4, starting transfers between devices, swapped_sum(): lax.ppermute(x, axis, [(i, (i + by) % devices) for i in range(devices)])  3.17 us
    ppermute x2, waiting for transfers between devices, rolled(): return lax.ppermute(x, ('tm', 'stn'), pairs)  2.44 us
    ppermute x2, starting transfers between devices, rolled(): return lax.ppermute(x, ('tm', 'stn'), pairs)  2.38 us
    ppermute x4, waiting for transfers between devices, swapped_sum(): lax.ppermute(x, axis, [(i, (i + by) % devices) for i in range(devices)])  2.28 us
    ppermute x2, waiting for transfers between devices, shared(): return lax.ppermute(x, ('tm', 'stn'), pairs)  1.64 us
    pallas_call x1, Pallas kernels, on_device(): pl.pallas_call(functools.partial(model_kernel, far), out_shape=[by_hour,...  1.53 us
    pallas_call x1, Pallas kernels, on_device(): pl.pallas_call(functools.partial(return_kernel, per, stations), out_shape...  1.12 us
  transfers between devices with their start and end apart: 8, of which 6 were waited for; matrix products, arithmetic and copies ran while one was open for 0% of the time, Pallas kernels for 3%

profile of v7, /device:TPU:0, one launch (start us, length us, event | category | flops | bytes accessed | tf_op | source)
XLA Modules:
  0.0 23.4 jit_solution(6049919006555587974)
XLA Ops:
  0.6 0.0 copy-start.1
  0.6 0.8 %copy-done.1 = f32[16,1024]{1,0:T(8,128)S(1)} copy-done((f32[16,1024]{1,0:T(8,128)S(1)}, f32[16,1024]{1,0:T(8,128)}, u32[]{:S(2)}) %copy-start.1) | copy-done | bytes 65560
  1.5 0.0 copy-start.6
  1.5 0.0 copy-start.7
  1.5 0.0 copy-start.2
  1.6 0.0 copy-start.3
  1.6 3.5 %collective-permute-start = (bf16[16,1024]{1,0:T(8,128)(2,1)S(1)}, bf16[16,1024]{1,0:T(8,128)(2,1)S(1)}, u32[]{:S(2)}, u32[]{:S(2)}) collective-permute-start(bf16[16,1024]{1,0:T(8,128)(2,1)S(1)} %shard_map.96.refs_3_), channel_id=1, source_target_pairs={{1,4},{0,9},{5,8},{4,13},{9,12},{8,1},{13,0},{12,5},{3,6},{2,11},{... | collective-permute-start | bytes 98312 | tf_op jit(solution)/shard_map/ppermute | solution.py:38
  5.1 1.1 %collective-permute-start.2 = (bf16[16,1024]{1,0:T(8,128)(2,1)S(1)}, bf16[16,1024]{1,0:T(8,128)(2,1)S(1)}, u32[]{:S(2)}, u32[]{:S(2)}) collective-permute-start(bf16[16,1024]{1,0:T(8,128)(2,1)S(1)} %shard_map.96.refs_3_), channel_id=1, source_target_pairs={{0,13},{1,12},{4,1},{5,0},{8,5},{9,4},{12,9},{13,8},{2,15},{3,14},... | collective-permute-start | bytes 98312 | tf_op jit(solution)/shard_map/ppermute | solution.py:18
  6.2 1.6 %collective-permute-done.refs_0_ = bf16[16,1024]{1,0:T(8,128)(2,1)S(1)} collective-permute-done((bf16[16,1024]{1,0:T(8,128)(2,1)S(1)}, bf16[16,1024]{1,0:T(8,128)(2,1)S(1)}, u32[]{:S(2)}, u32[]{:S(2)}) %collective-permute-start) | collective-permute-done | bytes 32800 | tf_op jit(solution)/shard_map/ppermute | solution.py:38
  7.8 0.0 collective-permute-start.1
  7.8 0.8 %collective-permute-done.2.refs_2_ = bf16[16,1024]{1,0:T(8,128)(2,1)S(1)} collective-permute-done((bf16[16,1024]{1,0:T(8,128)(2,1)S(1)}, bf16[16,1024]{1,0:T(8,128)(2,1)S(1)}, u32[]{:S(2)}, u32[]{:S(2)}) %collective-permute-start.2) | collective-permute-done | bytes 32800 | tf_op jit(solution)/shard_map/ppermute | solution.py:18
  8.7 0.4 %collective-permute-done.1.refs_1_ = bf16[16,1024]{1,0:T(8,128)(2,1)S(1)} collective-permute-done((bf16[16,1024]{1,0:T(8,128)(2,1)S(1)}, bf16[16,1024]{1,0:T(8,128)(2,1)S(1)}, u32[]{:S(2)}, u32[]{:S(2)}) %collective-permute-start.1) | collective-permute-done | bytes 32800 | tf_op jit(solution)/shard_map/ppermute | solution.py:325
  9.1 1.5 %shard_map.97 = (f32[16,128]{1,0:T(8,128)S(1)}, f32[8,256]{1,0:T(8,128)S(1)}, bf16[256,128]{1,0:T(8,128)(2,1)S(1)}, s32[16,128]{1,0:T(8,128)S(1)}, f32[16,128]{1,0:T(8,128)S(1)}, /*index=5*/f32[16,128]{1,0:T(8,128)S(1)}) custom-call(bf16[16,1024]{1,0:T(8,128)(2,1)S(1)} %collective-permute-done.refs_0_, bf16[16,1024]{1,0:T(8,128)(2,1)S(1)} %collective-permute-done.1.refs_1_, ...), custom_call_target="tpu_custom_call" | custom-call | flops 268435456 | bytes 4194304 | tf_op jit(solution)/shard_map/pallas_call | solution.py:271
  10.6 1.9 %collective-permute-start.3 = (f32[16,128]{1,0:T(8,128)S(1)}, f32[16,128]{1,0:T(8,128)S(1)}, u32[]{:S(2)}, u32[]{:S(2)}) collective-permute-start(f32[16,128]{1,0:T(8,128)S(1)} %get-tuple-element.13.refs_0_), channel_id=1, source_target_pairs={{0,2},{2,0},{1,3},{3,1},{4,6},{6,4},{5,7},{7,5},{8,10},{10,8},{9,1... | collective-permute-start | bytes 24584 | tf_op jit(solution)/shard_map/ppermute | solution.py:325
  12.5 1.8 %collective-permute-done.3.refs_1_ = f32[16,128]{1,0:T(8,128)S(1)} collective-permute-done((f32[16,128]{1,0:T(8,128)S(1)}, f32[16,128]{1,0:T(8,128)S(1)}, u32[]{:S(2)}, u32[]{:S(2)}) %collective-permute-start.3) | collective-permute-done | bytes 8224 | tf_op jit(solution)/shard_map/ppermute | solution.py:325
  14.3 1.1 %shard_map.98 = (f32[16,128]{1,0:T(8,128)S(1)}, f32[16,1024]{1,0:T(8,128)S(1)}, f32[16,1024]{1,0:T(8,128)S(1)}, f32[16,1024]{1,0:T(8,128)S(1)}, bf16[16,1024]{1,0:T(8,128)(2,1)S(1)}) custom-call(f32[16,128]{1,0:T(8,128)S(1)} %get-tuple-element.13.refs_0_, f32[16,128]{1,0:T(8,128)S(1)} %collective-permute-done.3.refs_1_, ...), custom_call_target="tpu_custom_call" | custom-call | flops 268435456 | bytes 4194304 | tf_op jit(solution)/shard_map/pallas_call | solution.py:290
  15.4 0.1 collective-permute-start.5
  15.5 1.3 %collective-permute-start.4 = (bf16[16,1024]{1,0:T(8,128)(2,1)S(1)}, bf16[16,1024]{1,0:T(8,128)(2,1)S(1)}, u32[]{:S(2)}, u32[]{:S(2)}) collective-permute-start(bf16[16,1024]{1,0:T(8,128)(2,1)S(1)} %get-tuple-element.21), channel_id=1, source_target_pairs={{0,5},{1,4},{4,9},{5,8},{8,13},{9,12},{12,1},{13,0},{2,7},{3,6},{6... | collective-permute-start | bytes 98312 | tf_op jit(solution)/shard_map/ppermute | solution.py:18
  16.8 2.3 %collective-permute-start.6 = (bf16[16,1024]{1,0:T(8,128)(2,1)S(1)}, bf16[16,1024]{1,0:T(8,128)(2,1)S(1)}, u32[]{:S(2)}, u32[]{:S(2)}) collective-permute-start(bf16[16,1024]{1,0:T(8,128)(2,1)S(1)} %add_convert_fusion), channel_id=1, source_target_pairs={{1,12},{0,9},{5,0},{4,13},{9,4},{8,1},{13,8},{12,5},{3,14},{2,11},... | collective-permute-start | bytes 98312 | tf_op jit(solution)/shard_map/ppermute | solution.py:38
  19.1 1.6 %collective-permute-done.4 = bf16[16,1024]{1,0:T(8,128)(2,1)S(1)} collective-permute-done((bf16[16,1024]{1,0:T(8,128)(2,1)S(1)}, bf16[16,1024]{1,0:T(8,128)(2,1)S(1)}, u32[]{:S(2)}, u32[]{:S(2)}) %collective-permute-start.4) | collective-permute-done | bytes 32800 | tf_op jit(solution)/shard_map/ppermute | solution.py:18
  20.7 1.2 %collective-permute-start.7 = (f32[16,1024]{1,0:T(8,128)S(1)}, f32[16,1024]{1,0:T(8,128)S(1)}, u32[]{:S(2)}, u32[]{:S(2)}) collective-permute-start(f32[16,1024]{1,0:T(8,128)S(1)} %convert_add_fusion), channel_id=1, source_target_pairs={{0,1},{1,0},{2,3},{3,2},{4,5},{5,4},{6,7},{7,6},{8,9},{9,8},{10,11... | collective-permute-start | bytes 196616 | tf_op jit(solution)/shard_map/ppermute | solution.py:325
  21.9 0.7 %shard_map.99 = f32[8,48]{1,0:T(8,128)} custom-call(f32[16,128]{1,0:T(8,128)S(1)} %get-tuple-element.19.slot_resid_ref), custom_call_target="tpu_custom_call" | custom-call | flops 1000000 | bytes 10000 | tf_op jit(solution)/shard_map/pallas_call | solution.py:308
  22.6 0.2 collective-permute-done.7
  22.8 0.6 %add.15 = f32[16,1024]{1,0:T(8,128)} add(f32[16,1024]{1,0:T(8,128)S(1)} %convert_add_fusion, f32[16,1024]{1,0:T(8,128)S(1)} %collective-permute-done.7) | non-fusion elementwise | flops 16384 | bytes 196608 | tf_op jit(solution)/shard_map/add | solution.py:317
  (18 shorter events, 0.1 us)
Async XLA Ops:
  0.6 0.8 %copy-start.1 = (f32[16,1024]{1,0:T(8,128)S(1)}, f32[16,1024]{1,0:T(8,128)}, u32[]{:S(2)}) copy-start(f32[16,1024]{1,0:T(8,128)} %refs_4_.3) | copy-start | bytes 196612
  1.5 7.5 %copy-start = (bf16[32,64,1024]{2,1,0:T(8,128)(2,1)S(1)}, bf16[32,64,1024]{2,1,0:T(8,128)(2,1)}, u32[]{:S(2)}) copy-start(bf16[32,64,1024]{2,1,0:T(8,128)(2,1)} %refs_6_.1) | copy-start | bytes 12582916
  1.5 7.5 %copy-start.4 = (f32[32,64]{1,0:T(8,128)S(1)}, f32[32,64]{1,0:T(8,128)}, u32[]{:S(2)}) copy-start(f32[32,64]{1,0:T(8,128)} %refs_5_.2) | copy-start | bytes 24580
  1.5 7.5 %copy-start.5 = (s32[48,8]{0,1:T(8,128)S(1)}, s32[48,8]{0,1:T(8,128)}, u32[]{:S(2)}) copy-start(s32[48,8]{0,1:T(8,128)} %param.12) | copy-start | bytes 4612
  1.5 7.5 %copy-start.6 = (f32[48,8]{0,1:T(8,128)S(1)}, f32[48,8]{0,1:T(8,128)}, u32[]{:S(2)}) copy-start(f32[48,8]{0,1:T(8,128)} %param.14) | copy-start | bytes 4612
  1.5 7.5 %copy-start.7 = (f32[48,8]{0,1:T(8,128)S(1)}, f32[48,8]{0,1:T(8,128)}, u32[]{:S(2)}) copy-start(f32[48,8]{0,1:T(8,128)} %param.15) | copy-start | bytes 4612
  1.5 7.5 %copy-start.8 = (s32[8]{0:T(128)S(1)}, s32[8]{0:T(128)}, u32[]{:S(2)}) copy-start(s32[8]{0:T(128)} %param.13) | copy-start | bytes 100
  1.5 12.7 %copy-start.2 = (f32[16,1024]{1,0:T(8,128)S(1)}, f32[16,1024]{1,0:T(8,128)}, u32[]{:S(2)}) copy-start(f32[16,1024]{1,0:T(8,128)} %refs_4_.3) | copy-start | bytes 196612
  1.6 12.7 %copy-start.3 = (f32[16,1024]{1,0:T(8,128)S(1)}, f32[16,1024]{1,0:T(8,128)}, u32[]{:S(2)}) copy-start(f32[16,1024]{1,0:T(8,128)} %refs_5_.3) | copy-start | bytes 196612
  1.6 6.2 %collective-permute-start = (bf16[16,1024]{1,0:T(8,128)(2,1)S(1)}, bf16[16,1024]{1,0:T(8,128)(2,1)S(1)}, u32[]{:S(2)}, u32[]{:S(2)}) collective-permute-start(bf16[16,1024]{1,0:T(8,128)(2,1)S(1)} %shard_map.96.refs_3_), channel_id=1, source_target_pairs={{1,4},{0,9},{5,8},{4,13},{9,12},{8,1},{13,0},{12,5},{3,6},{2,11},{... | collective-permute-start | bytes 98312 | tf_op jit(solution)/shard_map/ppermute | solution.py:38
  5.1 3.6 %collective-permute-start.2 = (bf16[16,1024]{1,0:T(8,128)(2,1)S(1)}, bf16[16,1024]{1,0:T(8,128)(2,1)S(1)}, u32[]{:S(2)}, u32[]{:S(2)}) collective-permute-start(bf16[16,1024]{1,0:T(8,128)(2,1)S(1)} %shard_map.96.refs_3_), channel_id=1, source_target_pairs={{0,13},{1,12},{4,1},{5,0},{8,5},{9,4},{12,9},{13,8},{2,15},{3,14},... | collective-permute-start | bytes 98312 | tf_op jit(solution)/shard_map/ppermute | solution.py:18
  7.8 1.2 %collective-permute-start.1 = (bf16[16,1024]{1,0:T(8,128)(2,1)S(1)}, bf16[16,1024]{1,0:T(8,128)(2,1)S(1)}, u32[]{:S(2)}, u32[]{:S(2)}) collective-permute-start(bf16[16,1024]{1,0:T(8,128)(2,1)S(1)} %collective-permute-done.refs_0_), channel_id=1, source_target_pairs={{0,1},{1,0},{2,3},{3,2},{4,5},{5,4},{6,7},{7,6},{8,9},{9,8},{10,11... | collective-permute-start | bytes 98312 | tf_op jit(solution)/shard_map/ppermute | solution.py:325
  10.6 3.7 %collective-permute-start.3 = (f32[16,128]{1,0:T(8,128)S(1)}, f32[16,128]{1,0:T(8,128)S(1)}, u32[]{:S(2)}, u32[]{:S(2)}) collective-permute-start(f32[16,128]{1,0:T(8,128)S(1)} %get-tuple-element.13.refs_0_), channel_id=1, source_target_pairs={{0,2},{2,0},{1,3},{3,1},{4,6},{6,4},{5,7},{7,5},{8,10},{10,8},{9,1... | collective-permute-start | bytes 24584 | tf_op jit(solution)/shard_map/ppermute | solution.py:325
  15.4 1.4 %collective-permute-start.5 = (f32[16,1024]{1,0:T(8,128)S(1)}, f32[16,1024]{1,0:T(8,128)S(1)}, u32[]{:S(2)}, u32[]{:S(2)}) collective-permute-start(f32[16,1024]{1,0:T(8,128)S(1)} %get-tuple-element.23), channel_id=1, source_target_pairs={{0,1},{1,0},{2,3},{3,2},{4,5},{5,4},{6,7},{7,6},{8,9},{9,8},{10,11... | collective-permute-start | bytes 196616 | tf_op jit(solution)/shard_map/ppermute | solution.py:325
  15.5 5.2 %collective-permute-start.4 = (bf16[16,1024]{1,0:T(8,128)(2,1)S(1)}, bf16[16,1024]{1,0:T(8,128)(2,1)S(1)}, u32[]{:S(2)}, u32[]{:S(2)}) collective-permute-start(bf16[16,1024]{1,0:T(8,128)(2,1)S(1)} %get-tuple-element.21), channel_id=1, source_target_pairs={{0,5},{1,4},{4,9},{5,8},{8,13},{9,12},{12,1},{13,0},{2,7},{3,6},{6... | collective-permute-start | bytes 98312 | tf_op jit(solution)/shard_map/ppermute | solution.py:18
  16.8 3.9 %collective-permute-start.6 = (bf16[16,1024]{1,0:T(8,128)(2,1)S(1)}, bf16[16,1024]{1,0:T(8,128)(2,1)S(1)}, u32[]{:S(2)}, u32[]{:S(2)}) collective-permute-start(bf16[16,1024]{1,0:T(8,128)(2,1)S(1)} %add_convert_fusion), channel_id=1, source_target_pairs={{1,12},{0,9},{5,0},{4,13},{9,4},{8,1},{13,8},{12,5},{3,14},{2,11},... | collective-permute-start | bytes 98312 | tf_op jit(solution)/shard_map/ppermute | solution.py:38
  20.7 2.1 %collective-permute-start.7 = (f32[16,1024]{1,0:T(8,128)S(1)}, f32[16,1024]{1,0:T(8,128)S(1)}, u32[]{:S(2)}, u32[]{:S(2)}) collective-permute-start(f32[16,1024]{1,0:T(8,128)S(1)} %convert_add_fusion), channel_id=1, source_target_pairs={{0,1},{1,0},{2,3},{3,2},{4,5},{5,4},{6,7},{7,6},{8,9},{9,8},{10,11... | collective-permute-start | bytes 196616 | tf_op jit(solution)/shard_map/ppermute | solution.py:325

commit v8 on v7

--- a/solution.py
+++ b/solution.py
@@ -18,6 +18,11 @@
     return lax.ppermute(x, ("tm", "stn"), pairs)
 
 
+def straight(x, by):
+    devices = lax.axis_size("tm")
+    return lax.ppermute(x, "tm", [(t, (t + by) % devices) for t in range(devices)])
+
+
 def grouped(far, single):
     rest = [d for d in range(1, far + 1) if d != single or far % 2 == 0]
     groups = [(rest[i + 1], rest[i]) for i in range(0, len(rest), 2)]
@@ -32,16 +37,6 @@
     devices = lax.axis_size("tm")
     pairs = [
         (t * 2 + 1 - core, (t + by[core]) % devices * 2 + core)
-        for t in range(devices)
-        for core in (0, 1)
-    ]
-    return lax.ppermute(x, ("tm", "stn"), pairs)
-
-
-def shared_back(x, by):
-    devices = lax.axis_size("tm")
-    pairs = [
-        (t * 2 + core, (t + by[core]) % devices * 2 + core)
         for t in range(devices)
         for core in (0, 1)
     ]
@@ -163,11 +158,18 @@
     terms = []
     for g in range(groups):
         table = table_ref[g * GROUP : (g + 1) * GROUP].reshape(GROUP * lags, cells)
-        products = lax.dot_general(
-            table, window, (((1,), (1,)), ((), ())), preferred_element_type=F32
-        ).T
+        if g < groups - 1:
+            products = lax.dot_general(
+                table, window, (((1,), (1,)), ((), ())), preferred_element_type=F32
+            ).T
+        else:
+            products = lax.dot_general(
+                window, table, (((1,), (1,)), ((), ())), preferred_element_type=F32
+            )
         terms.append(skew_down(products, lags, slots) * scale[g : g + 1])
-    sums = two_term_dot(jnp.concatenate(terms, 0), mask, 0)
+    early = two_term_dot(jnp.concatenate(terms[:-2], 0), mask, 0)
+    late = two_term_dot(jnp.concatenate(terms[-2:], 0), mask, 0)
+    sums = jnp.concatenate([early, late], 0)
     picked = jnp.zeros((slots, wide), F32)
     for g in range(groups):
         picked = jnp.where(first == g * GROUP, sums[g * slots : (g + 1) * slots], picked)
@@ -257,7 +259,7 @@
     moved = []
     for group in grouped_fwd(far, 3):
         if len(group) == 1:
-            moved.append(rolled(own, group[0]))
+            moved.append(straight(own, group[0]))
         else:
             got = shared(own, group)
             moved += [got, swapped_sum(got, "stn")]

time: 23.6 us -> 23.4 us (level)
  waiting for transfers between devices: 6.36 us -> 5.87 us
  starting transfers between devices: 11.4 us -> 11.7 us
    ppermute x0 -> x1, starting transfers between devices: none -> 1.64 us  [straight(): lax.ppermute(x, 'tm', [(t, (t + by) % devices) for t in range(devices)])]
    ppermute x0 -> x1, waiting for transfers between devices: none -> 1.15 us  [straight(): lax.ppermute(x, 'tm', [(t, (t + by) % devices) for t in range(devices)])]
    ppermute x2 -> x1, waiting for transfers between devices: 2.44 us -> 1.5 us  [rolled(): return lax.ppermute(x, ('tm', 'stn'), pairs)]
    ppermute x2 -> x1, starting transfers between devices: 2.38 us -> 1.62 us  [rolled(): return lax.ppermute(x, ('tm', 'stn'), pairs)]
    ppermute x4, starting transfers between devices: 3.17 us -> 2.74 us  [swapped_sum(): lax.ppermute(x, axis, [(i, (i + by) % devices) for i in range(devices)])]
    ppermute x2, waiting for transfers between devices: 1.64 us -> 1.22 us  [shared(): return lax.ppermute(x, ('tm', 'stn'), pairs)]
    ppermute x4, waiting for transfers between devices: 2.28 us -> 2 us  [swapped_sum(): lax.ppermute(x, axis, [(i, (i + by) % devices) for i in range(devices)])]
  transfers between devices with their start and end apart: 8 -> 8, of which waited for: 6 -> 7; matrix products, arithmetic and copies ran while one was open for 0% -> 0% of each run, Pallas kernels for 3% -> 3%
where the time goes in v8:
time: 23.4 us; the launch traced here: 23.3 us
  starting transfers between devices  11.7 us (50%)
  waiting for transfers between devices  5.87 us (25%)
  Pallas kernels  3.39 us (14%)
  local copies, waits for them, and re-layouts  0.88 us (4%)
  between operations  0.75 us (3%)
  other arithmetic  0.66 us (3%)
    ppermute x2, starting transfers between devices, shared(): return lax.ppermute(x, ('tm', 'stn'), pairs)  5.69 us
    ppermute x4, starting transfers between devices, swapped_sum(): lax.ppermute(x, axis, [(i, (i + by) % devices) for i in range(devices)])  2.74 us
    ppermute x4, waiting for transfers between devices, swapped_sum(): lax.ppermute(x, axis, [(i, (i + by) % devices) for i in range(devices)])  2 us
    ppermute x1, starting transfers between devices, straight(): lax.ppermute(x, 'tm', [(t, (t + by) % devices) for t in range(devices)])  1.64 us
    ppermute x1, starting transfers between devices, rolled(): return lax.ppermute(x, ('tm', 'stn'), pairs)  1.62 us
    pallas_call x1, Pallas kernels, on_device(): pl.pallas_call(functools.partial(model_kernel, far), out_shape=[by_hour,...  1.53 us
    ppermute x1, waiting for transfers between devices, rolled(): return lax.ppermute(x, ('tm', 'stn'), pairs)  1.5 us
    ppermute x2, waiting for transfers between devices, shared(): return lax.ppermute(x, ('tm', 'stn'), pairs)  1.22 us
  transfers between devices with their start and end apart: 8, of which 7 were waited for; matrix products, arithmetic and copies ran while one was open for 0% of the time, Pallas kernels for 3%

profile of v8, /device:TPU:0, one launch (start us, length us, event | category | flops | bytes accessed | tf_op | source)
XLA Modules:
  0.0 23.3 jit_solution(1805691443548792022)
XLA Ops:
  0.6 0.0 copy-start.1
  0.6 0.8 %copy-done.1 = f32[16,1024]{1,0:T(8,128)S(1)} copy-done((f32[16,1024]{1,0:T(8,128)S(1)}, f32[16,1024]{1,0:T(8,128)}, u32[]{:S(2)}) %copy-start.1) | copy-done | bytes 65560
  1.5 0.0 copy-start.5
  1.5 0.0 copy-start.6
  1.5 0.0 copy-start.7
  1.5 0.0 copy-start.8
  1.6 3.5 %collective-permute-start = (bf16[16,1024]{1,0:T(8,128)(2,1)S(1)}, bf16[16,1024]{1,0:T(8,128)(2,1)S(1)}, u32[]{:S(2)}, u32[]{:S(2)}) collective-permute-start(bf16[16,1024]{1,0:T(8,128)(2,1)S(1)} %shard_map.96.refs_3_), channel_id=1, source_target_pairs={{1,4},{0,9},{5,8},{4,13},{9,12},{8,1},{13,0},{12,5},{3,6},{2,11},{... | collective-permute-start | bytes 98312 | tf_op jit(solution)/shard_map/ppermute | solution.py:43
  5.1 1.6 %collective-permute-start.2 = (bf16[16,1024]{1,0:T(8,128)(2,1)S(1)}, bf16[16,1024]{1,0:T(8,128)(2,1)S(1)}, u32[]{:S(2)}, u32[]{:S(2)}) collective-permute-start(bf16[16,1024]{1,0:T(8,128)(2,1)S(1)} %shard_map.96.refs_3_), channel_id=1, source_target_pairs={{0,12},{4,0},{8,4},{12,8},{1,13},{5,1},{9,5},{13,9},{2,14},{6,2},{... | collective-permute-start | bytes 98312 | tf_op jit(solution)/shard_map/ppermute | solution.py:23
  6.7 1.1 %collective-permute-done.refs_0_ = bf16[16,1024]{1,0:T(8,128)(2,1)S(1)} collective-permute-done((bf16[16,1024]{1,0:T(8,128)(2,1)S(1)}, bf16[16,1024]{1,0:T(8,128)(2,1)S(1)}, u32[]{:S(2)}, u32[]{:S(2)}) %collective-permute-start) | collective-permute-done | bytes 32800 | tf_op jit(solution)/shard_map/ppermute | solution.py:43
  7.9 1.1 %collective-permute-done.2.refs_2_ = bf16[16,1024]{1,0:T(8,128)(2,1)S(1)} collective-permute-done((bf16[16,1024]{1,0:T(8,128)(2,1)S(1)}, bf16[16,1024]{1,0:T(8,128)(2,1)S(1)}, u32[]{:S(2)}, u32[]{:S(2)}) %collective-permute-start.2) | collective-permute-done | bytes 32800 | tf_op jit(solution)/shard_map/ppermute | solution.py:23
  9.0 0.1 collective-permute-done.1.refs_1_
  9.1 1.5 %shard_map.97 = (f32[16,128]{1,0:T(8,128)S(1)}, f32[8,256]{1,0:T(8,128)S(1)}, bf16[256,128]{1,0:T(8,128)(2,1)S(1)}, s32[16,128]{1,0:T(8,128)S(1)}, f32[16,128]{1,0:T(8,128)S(1)}, /*index=5*/f32[16,128]{1,0:T(8,128)S(1)}) custom-call(bf16[16,1024]{1,0:T(8,128)(2,1)S(1)} %collective-permute-done.refs_0_, bf16[16,1024]{1,0:T(8,128)(2,1)S(1)} %collective-permute-done.1.refs_1_, ...), custom_call_target="tpu_custom_call" | custom-call | flops 268435456 | bytes 4194304 | tf_op jit(solution)/shard_map/pallas_call | solution.py:273
  10.6 1.9 %collective-permute-start.3 = (f32[16,128]{1,0:T(8,128)S(1)}, f32[16,128]{1,0:T(8,128)S(1)}, u32[]{:S(2)}, u32[]{:S(2)}) collective-permute-start(f32[16,128]{1,0:T(8,128)S(1)} %get-tuple-element.13.refs_0_), channel_id=1, source_target_pairs={{0,2},{2,0},{1,3},{3,1},{4,6},{6,4},{5,7},{7,5},{8,10},{10,8},{9,1... | collective-permute-start | bytes 24584 | tf_op jit(solution)/shard_map/ppermute | solution.py:327
  12.5 1.8 %collective-permute-done.3.refs_1_ = f32[16,128]{1,0:T(8,128)S(1)} collective-permute-done((f32[16,128]{1,0:T(8,128)S(1)}, f32[16,128]{1,0:T(8,128)S(1)}, u32[]{:S(2)}, u32[]{:S(2)}) %collective-permute-start.3) | collective-permute-done | bytes 8224 | tf_op jit(solution)/shard_map/ppermute | solution.py:327
  14.3 1.1 %shard_map.98 = (f32[16,128]{1,0:T(8,128)S(1)}, f32[16,1024]{1,0:T(8,128)S(1)}, f32[16,1024]{1,0:T(8,128)S(1)}, f32[16,1024]{1,0:T(8,128)S(1)}, bf16[16,1024]{1,0:T(8,128)(2,1)S(1)}) custom-call(f32[16,128]{1,0:T(8,128)S(1)} %get-tuple-element.13.refs_0_, f32[16,128]{1,0:T(8,128)S(1)} %collective-permute-done.3.refs_1_, ...), custom_call_target="tpu_custom_call" | custom-call | flops 268435456 | bytes 4194304 | tf_op jit(solution)/shard_map/pallas_call | solution.py:292
  15.4 0.1 collective-permute-start.5
  15.5 1.6 %collective-permute-start.4 = (bf16[16,1024]{1,0:T(8,128)(2,1)S(1)}, bf16[16,1024]{1,0:T(8,128)(2,1)S(1)}, u32[]{:S(2)}, u32[]{:S(2)}) collective-permute-start(bf16[16,1024]{1,0:T(8,128)(2,1)S(1)} %get-tuple-element.21), channel_id=1, source_target_pairs={{0,5},{1,4},{4,9},{5,8},{8,13},{9,12},{12,1},{13,0},{2,7},{3,6},{6... | collective-permute-start | bytes 98312 | tf_op jit(solution)/shard_map/ppermute | solution.py:18
  17.1 2.2 %collective-permute-start.6 = (bf16[16,1024]{1,0:T(8,128)(2,1)S(1)}, bf16[16,1024]{1,0:T(8,128)(2,1)S(1)}, u32[]{:S(2)}, u32[]{:S(2)}) collective-permute-start(bf16[16,1024]{1,0:T(8,128)(2,1)S(1)} %add_convert_fusion), channel_id=1, source_target_pairs={{1,12},{0,9},{5,0},{4,13},{9,4},{8,1},{13,8},{12,5},{3,14},{2,11},... | collective-permute-start | bytes 98312 | tf_op jit(solution)/shard_map/ppermute | solution.py:43
  19.3 1.5 %collective-permute-done.4 = bf16[16,1024]{1,0:T(8,128)(2,1)S(1)} collective-permute-done((bf16[16,1024]{1,0:T(8,128)(2,1)S(1)}, bf16[16,1024]{1,0:T(8,128)(2,1)S(1)}, u32[]{:S(2)}, u32[]{:S(2)}) %collective-permute-start.4) | collective-permute-done | bytes 32800 | tf_op jit(solution)/shard_map/ppermute | solution.py:18
  20.8 0.1 collective-permute-done.6
  20.9 0.8 %collective-permute-start.7 = (f32[16,1024]{1,0:T(8,128)S(1)}, f32[16,1024]{1,0:T(8,128)S(1)}, u32[]{:S(2)}, u32[]{:S(2)}) collective-permute-start(f32[16,1024]{1,0:T(8,128)S(1)} %convert_add_fusion), channel_id=1, source_target_pairs={{0,1},{1,0},{2,3},{3,2},{4,5},{5,4},{6,7},{7,6},{8,9},{9,8},{10,11... | collective-permute-start | bytes 196616 | tf_op jit(solution)/shard_map/ppermute | solution.py:327
  21.7 0.7 %shard_map.99 = f32[8,48]{1,0:T(8,128)} custom-call(f32[16,128]{1,0:T(8,128)S(1)} %get-tuple-element.19.slot_resid_ref), custom_call_target="tpu_custom_call" | custom-call | flops 1000000 | bytes 10000 | tf_op jit(solution)/shard_map/pallas_call | solution.py:310
  22.4 0.2 collective-permute-done.7
  22.6 0.6 %add.15 = f32[16,1024]{1,0:T(8,128)} add(f32[16,1024]{1,0:T(8,128)S(1)} %convert_add_fusion, f32[16,1024]{1,0:T(8,128)S(1)} %collective-permute-done.7) | non-fusion elementwise | flops 16384 | bytes 196608 | tf_op jit(solution)/shard_map/add | solution.py:319
  (18 shorter events, 0.1 us)
Async XLA Ops:
  0.6 0.8 %copy-start.1 = (f32[16,1024]{1,0:T(8,128)S(1)}, f32[16,1024]{1,0:T(8,128)}, u32[]{:S(2)}) copy-start(f32[16,1024]{1,0:T(8,128)} %refs_4_.3) | copy-start | bytes 196612
  1.5 7.6 %copy-start = (bf16[32,64,1024]{2,1,0:T(8,128)(2,1)S(1)}, bf16[32,64,1024]{2,1,0:T(8,128)(2,1)}, u32[]{:S(2)}) copy-start(bf16[32,64,1024]{2,1,0:T(8,128)(2,1)} %refs_6_.1) | copy-start | bytes 12582916
  1.5 7.6 %copy-start.4 = (f32[32,64]{1,0:T(8,128)S(1)}, f32[32,64]{1,0:T(8,128)}, u32[]{:S(2)}) copy-start(f32[32,64]{1,0:T(8,128)} %refs_5_.2) | copy-start | bytes 24580
  1.5 7.6 %copy-start.5 = (s32[48,8]{0,1:T(8,128)S(1)}, s32[48,8]{0,1:T(8,128)}, u32[]{:S(2)}) copy-start(s32[48,8]{0,1:T(8,128)} %param.12) | copy-start | bytes 4612
  1.5 7.6 %copy-start.6 = (f32[48,8]{0,1:T(8,128)S(1)}, f32[48,8]{0,1:T(8,128)}, u32[]{:S(2)}) copy-start(f32[48,8]{0,1:T(8,128)} %param.14) | copy-start | bytes 4612
  1.5 7.6 %copy-start.7 = (f32[48,8]{0,1:T(8,128)S(1)}, f32[48,8]{0,1:T(8,128)}, u32[]{:S(2)}) copy-start(f32[48,8]{0,1:T(8,128)} %param.15) | copy-start | bytes 4612
  1.5 7.6 %copy-start.8 = (s32[8]{0:T(128)S(1)}, s32[8]{0:T(128)}, u32[]{:S(2)}) copy-start(s32[8]{0:T(128)} %param.13) | copy-start | bytes 100
  1.5 12.8 %copy-start.2 = (f32[16,1024]{1,0:T(8,128)S(1)}, f32[16,1024]{1,0:T(8,128)}, u32[]{:S(2)}) copy-start(f32[16,1024]{1,0:T(8,128)} %refs_4_.3) | copy-start | bytes 196612
  1.6 12.7 %copy-start.3 = (f32[16,1024]{1,0:T(8,128)S(1)}, f32[16,1024]{1,0:T(8,128)}, u32[]{:S(2)}) copy-start(f32[16,1024]{1,0:T(8,128)} %refs_5_.3) | copy-start | bytes 196612
  1.6 6.3 %collective-permute-start = (bf16[16,1024]{1,0:T(8,128)(2,1)S(1)}, bf16[16,1024]{1,0:T(8,128)(2,1)S(1)}, u32[]{:S(2)}, u32[]{:S(2)}) collective-permute-start(bf16[16,1024]{1,0:T(8,128)(2,1)S(1)} %shard_map.96.refs_3_), channel_id=1, source_target_pairs={{1,4},{0,9},{5,8},{4,13},{9,12},{8,1},{13,0},{12,5},{3,6},{2,11},{... | collective-permute-start | bytes 98312 | tf_op jit(solution)/shard_map/ppermute | solution.py:43
  5.1 3.9 %collective-permute-start.2 = (bf16[16,1024]{1,0:T(8,128)(2,1)S(1)}, bf16[16,1024]{1,0:T(8,128)(2,1)S(1)}, u32[]{:S(2)}, u32[]{:S(2)}) collective-permute-start(bf16[16,1024]{1,0:T(8,128)(2,1)S(1)} %shard_map.96.refs_3_), channel_id=1, source_target_pairs={{0,12},{4,0},{8,4},{12,8},{1,13},{5,1},{9,5},{13,9},{2,14},{6,2},{... | collective-permute-start | bytes 98312 | tf_op jit(solution)/shard_map/ppermute | solution.py:23
  7.9 1.2 %collective-permute-start.1 = (bf16[16,1024]{1,0:T(8,128)(2,1)S(1)}, bf16[16,1024]{1,0:T(8,128)(2,1)S(1)}, u32[]{:S(2)}, u32[]{:S(2)}) collective-permute-start(bf16[16,1024]{1,0:T(8,128)(2,1)S(1)} %collective-permute-done.refs_0_), channel_id=1, source_target_pairs={{0,1},{1,0},{2,3},{3,2},{4,5},{5,4},{6,7},{7,6},{8,9},{9,8},{10,11... | collective-permute-start | bytes 98312 | tf_op jit(solution)/shard_map/ppermute | solution.py:327
  10.6 3.7 %collective-permute-start.3 = (f32[16,128]{1,0:T(8,128)S(1)}, f32[16,128]{1,0:T(8,128)S(1)}, u32[]{:S(2)}, u32[]{:S(2)}) collective-permute-start(f32[16,128]{1,0:T(8,128)S(1)} %get-tuple-element.13.refs_0_), channel_id=1, source_target_pairs={{0,2},{2,0},{1,3},{3,1},{4,6},{6,4},{5,7},{7,5},{8,10},{10,8},{9,1... | collective-permute-start | bytes 24584 | tf_op jit(solution)/shard_map/ppermute | solution.py:327
  15.4 1.7 %collective-permute-start.5 = (f32[16,1024]{1,0:T(8,128)S(1)}, f32[16,1024]{1,0:T(8,128)S(1)}, u32[]{:S(2)}, u32[]{:S(2)}) collective-permute-start(f32[16,1024]{1,0:T(8,128)S(1)} %get-tuple-element.23), channel_id=1, source_target_pairs={{0,1},{1,0},{2,3},{3,2},{4,5},{5,4},{6,7},{7,6},{8,9},{9,8},{10,11... | collective-permute-start | bytes 196616 | tf_op jit(solution)/shard_map/ppermute | solution.py:327
  15.5 5.3 %collective-permute-start.4 = (bf16[16,1024]{1,0:T(8,128)(2,1)S(1)}, bf16[16,1024]{1,0:T(8,128)(2,1)S(1)}, u32[]{:S(2)}, u32[]{:S(2)}) collective-permute-start(bf16[16,1024]{1,0:T(8,128)(2,1)S(1)} %get-tuple-element.21), channel_id=1, source_target_pairs={{0,5},{1,4},{4,9},{5,8},{8,13},{9,12},{12,1},{13,0},{2,7},{3,6},{6... | collective-permute-start | bytes 98312 | tf_op jit(solution)/shard_map/ppermute | solution.py:18
  17.1 3.8 %collective-permute-start.6 = (bf16[16,1024]{1,0:T(8,128)(2,1)S(1)}, bf16[16,1024]{1,0:T(8,128)(2,1)S(1)}, u32[]{:S(2)}, u32[]{:S(2)}) collective-permute-start(bf16[16,1024]{1,0:T(8,128)(2,1)S(1)} %add_convert_fusion), channel_id=1, source_target_pairs={{1,12},{0,9},{5,0},{4,13},{9,4},{8,1},{13,8},{12,5},{3,14},{2,11},... | collective-permute-start | bytes 98312 | tf_op jit(solution)/shard_map/ppermute | solution.py:43
  20.9 1.7 %collective-permute-start.7 = (f32[16,1024]{1,0:T(8,128)S(1)}, f32[16,1024]{1,0:T(8,128)S(1)}, u32[]{:S(2)}, u32[]{:S(2)}) collective-permute-start(f32[16,1024]{1,0:T(8,128)S(1)} %convert_add_fusion), channel_id=1, source_target_pairs={{0,1},{1,0},{2,3},{3,2},{4,5},{5,4},{6,7},{7,6},{8,9},{9,8},{10,11... | collective-permute-start | bytes 196616 | tf_op jit(solution)/shard_map/ppermute | solution.py:327

commit v9 on v8

--- a/solution.py
+++ b/solution.py
@@ -107,8 +107,21 @@
     return x[x.shape[0] - rows :]
 
 
-def round_kernel(flux_ref, out_ref):
-    out_ref[...] = flux_ref[...].astype(out_ref.dtype)
+def fetch_kernel(flux_hbm, out_ref, flux_ref, sems):
+    part = flux_ref.shape[1] // 4
+    at = [(slice(None), pl.ds(i * part, part)) for i in range(4)]
+    copies = [
+        pltpu.make_async_copy(flux_hbm.at[at[i]], flux_ref.at[at[i]], sems.at[i]) for i in range(4)
+    ]
+    for copy in copies:
+        copy.start()
+    for i, copy in enumerate(copies):
+        copy.wait()
+        out_ref[at[i]] = flux_ref[at[i]].astype(out_ref.dtype)
+
+
+def pass_kernel(in_ref, out_ref):
+    out_ref[...] = in_ref[...]
 
 
 def model_kernel(far, *refs):
@@ -158,7 +171,7 @@
     terms = []
     for g in range(groups):
         table = table_ref[g * GROUP : (g + 1) * GROUP].reshape(GROUP * lags, cells)
-        if g < groups - 1:
+        if g < groups - 3:
             products = lax.dot_general(
                 table, window, (((1,), (1,)), ((), ())), preferred_element_type=F32
             ).T
@@ -167,8 +180,8 @@
                 window, table, (((1,), (1,)), ((), ())), preferred_element_type=F32
             )
         terms.append(skew_down(products, lags, slots) * scale[g : g + 1])
-    early = two_term_dot(jnp.concatenate(terms[:-2], 0), mask, 0)
-    late = two_term_dot(jnp.concatenate(terms[-2:], 0), mask, 0)
+    early = two_term_dot(jnp.concatenate(terms[:-4], 0), mask, 0)
+    late = two_term_dot(jnp.concatenate(terms[-4:], 0), mask, 0)
     sums = jnp.concatenate([early, late], 0)
     picked = jnp.zeros((slots, wide), F32)
     for g in range(groups):
@@ -246,16 +259,25 @@
     hours, stations = block_index.shape
     far = min(lags // slots, lax.axis_size("tm") - 1)
     rows = slots * (far + 1)
-    own = fluxes
-    for flops in (10**4, 2 * 10**10):
-        own = pl.pallas_call(
-            round_kernel,
-            out_shape=jax.ShapeDtypeStruct((slots, cells), BF16),
-            in_specs=[VMEM],
-            out_specs=VMEM,
-            compiler_params=pltpu.CompilerParams(vmem_limit_bytes=2 * 1024 * 1024),
-            cost_estimate=pl.CostEstimate(flops=flops, bytes_accessed=10**5, transcendentals=0),
-        )(own)
+    half = jax.ShapeDtypeStruct((slots, cells), BF16)
+    small = pltpu.CompilerParams(vmem_limit_bytes=2 * 1024 * 1024)
+    own = pl.pallas_call(
+        fetch_kernel,
+        out_shape=half,
+        in_specs=[pl.BlockSpec(memory_space=pltpu.HBM)],
+        out_specs=VMEM,
+        scratch_shapes=[pltpu.VMEM((slots, cells), F32), pltpu.SemaphoreType.DMA((4,))],
+        compiler_params=small,
+        cost_estimate=pl.CostEstimate(flops=10**4, bytes_accessed=10**5, transcendentals=0),
+    )(pltpu.with_memory_space_constraint(fluxes, pltpu.HBM))
+    own = pl.pallas_call(
+        pass_kernel,
+        out_shape=half,
+        in_specs=[VMEM],
+        out_specs=VMEM,
+        compiler_params=small,
+        cost_estimate=pl.CostEstimate(flops=2 * 10**10, bytes_accessed=10**5, transcendentals=0),
+    )(own)
     moved = []
     for group in grouped_fwd(far, 3):
         if len(group) == 1:

time: 23.4 us -> 23.4 us (level)
  local copies, waits for them, and re-layouts: 0.88 us -> 0.05 us
  Pallas kernels: 3.39 us -> 4.16 us
    unnamed x18 -> x16, local copies, waits for them, and re-layouts: 0.88 us -> 0.05 us
    pallas_call x2, Pallas kernels: 0.01 us -> 0.81 us  [the longest x1 0.81 us: on_device(): pl.pallas_call(fetch_kernel, out_shape=half, in_specs=[pl.BlockSpec(memor...]
where the time goes in v9:
time: 23.4 us; the launch traced here: 23.2 us
  starting transfers between devices  11.7 us (50%)
  waiting for transfers between devices  5.87 us (25%)
  Pallas kernels  4.16 us (18%)
  between operations  0.76 us (3%)
  other arithmetic  0.66 us (3%)
    ppermute x2, starting transfers between devices, shared(): return lax.ppermute(x, ('tm', 'stn'), pairs)  5.68 us
    ppermute x4, starting transfers between devices, swapped_sum(): lax.ppermute(x, axis, [(i, (i + by) % devices) for i in range(devices)])  2.76 us
    ppermute x4, waiting for transfers between devices, swapped_sum(): lax.ppermute(x, axis, [(i, (i + by) % devices) for i in range(devices)])  2 us
    ppermute x1, starting transfers between devices, straight(): lax.ppermute(x, 'tm', [(t, (t + by) % devices) for t in range(devices)])  1.64 us
    ppermute x1, starting transfers between devices, rolled(): return lax.ppermute(x, ('tm', 'stn'), pairs)  1.62 us
    ppermute x1, waiting for transfers between devices, rolled(): return lax.ppermute(x, ('tm', 'stn'), pairs)  1.51 us
    pallas_call x1, Pallas kernels, on_device(): pl.pallas_call(functools.partial(model_kernel, far), out_shape=[by_hour,...  1.49 us
    ppermute x2, waiting for transfers between devices, shared(): return lax.ppermute(x, ('tm', 'stn'), pairs)  1.21 us
  transfers between devices with their start and end apart: 8, of which 7 were waited for; matrix products, arithmetic and copies ran while one was open for 0% of the time, Pallas kernels for 3%

profile of v9, /device:TPU:0, one launch (start us, length us, event | category | flops | bytes accessed | tf_op | source)
XLA Modules:
  0.0 23.2 jit_solution(5179086883230339515)
XLA Ops:
  0.6 0.8 %shard_map.95.in_ref = bf16[16,1024]{1,0:T(8,128)(2,1)S(1)} custom-call(f32[16,1024]{1,0:T(8,128)} %refs_4_.3), custom_call_target="tpu_custom_call" | custom-call | flops 10000 | bytes 100000 | tf_op jit(solution)/shard_map/pallas_call | solution.py:264
  1.4 0.0 copy-start
  1.5 0.0 copy-start.3
  1.5 0.0 copy-start.4
  1.5 0.0 copy-start.5
  1.5 0.0 copy-start.1
  1.6 3.5 %collective-permute-start = (bf16[16,1024]{1,0:T(8,128)(2,1)S(1)}, bf16[16,1024]{1,0:T(8,128)(2,1)S(1)}, u32[]{:S(2)}, u32[]{:S(2)}) collective-permute-start(bf16[16,1024]{1,0:T(8,128)(2,1)S(1)} %shard_map.96.refs_3_), channel_id=1, source_target_pairs={{1,4},{0,9},{5,8},{4,13},{9,12},{8,1},{13,0},{12,5},{3,6},{2,11},{... | collective-permute-start | bytes 98312 | tf_op jit(solution)/shard_map/ppermute | solution.py:43
  5.1 1.6 %collective-permute-start.2 = (bf16[16,1024]{1,0:T(8,128)(2,1)S(1)}, bf16[16,1024]{1,0:T(8,128)(2,1)S(1)}, u32[]{:S(2)}, u32[]{:S(2)}) collective-permute-start(bf16[16,1024]{1,0:T(8,128)(2,1)S(1)} %shard_map.96.refs_3_), channel_id=1, source_target_pairs={{0,12},{4,0},{8,4},{12,8},{1,13},{5,1},{9,5},{13,9},{2,14},{6,2},{... | collective-permute-start | bytes 98312 | tf_op jit(solution)/shard_map/ppermute | solution.py:23
  6.7 1.1 %collective-permute-done.refs_0_ = bf16[16,1024]{1,0:T(8,128)(2,1)S(1)} collective-permute-done((bf16[16,1024]{1,0:T(8,128)(2,1)S(1)}, bf16[16,1024]{1,0:T(8,128)(2,1)S(1)}, u32[]{:S(2)}, u32[]{:S(2)}) %collective-permute-start) | collective-permute-done | bytes 32800 | tf_op jit(solution)/shard_map/ppermute | solution.py:43
  7.8 1.1 %collective-permute-done.2.refs_2_ = bf16[16,1024]{1,0:T(8,128)(2,1)S(1)} collective-permute-done((bf16[16,1024]{1,0:T(8,128)(2,1)S(1)}, bf16[16,1024]{1,0:T(8,128)(2,1)S(1)}, u32[]{:S(2)}, u32[]{:S(2)}) %collective-permute-start.2) | collective-permute-done | bytes 32800 | tf_op jit(solution)/shard_map/ppermute | solution.py:23
  9.0 0.1 collective-permute-done.1.refs_1_
  9.1 1.5 %shard_map.97 = (f32[16,128]{1,0:T(8,128)S(1)}, f32[8,256]{1,0:T(8,128)S(1)}, bf16[256,128]{1,0:T(8,128)(2,1)S(1)}, s32[16,128]{1,0:T(8,128)S(1)}, f32[16,128]{1,0:T(8,128)S(1)}, /*index=5*/f32[16,128]{1,0:T(8,128)S(1)}) custom-call(bf16[16,1024]{1,0:T(8,128)(2,1)S(1)} %collective-permute-done.refs_0_, bf16[16,1024]{1,0:T(8,128)(2,1)S(1)} %collective-permute-done.1.refs_1_, ...), custom_call_target="tpu_custom_call" | custom-call | flops 268435456 | bytes 4194304 | tf_op jit(solution)/shard_map/pallas_call | solution.py:295
  10.6 1.9 %collective-permute-start.3 = (f32[16,128]{1,0:T(8,128)S(1)}, f32[16,128]{1,0:T(8,128)S(1)}, u32[]{:S(2)}, u32[]{:S(2)}) collective-permute-start(f32[16,128]{1,0:T(8,128)S(1)} %get-tuple-element.13.refs_0_), channel_id=1, source_target_pairs={{0,2},{2,0},{1,3},{3,1},{4,6},{6,4},{5,7},{7,5},{8,10},{10,8},{9,1... | collective-permute-start | bytes 24584 | tf_op jit(solution)/shard_map/ppermute | solution.py:349
  12.5 1.8 %collective-permute-done.3.refs_1_ = f32[16,128]{1,0:T(8,128)S(1)} collective-permute-done((f32[16,128]{1,0:T(8,128)S(1)}, f32[16,128]{1,0:T(8,128)S(1)}, u32[]{:S(2)}, u32[]{:S(2)}) %collective-permute-start.3) | collective-permute-done | bytes 8224 | tf_op jit(solution)/shard_map/ppermute | solution.py:349
  14.2 1.1 %shard_map.98 = (f32[16,128]{1,0:T(8,128)S(1)}, f32[16,1024]{1,0:T(8,128)S(1)}, f32[16,1024]{1,0:T(8,128)S(1)}, f32[16,1024]{1,0:T(8,128)S(1)}, bf16[16,1024]{1,0:T(8,128)(2,1)S(1)}) custom-call(f32[16,128]{1,0:T(8,128)S(1)} %get-tuple-element.13.refs_0_, f32[16,128]{1,0:T(8,128)S(1)} %collective-permute-done.3.refs_1_, ...), custom_call_target="tpu_custom_call" | custom-call | flops 268435456 | bytes 4194304 | tf_op jit(solution)/shard_map/pallas_call | solution.py:314
  15.4 0.1 collective-permute-start.5
  15.4 1.6 %collective-permute-start.4 = (bf16[16,1024]{1,0:T(8,128)(2,1)S(1)}, bf16[16,1024]{1,0:T(8,128)(2,1)S(1)}, u32[]{:S(2)}, u32[]{:S(2)}) collective-permute-start(bf16[16,1024]{1,0:T(8,128)(2,1)S(1)} %get-tuple-element.21), channel_id=1, source_target_pairs={{0,5},{1,4},{4,9},{5,8},{8,13},{9,12},{12,1},{13,0},{2,7},{3,6},{6... | collective-permute-start | bytes 98312 | tf_op jit(solution)/shard_map/ppermute | solution.py:18
  17.1 2.2 %collective-permute-start.6 = (bf16[16,1024]{1,0:T(8,128)(2,1)S(1)}, bf16[16,1024]{1,0:T(8,128)(2,1)S(1)}, u32[]{:S(2)}, u32[]{:S(2)}) collective-permute-start(bf16[16,1024]{1,0:T(8,128)(2,1)S(1)} %add_convert_fusion), channel_id=1, source_target_pairs={{1,12},{0,9},{5,0},{4,13},{9,4},{8,1},{13,8},{12,5},{3,14},{2,11},... | collective-permute-start | bytes 98312 | tf_op jit(solution)/shard_map/ppermute | solution.py:43
  19.2 1.5 %collective-permute-done.4 = bf16[16,1024]{1,0:T(8,128)(2,1)S(1)} collective-permute-done((bf16[16,1024]{1,0:T(8,128)(2,1)S(1)}, bf16[16,1024]{1,0:T(8,128)(2,1)S(1)}, u32[]{:S(2)}, u32[]{:S(2)}) %collective-permute-start.4) | collective-permute-done | bytes 32800 | tf_op jit(solution)/shard_map/ppermute | solution.py:18
  20.7 0.1 collective-permute-done.6
  20.9 0.8 %collective-permute-start.7 = (f32[16,1024]{1,0:T(8,128)S(1)}, f32[16,1024]{1,0:T(8,128)S(1)}, u32[]{:S(2)}, u32[]{:S(2)}) collective-permute-start(f32[16,1024]{1,0:T(8,128)S(1)} %convert_add_fusion), channel_id=1, source_target_pairs={{0,1},{1,0},{2,3},{3,2},{4,5},{5,4},{6,7},{7,6},{8,9},{9,8},{10,11... | collective-permute-start | bytes 196616 | tf_op jit(solution)/shard_map/ppermute | solution.py:349
  21.7 0.7 %shard_map.99 = f32[8,48]{1,0:T(8,128)} custom-call(f32[16,128]{1,0:T(8,128)S(1)} %get-tuple-element.19.slot_resid_ref), custom_call_target="tpu_custom_call" | custom-call | flops 1000000 | bytes 10000 | tf_op jit(solution)/shard_map/pallas_call | solution.py:332
  22.4 0.2 collective-permute-done.7
  22.6 0.6 %add.15 = f32[16,1024]{1,0:T(8,128)} add(f32[16,1024]{1,0:T(8,128)S(1)} %convert_add_fusion, f32[16,1024]{1,0:T(8,128)S(1)} %collective-permute-done.7) | non-fusion elementwise | flops 16384 | bytes 196608 | tf_op jit(solution)/shard_map/add | solution.py:341
  (16 shorter events, 0.1 us)
Async XLA Ops:
  1.4 7.6 %copy-start = (bf16[32,64,1024]{2,1,0:T(8,128)(2,1)S(1)}, bf16[32,64,1024]{2,1,0:T(8,128)(2,1)}, u32[]{:S(2)}) copy-start(bf16[32,64,1024]{2,1,0:T(8,128)(2,1)} %refs_6_.1) | copy-start | bytes 12582916
  1.5 7.6 %copy-start.3 = (f32[32,64]{1,0:T(8,128)S(1)}, f32[32,64]{1,0:T(8,128)}, u32[]{:S(2)}) copy-start(f32[32,64]{1,0:T(8,128)} %refs_5_.2) | copy-start | bytes 24580
  1.5 7.6 %copy-start.4 = (s32[48,8]{0,1:T(8,128)S(1)}, s32[48,8]{0,1:T(8,128)}, u32[]{:S(2)}) copy-start(s32[48,8]{0,1:T(8,128)} %param.12) | copy-start | bytes 4612
  1.5 7.6 %copy-start.5 = (f32[48,8]{0,1:T(8,128)S(1)}, f32[48,8]{0,1:T(8,128)}, u32[]{:S(2)}) copy-start(f32[48,8]{0,1:T(8,128)} %param.14) | copy-start | bytes 4612
  1.5 7.6 %copy-start.6 = (f32[48,8]{0,1:T(8,128)S(1)}, f32[48,8]{0,1:T(8,128)}, u32[]{:S(2)}) copy-start(f32[48,8]{0,1:T(8,128)} %param.15) | copy-start | bytes 4612
  1.5 7.6 %copy-start.7 = (s32[8]{0:T(128)S(1)}, s32[8]{0:T(128)}, u32[]{:S(2)}) copy-start(s32[8]{0:T(128)} %param.13) | copy-start | bytes 100
  1.5 12.7 %copy-start.1 = (f32[16,1024]{1,0:T(8,128)S(1)}, f32[16,1024]{1,0:T(8,128)}, u32[]{:S(2)}) copy-start(f32[16,1024]{1,0:T(8,128)} %refs_4_.3) | copy-start | bytes 196612
  1.5 12.7 %copy-start.2 = (f32[16,1024]{1,0:T(8,128)S(1)}, f32[16,1024]{1,0:T(8,128)}, u32[]{:S(2)}) copy-start(f32[16,1024]{1,0:T(8,128)} %refs_5_.3) | copy-start | bytes 196612
  1.6 6.3 %collective-permute-start = (bf16[16,1024]{1,0:T(8,128)(2,1)S(1)}, bf16[16,1024]{1,0:T(8,128)(2,1)S(1)}, u32[]{:S(2)}, u32[]{:S(2)}) collective-permute-start(bf16[16,1024]{1,0:T(8,128)(2,1)S(1)} %shard_map.96.refs_3_), channel_id=1, source_target_pairs={{1,4},{0,9},{5,8},{4,13},{9,12},{8,1},{13,0},{12,5},{3,6},{2,11},{... | collective-permute-start | bytes 98312 | tf_op jit(solution)/shard_map/ppermute | solution.py:43
  5.1 3.9 %collective-permute-start.2 = (bf16[16,1024]{1,0:T(8,128)(2,1)S(1)}, bf16[16,1024]{1,0:T(8,128)(2,1)S(1)}, u32[]{:S(2)}, u32[]{:S(2)}) collective-permute-start(bf16[16,1024]{1,0:T(8,128)(2,1)S(1)} %shard_map.96.refs_3_), channel_id=1, source_target_pairs={{0,12},{4,0},{8,4},{12,8},{1,13},{5,1},{9,5},{13,9},{2,14},{6,2},{... | collective-permute-start | bytes 98312 | tf_op jit(solution)/shard_map/ppermute | solution.py:23
  7.8 1.2 %collective-permute-start.1 = (bf16[16,1024]{1,0:T(8,128)(2,1)S(1)}, bf16[16,1024]{1,0:T(8,128)(2,1)S(1)}, u32[]{:S(2)}, u32[]{:S(2)}) collective-permute-start(bf16[16,1024]{1,0:T(8,128)(2,1)S(1)} %collective-permute-done.refs_0_), channel_id=1, source_target_pairs={{0,1},{1,0},{2,3},{3,2},{4,5},{5,4},{6,7},{7,6},{8,9},{9,8},{10,11... | collective-permute-start | bytes 98312 | tf_op jit(solution)/shard_map/ppermute | solution.py:349
  10.6 3.7 %collective-permute-start.3 = (f32[16,128]{1,0:T(8,128)S(1)}, f32[16,128]{1,0:T(8,128)S(1)}, u32[]{:S(2)}, u32[]{:S(2)}) collective-permute-start(f32[16,128]{1,0:T(8,128)S(1)} %get-tuple-element.13.refs_0_), channel_id=1, source_target_pairs={{0,2},{2,0},{1,3},{3,1},{4,6},{6,4},{5,7},{7,5},{8,10},{10,8},{9,1... | collective-permute-start | bytes 24584 | tf_op jit(solution)/shard_map/ppermute | solution.py:349
  15.4 1.7 %collective-permute-start.5 = (f32[16,1024]{1,0:T(8,128)S(1)}, f32[16,1024]{1,0:T(8,128)S(1)}, u32[]{:S(2)}, u32[]{:S(2)}) collective-permute-start(f32[16,1024]{1,0:T(8,128)S(1)} %get-tuple-element.23), channel_id=1, source_target_pairs={{0,1},{1,0},{2,3},{3,2},{4,5},{5,4},{6,7},{7,6},{8,9},{9,8},{10,11... | collective-permute-start | bytes 196616 | tf_op jit(solution)/shard_map/ppermute | solution.py:349
  15.4 5.3 %collective-permute-start.4 = (bf16[16,1024]{1,0:T(8,128)(2,1)S(1)}, bf16[16,1024]{1,0:T(8,128)(2,1)S(1)}, u32[]{:S(2)}, u32[]{:S(2)}) collective-permute-start(bf16[16,1024]{1,0:T(8,128)(2,1)S(1)} %get-tuple-element.21), channel_id=1, source_target_pairs={{0,5},{1,4},{4,9},{5,8},{8,13},{9,12},{12,1},{13,0},{2,7},{3,6},{6... | collective-permute-start | bytes 98312 | tf_op jit(solution)/shard_map/ppermute | solution.py:18
  17.1 3.8 %collective-permute-start.6 = (bf16[16,1024]{1,0:T(8,128)(2,1)S(1)}, bf16[16,1024]{1,0:T(8,128)(2,1)S(1)}, u32[]{:S(2)}, u32[]{:S(2)}) collective-permute-start(bf16[16,1024]{1,0:T(8,128)(2,1)S(1)} %add_convert_fusion), channel_id=1, source_target_pairs={{1,12},{0,9},{5,0},{4,13},{9,4},{8,1},{13,8},{12,5},{3,14},{2,11},... | collective-permute-start | bytes 98312 | tf_op jit(solution)/shard_map/ppermute | solution.py:43
  20.9 1.7 %collective-permute-start.7 = (f32[16,1024]{1,0:T(8,128)S(1)}, f32[16,1024]{1,0:T(8,128)S(1)}, u32[]{:S(2)}, u32[]{:S(2)}) collective-permute-start(f32[16,1024]{1,0:T(8,128)S(1)} %convert_add_fusion), channel_id=1, source_target_pairs={{0,1},{1,0},{2,3},{3,2},{4,5},{5,4},{6,7},{7,6},{8,9},{9,8},{10,11... | collective-permute-start | bytes 196616 | tf_op jit(solution)/shard_map/ppermute | solution.py:349

commit v10 on v9

--- a/solution.py
+++ b/solution.py
@@ -193,7 +193,7 @@
 
 
 def return_kernel(per, stations, *refs):
-    (mine_ref, other_ref, seen_ref, weight_ref, flux_ref, prior_ref, table_ref, scale_ref,
+    (mine_ref, other_ref, seen_ref, weight_ref, table_ref, scale_ref,
      mask_ref, first_ref, resid_ref, own_ref, *rest) = refs
     *sent_refs, spread_ref = rest
     blocks, lags, cells = table_ref.shape
@@ -220,7 +220,7 @@
         spread_ref[:, g * GROUP * lags : (g + 1) * GROUP * lags] = spread
     table = table_ref[...].reshape(blocks * lags, cells)
     returned = jnp.dot(spread_ref[...], table, preferred_element_type=F32)
-    own_ref[...] = returned[rows - slots :] + 0.5 * prior_ref[...] * flux_ref[...]
+    own_ref[...] = returned[rows - slots :]
     core = lax.axis_index("stn")
     near = []
     for distance in range(1, rows // slots):
@@ -314,12 +314,12 @@
     resid, total, *back = pl.pallas_call(
         functools.partial(return_kernel, per, stations),
         out_shape=[by_hour, piece] + [piece] * (far // 2 * 2) + [sent] * (far % 2),
-        in_specs=[VMEM] * 10,
+        in_specs=[VMEM] * 8,
         out_specs=[VMEM] * (2 + far),
         scratch_shapes=[pltpu.VMEM((rows, blocks * lags), BF16)],
         compiler_params=PARAMS,
         cost_estimate=cost,
-    )(mine, other, seen, weight, fluxes, prior_weight, footprint, scale, mask, first)
+    )(mine, other, seen, weight, footprint, scale, mask, first)
     arrived = []
     for group in grouped_fwd(far, 3):
         if len(group) == 1:
@@ -327,6 +327,7 @@
         else:
             both = back.pop(0) + swapped_sum(back.pop(0), "stn")
             arrived.append(shared(both.astype(BF16), [-d for d in group]))
+    total = total + 0.5 * prior_weight * fluxes
     for piece in arrived[::-1]:
         total = total + piece
     resid = pl.pallas_call(

time: 23.4 us -> 23.4 us (level)
  no operation moved by 1% of the time
where the time goes in v10:
time: 23.4 us; the launch traced here: 23.2 us
  starting transfers between devices  11.7 us (50%)
  waiting for transfers between devices  5.87 us (25%)
  Pallas kernels  4.14 us (18%)
  between operations  0.76 us (3%)
  other arithmetic  0.67 us (3%)
    ppermute x2, starting transfers between devices, shared(): return lax.ppermute(x, ('tm', 'stn'), pairs)  5.68 us
    ppermute x4, starting transfers between devices, swapped_sum(): lax.ppermute(x, axis, [(i, (i + by) % devices) for i in range(devices)])  2.76 us
    ppermute x4, waiting for transfers between devices, swapped_sum(): lax.ppermute(x, axis, [(i, (i + by) % devices) for i in range(devices)])  2 us
    ppermute x1, starting transfers between devices, straight(): lax.ppermute(x, 'tm', [(t, (t + by) % devices) for t in range(devices)])  1.64 us
    ppermute x1, starting transfers between devices, rolled(): return lax.ppermute(x, ('tm', 'stn'), pairs)  1.62 us
    ppermute x1, waiting for transfers between devices, rolled(): return lax.ppermute(x, ('tm', 'stn'), pairs)  1.51 us
    pallas_call x1, Pallas kernels, on_device(): pl.pallas_call(functools.partial(model_kernel, far), out_shape=[by_hour,...  1.49 us
    ppermute x2, waiting for transfers between devices, shared(): return lax.ppermute(x, ('tm', 'stn'), pairs)  1.21 us
  transfers between devices with their start and end apart: 8, of which 7 were waited for; matrix products, arithmetic and copies ran while one was open for 0% of the time, Pallas kernels for 3%

profile of v10, /device:TPU:0, one launch (start us, length us, event | category | flops | bytes accessed | tf_op | source)
XLA Modules:
  0.0 23.2 jit_solution(9388917606945709841)
XLA Ops:
  0.6 0.8 %shard_map.95.in_ref = bf16[16,1024]{1,0:T(8,128)(2,1)S(1)} custom-call(f32[16,1024]{1,0:T(8,128)} %flux_hbm.1), custom_call_target="tpu_custom_call" | custom-call | flops 10000 | bytes 100000 | tf_op jit(solution)/shard_map/pallas_call | solution.py:264
  1.4 0.0 copy-start
  1.5 0.0 copy-start.1
  1.5 0.0 copy-start.2
  1.5 0.0 copy-start.3
  1.5 0.0 copy-start.5
  1.5 3.5 %collective-permute-start = (bf16[16,1024]{1,0:T(8,128)(2,1)S(1)}, bf16[16,1024]{1,0:T(8,128)(2,1)S(1)}, u32[]{:S(2)}, u32[]{:S(2)}) collective-permute-start(bf16[16,1024]{1,0:T(8,128)(2,1)S(1)} %shard_map.96.refs_3_), channel_id=1, source_target_pairs={{1,4},{0,9},{5,8},{4,13},{9,12},{8,1},{13,0},{12,5},{3,6},{2,11},{... | collective-permute-start | bytes 98312 | tf_op jit(solution)/shard_map/ppermute | solution.py:43
  5.1 1.6 %collective-permute-start.2 = (bf16[16,1024]{1,0:T(8,128)(2,1)S(1)}, bf16[16,1024]{1,0:T(8,128)(2,1)S(1)}, u32[]{:S(2)}, u32[]{:S(2)}) collective-permute-start(bf16[16,1024]{1,0:T(8,128)(2,1)S(1)} %shard_map.96.refs_3_), channel_id=1, source_target_pairs={{0,12},{4,0},{8,4},{12,8},{1,13},{5,1},{9,5},{13,9},{2,14},{6,2},{... | collective-permute-start | bytes 98312 | tf_op jit(solution)/shard_map/ppermute | solution.py:23
  6.7 1.1 %collective-permute-done.refs_0_ = bf16[16,1024]{1,0:T(8,128)(2,1)S(1)} collective-permute-done((bf16[16,1024]{1,0:T(8,128)(2,1)S(1)}, bf16[16,1024]{1,0:T(8,128)(2,1)S(1)}, u32[]{:S(2)}, u32[]{:S(2)}) %collective-permute-start) | collective-permute-done | bytes 32800 | tf_op jit(solution)/shard_map/ppermute | solution.py:43
  7.8 1.1 %collective-permute-done.2.refs_2_ = bf16[16,1024]{1,0:T(8,128)(2,1)S(1)} collective-permute-done((bf16[16,1024]{1,0:T(8,128)(2,1)S(1)}, bf16[16,1024]{1,0:T(8,128)(2,1)S(1)}, u32[]{:S(2)}, u32[]{:S(2)}) %collective-permute-start.2) | collective-permute-done | bytes 32800 | tf_op jit(solution)/shard_map/ppermute | solution.py:23
  9.0 0.1 collective-permute-done.1.refs_1_
  9.1 1.5 %shard_map.97 = (f32[16,128]{1,0:T(8,128)S(1)}, f32[8,256]{1,0:T(8,128)S(1)}, bf16[256,128]{1,0:T(8,128)(2,1)S(1)}, s32[16,128]{1,0:T(8,128)S(1)}, f32[16,128]{1,0:T(8,128)S(1)}, /*index=5*/f32[16,128]{1,0:T(8,128)S(1)}) custom-call(bf16[16,1024]{1,0:T(8,128)(2,1)S(1)} %collective-permute-done.refs_0_, bf16[16,1024]{1,0:T(8,128)(2,1)S(1)} %collective-permute-done.1.refs_1_, ...), custom_call_target="tpu_custom_call" | custom-call | flops 268435456 | bytes 4194304 | tf_op jit(solution)/shard_map/pallas_call | solution.py:295
  10.6 1.9 %collective-permute-start.3 = (f32[16,128]{1,0:T(8,128)S(1)}, f32[16,128]{1,0:T(8,128)S(1)}, u32[]{:S(2)}, u32[]{:S(2)}) collective-permute-start(f32[16,128]{1,0:T(8,128)S(1)} %get-tuple-element.13.refs_0_), channel_id=1, source_target_pairs={{0,2},{2,0},{1,3},{3,1},{4,6},{6,4},{5,7},{7,5},{8,10},{10,8},{9,1... | collective-permute-start | bytes 24584 | tf_op jit(solution)/shard_map/ppermute | solution.py:350
  12.5 1.8 %collective-permute-done.3.refs_1_ = f32[16,128]{1,0:T(8,128)S(1)} collective-permute-done((f32[16,128]{1,0:T(8,128)S(1)}, f32[16,128]{1,0:T(8,128)S(1)}, u32[]{:S(2)}, u32[]{:S(2)}) %collective-permute-start.3) | collective-permute-done | bytes 8224 | tf_op jit(solution)/shard_map/ppermute | solution.py:350
  14.2 1.1 %shard_map.98 = (f32[16,128]{1,0:T(8,128)S(1)}, f32[16,1024]{1,0:T(8,128)S(1)}, f32[16,1024]{1,0:T(8,128)S(1)}, f32[16,1024]{1,0:T(8,128)S(1)}, bf16[16,1024]{1,0:T(8,128)(2,1)S(1)}) custom-call(f32[16,128]{1,0:T(8,128)S(1)} %get-tuple-element.13.refs_0_, f32[16,128]{1,0:T(8,128)S(1)} %collective-permute-done.3.refs_1_, ...), custom_call_target="tpu_custom_call" | custom-call | flops 268435456 | bytes 4194304 | tf_op jit(solution)/shard_map/pallas_call | solution.py:314
  15.4 0.1 collective-permute-start.5
  15.4 1.6 %collective-permute-start.4 = (bf16[16,1024]{1,0:T(8,128)(2,1)S(1)}, bf16[16,1024]{1,0:T(8,128)(2,1)S(1)}, u32[]{:S(2)}, u32[]{:S(2)}) collective-permute-start(bf16[16,1024]{1,0:T(8,128)(2,1)S(1)} %get-tuple-element.21), channel_id=1, source_target_pairs={{0,5},{1,4},{4,9},{5,8},{8,13},{9,12},{12,1},{13,0},{2,7},{3,6},{6... | collective-permute-start | bytes 98312 | tf_op jit(solution)/shard_map/ppermute | solution.py:18
  17.1 2.2 %collective-permute-start.6 = (bf16[16,1024]{1,0:T(8,128)(2,1)S(1)}, bf16[16,1024]{1,0:T(8,128)(2,1)S(1)}, u32[]{:S(2)}, u32[]{:S(2)}) collective-permute-start(bf16[16,1024]{1,0:T(8,128)(2,1)S(1)} %add_convert_fusion), channel_id=1, source_target_pairs={{1,12},{0,9},{5,0},{4,13},{9,4},{8,1},{13,8},{12,5},{3,14},{2,11},... | collective-permute-start | bytes 98312 | tf_op jit(solution)/shard_map/ppermute | solution.py:43
  19.2 1.5 %collective-permute-done.4 = bf16[16,1024]{1,0:T(8,128)(2,1)S(1)} collective-permute-done((bf16[16,1024]{1,0:T(8,128)(2,1)S(1)}, bf16[16,1024]{1,0:T(8,128)(2,1)S(1)}, u32[]{:S(2)}, u32[]{:S(2)}) %collective-permute-start.4) | collective-permute-done | bytes 32800 | tf_op jit(solution)/shard_map/ppermute | solution.py:18
  20.7 0.1 collective-permute-done.6
  20.9 0.8 %collective-permute-start.7 = (f32[16,1024]{1,0:T(8,128)S(1)}, f32[16,1024]{1,0:T(8,128)S(1)}, u32[]{:S(2)}, u32[]{:S(2)}) collective-permute-start(f32[16,1024]{1,0:T(8,128)S(1)} %convert_add_fusion), channel_id=1, source_target_pairs={{0,1},{1,0},{2,3},{3,2},{4,5},{5,4},{6,7},{7,6},{8,9},{9,8},{10,11... | collective-permute-start | bytes 196616 | tf_op jit(solution)/shard_map/ppermute | solution.py:350
  21.7 0.7 %shard_map.99 = f32[8,48]{1,0:T(8,128)} custom-call(f32[16,128]{1,0:T(8,128)S(1)} %get-tuple-element.19.slot_resid_ref), custom_call_target="tpu_custom_call" | custom-call | flops 1000000 | bytes 10000 | tf_op jit(solution)/shard_map/pallas_call | solution.py:333
  22.4 0.2 collective-permute-done.7
  22.6 0.6 %add.19 = f32[16,1024]{1,0:T(8,128)} add(f32[16,1024]{1,0:T(8,128)S(1)} %convert_add_fusion, f32[16,1024]{1,0:T(8,128)S(1)} %collective-permute-done.7) | non-fusion elementwise | flops 16384 | bytes 196608 | tf_op jit(solution)/shard_map/add | solution.py:342
  (16 shorter events, 0.1 us)
Async XLA Ops:
  1.4 7.6 %copy-start = (bf16[32,64,1024]{2,1,0:T(8,128)(2,1)S(1)}, bf16[32,64,1024]{2,1,0:T(8,128)(2,1)}, u32[]{:S(2)}) copy-start(bf16[32,64,1024]{2,1,0:T(8,128)(2,1)} %refs_4_.3) | copy-start | bytes 12582916
  1.5 7.6 %copy-start.1 = (f32[32,64]{1,0:T(8,128)S(1)}, f32[32,64]{1,0:T(8,128)}, u32[]{:S(2)}) copy-start(f32[32,64]{1,0:T(8,128)} %refs_5_.1) | copy-start | bytes 24580
  1.5 7.6 %copy-start.2 = (s32[48,8]{0,1:T(8,128)S(1)}, s32[48,8]{0,1:T(8,128)}, u32[]{:S(2)}) copy-start(s32[48,8]{0,1:T(8,128)} %param.12) | copy-start | bytes 4612
  1.5 7.6 %copy-start.3 = (f32[48,8]{0,1:T(8,128)S(1)}, f32[48,8]{0,1:T(8,128)}, u32[]{:S(2)}) copy-start(f32[48,8]{0,1:T(8,128)} %param.14) | copy-start | bytes 4612
  1.5 7.6 %copy-start.4 = (f32[48,8]{0,1:T(8,128)S(1)}, f32[48,8]{0,1:T(8,128)}, u32[]{:S(2)}) copy-start(f32[48,8]{0,1:T(8,128)} %param.15) | copy-start | bytes 4612
  1.5 7.6 %copy-start.5 = (s32[8]{0:T(128)S(1)}, s32[8]{0:T(128)}, u32[]{:S(2)}) copy-start(s32[8]{0:T(128)} %param.13) | copy-start | bytes 100
  1.5 6.3 %collective-permute-start = (bf16[16,1024]{1,0:T(8,128)(2,1)S(1)}, bf16[16,1024]{1,0:T(8,128)(2,1)S(1)}, u32[]{:S(2)}, u32[]{:S(2)}) collective-permute-start(bf16[16,1024]{1,0:T(8,128)(2,1)S(1)} %shard_map.96.refs_3_), channel_id=1, source_target_pairs={{1,4},{0,9},{5,8},{4,13},{9,12},{8,1},{13,0},{12,5},{3,6},{2,11},{... | collective-permute-start | bytes 98312 | tf_op jit(solution)/shard_map/ppermute | solution.py:43
  5.1 3.9 %collective-permute-start.2 = (bf16[16,1024]{1,0:T(8,128)(2,1)S(1)}, bf16[16,1024]{1,0:T(8,128)(2,1)S(1)}, u32[]{:S(2)}, u32[]{:S(2)}) collective-permute-start(bf16[16,1024]{1,0:T(8,128)(2,1)S(1)} %shard_map.96.refs_3_), channel_id=1, source_target_pairs={{0,12},{4,0},{8,4},{12,8},{1,13},{5,1},{9,5},{13,9},{2,14},{6,2},{... | collective-permute-start | bytes 98312 | tf_op jit(solution)/shard_map/ppermute | solution.py:23
  7.8 1.2 %collective-permute-start.1 = (bf16[16,1024]{1,0:T(8,128)(2,1)S(1)}, bf16[16,1024]{1,0:T(8,128)(2,1)S(1)}, u32[]{:S(2)}, u32[]{:S(2)}) collective-permute-start(bf16[16,1024]{1,0:T(8,128)(2,1)S(1)} %collective-permute-done.refs_0_), channel_id=1, source_target_pairs={{0,1},{1,0},{2,3},{3,2},{4,5},{5,4},{6,7},{7,6},{8,9},{9,8},{10,11... | collective-permute-start | bytes 98312 | tf_op jit(solution)/shard_map/ppermute | solution.py:350
  9.1 11.8 %copy-start.6 = (f32[16,1024]{1,0:T(8,128)S(1)}, f32[16,1024]{1,0:T(8,128)}, u32[]{:S(2)}) copy-start(f32[16,1024]{1,0:T(8,128)} %flux_hbm.1) | copy-start | bytes 196612
  9.1 11.7 %copy-start.7 = (f32[16,1024]{1,0:T(8,128)S(1)}, f32[16,1024]{1,0:T(8,128)}, u32[]{:S(2)}) copy-start(f32[16,1024]{1,0:T(8,128)} %param.9) | copy-start | bytes 196612
  10.6 3.7 %collective-permute-start.3 = (f32[16,128]{1,0:T(8,128)S(1)}, f32[16,128]{1,0:T(8,128)S(1)}, u32[]{:S(2)}, u32[]{:S(2)}) collective-permute-start(f32[16,128]{1,0:T(8,128)S(1)} %get-tuple-element.13.refs_0_), channel_id=1, source_target_pairs={{0,2},{2,0},{1,3},{3,1},{4,6},{6,4},{5,7},{7,5},{8,10},{10,8},{9,1... | collective-permute-start | bytes 24584 | tf_op jit(solution)/shard_map/ppermute | solution.py:350
  15.4 1.7 %collective-permute-start.5 = (f32[16,1024]{1,0:T(8,128)S(1)}, f32[16,1024]{1,0:T(8,128)S(1)}, u32[]{:S(2)}, u32[]{:S(2)}) collective-permute-start(f32[16,1024]{1,0:T(8,128)S(1)} %get-tuple-element.23), channel_id=1, source_target_pairs={{0,1},{1,0},{2,3},{3,2},{4,5},{5,4},{6,7},{7,6},{8,9},{9,8},{10,11... | collective-permute-start | bytes 196616 | tf_op jit(solution)/shard_map/ppermute | solution.py:350
  15.4 5.3 %collective-permute-start.4 = (bf16[16,1024]{1,0:T(8,128)(2,1)S(1)}, bf16[16,1024]{1,0:T(8,128)(2,1)S(1)}, u32[]{:S(2)}, u32[]{:S(2)}) collective-permute-start(bf16[16,1024]{1,0:T(8,128)(2,1)S(1)} %get-tuple-element.21), channel_id=1, source_target_pairs={{0,5},{1,4},{4,9},{5,8},{8,13},{9,12},{12,1},{13,0},{2,7},{3,6},{6... | collective-permute-start | bytes 98312 | tf_op jit(solution)/shard_map/ppermute | solution.py:18
  17.1 3.8 %collective-permute-start.6 = (bf16[16,1024]{1,0:T(8,128)(2,1)S(1)}, bf16[16,1024]{1,0:T(8,128)(2,1)S(1)}, u32[]{:S(2)}, u32[]{:S(2)}) collective-permute-start(bf16[16,1024]{1,0:T(8,128)(2,1)S(1)} %add_convert_fusion), channel_id=1, source_target_pairs={{1,12},{0,9},{5,0},{4,13},{9,4},{8,1},{13,8},{12,5},{3,14},{2,11},... | collective-permute-start | bytes 98312 | tf_op jit(solution)/shard_map/ppermute | solution.py:43
  20.9 1.7 %collective-permute-start.7 = (f32[16,1024]{1,0:T(8,128)S(1)}, f32[16,1024]{1,0:T(8,128)S(1)}, u32[]{:S(2)}, u32[]{:S(2)}) collective-permute-start(f32[16,1024]{1,0:T(8,128)S(1)} %convert_add_fusion), channel_id=1, source_target_pairs={{0,1},{1,0},{2,3},{3,2},{4,5},{5,4},{6,7},{7,6},{8,9},{9,8},{10,11... | collective-permute-start | bytes 196616 | tf_op jit(solution)/shard_map/ppermute | solution.py:350
